TPU v7x, 32 devices: a whole 2x2x4 slice. The times are simulated.
32 devices in a mesh: expert: 2 (over x), dp: 16 (over z, y, core).
Axes of the slice: x: 2, y: 2, z: 4, core: 2. Of those that a mesh axis runs over, the one named last changes fastest.
Arguments:
- tokens: bfloat16 [16, 4, 2048], P('dp', 'expert'), may hold values from -6 to 6
- out_grad: bfloat16 [16, 4, 2048], P('dp', 'expert'), may hold values from -6 to 6
- expert_ids: int32 [16, 4, 2], P('dp'), may hold values from 0 to 1, as said below
- gate_scores: bfloat16 [16, 4, 2], P('dp'), may hold values from 0.25 to 1
- w_gate: bfloat16 [2, 2048, 8192], P('expert', None, 'dp'), may hold values from -0.125 to 0.125
- w_up: bfloat16 [2, 2048, 8192], P('expert', None, 'dp'), may hold values from -0.125 to 0.125
- w_down: bfloat16 [2, 8192, 2048], P('expert', 'dp'), may hold values from -0.0625 to 0.0625
Outputs:
- token_grad: bfloat16 [16, 4, 2048], P('dp', 'expert')
- grad_gate: bfloat16 [2, 2048, 8192], P('expert', None, 'dp')
- grad_up: bfloat16 [2, 2048, 8192], P('expert', None, 'dp')
- grad_down: bfloat16 [2, 8192, 2048], P('expert', 'dp')
Inputs may be any that keep to these rules, and one draw needn't show every extreme that they name: `expert_ids`: each token names two different experts; within a group no expert is named by more than 4 tokens, and in every group some expert is named by exactly 4 tokens.
All inputs are finite; a program needn't handle non-finite values.
Results may differ from a plain program's by a relative error of at most 0.0058.
Values may be sent and summed in bfloat16 or wider, within the bound.
No kernel may reach another device: no remote copies, remote signals or barrier semaphores. Data moves between devices by JAX's collectives and lax.ppermute only.
A program may use at most 64 MiB of HBM per device.

v0:
```python
import functools

import jax
import jax.numpy as jnp
from jax import lax
from jax.experimental import pallas as pl
from jax.experimental.pallas import tpu as pltpu
from jax.sharding import PartitionSpec as P

LANES = 128
CORES = 2
BOTH = ("expert", "dp")
ROWS = 64
TILE = 16
CONTRACT_LAST = (((1,), (1,)), ((), ()))
PIECES = 4
VMEM = pl.BlockSpec(memory_space=pltpu.VMEM)
HBM = pl.BlockSpec(memory_space=pltpu.HBM)


def vmem(size):
    return pltpu.CompilerParams(vmem_limit_bytes=min(size, 36 << 20))


def pack_kernel(
    tokens_hbm, grad_hbm, ids_hbm, scores_hbm, out_ref,
    tokens_ref, grad_ref, ids_ref, scores_ref, sems,
):
    copies = [
        pltpu.make_async_copy(src, dst, sems.at[i])
        for i, (src, dst) in enumerate((
            (ids_hbm, ids_ref),
            (scores_hbm, scores_ref),
            (tokens_hbm, tokens_ref),
            (grad_hbm, grad_ref),
        ))
    ]
    for copy in copies:
        copy.start()
    for copy in copies:
        copy.wait()
    chips, tok_dev, _ = out_ref.shape
    width = tokens_ref.shape[2]
    first = lax.axis_index("expert") * tok_dev
    ids = ids_ref[0]
    scores = scores_ref[0].astype(jnp.float32)
    token = lax.broadcasted_iota(jnp.int32, ids.shape, 1)
    lane = lax.broadcasted_iota(jnp.int32, (ids.shape[0], LANES), 1)
    row = lax.broadcasted_iota(jnp.int32, (tok_dev, LANES), 0)
    table = jnp.zeros((tok_dev, LANES), jnp.float32)
    for i in range(tok_dev):
        mine = token == first + i
        named = jnp.sum(jnp.where(mine, ids, 0), axis=1, keepdims=True)
        score = jnp.sum(jnp.where(mine, scores, 0.0), axis=1, keepdims=True)
        weights = jnp.sum(jnp.where(lane == named, score, 0.0), axis=0, keepdims=True)
        table = jnp.where(row == i, weights, table)
    table = table.astype(jnp.bfloat16)

    def write(chip, carry):
        out_ref[chip, :, :width] = tokens_ref[0]
        out_ref[chip, :, width : 2 * width] = grad_ref[0]
        out_ref[chip, :, 2 * width :] = table
        return carry

    lax.fori_loop(0, chips, write, 0, unroll=chips <= 16)


def pack(tokens, out_grad, expert_ids, gate_scores, chips):
    _, tok_dev, width = tokens.shape
    operands = [
        pltpu.with_memory_space_constraint(a, pltpu.HBM)
        for a in (
            tokens, out_grad, jnp.swapaxes(expert_ids, 1, 2), jnp.swapaxes(gate_scores, 1, 2)
        )
    ]
    return pl.pallas_call(
        pack_kernel,
        out_shape=jax.ShapeDtypeStruct((chips, tok_dev, 2 * width + LANES), jnp.bfloat16),
        in_specs=[HBM] * 4,
        out_specs=VMEM,
        scratch_shapes=[pltpu.VMEM(a.shape, a.dtype) for a in operands]
        + [pltpu.SemaphoreType.DMA((4,))],
        compiler_params=vmem(16 << 20),
    )(*operands)


def copy_pieces(src, dst, sems):
    rows = dst.shape[0] // PIECES
    parts = [pl.ds(piece * rows, rows) for piece in range(PIECES)]
    copies = [
        pltpu.make_async_copy(src.at[0, part], dst.at[part], sems.at[piece])
        for piece, part in enumerate(parts)
    ]
    for copy in copies:
        copy.start()
    return copies


def lay_out(src_ref, x_ref, dy_ref, table_ref, first):
    chips, tok_dev, _ = src_ref.shape
    width = x_ref.shape[1]
    my_expert = lax.axis_index("expert")
    lane = lax.broadcasted_iota(jnp.int32, (TILE, LANES), 1)
    per_tile = TILE // tok_dev

    def step(tile, carry):
        rows = pl.ds(pl.multiple_of(first + tile * TILE, TILE), TILE)
        for j in range(per_tile):
            part = slice(j * tok_dev, (j + 1) * tok_dev)
            chip = tile * per_tile + j
            table_ref[part] = src_ref[chip, :, 2 * width :]
        table = table_ref[...].astype(jnp.float32)
        weight = jnp.sum(jnp.where(lane == my_expert, table, 0.0), axis=1, keepdims=True)
        blocks = [src_ref[tile * per_tile + j] for j in range(per_tile)]
        x_ref[rows] = jnp.concatenate([b[:, :width] for b in blocks], axis=0)
        raw = jnp.concatenate([b[:, width : 2 * width] for b in blocks], axis=0)
        dy_ref[rows] = (raw.astype(jnp.float32) * weight).astype(jnp.bfloat16)
        return carry

    tiles = chips // per_tile
    lax.fori_loop(0, tiles, step, 0, unroll=tiles <= 2)


def fetch_kernel(mine_ref, gate_hbm, gate_ref, x_ref, dy_ref, table_ref, sems):
    copies = copy_pieces(gate_hbm, gate_ref, sems)
    lay_out(mine_ref, x_ref, dy_ref, table_ref, 0)
    for copy in copies:
        copy.wait()


def fetch(mine, w_gate):
    chips, tok_dev, row = mine.shape
    _, width, hidden = w_gate.shape
    half = chips * tok_dev
    moved = 2 * width * hidden
    return pl.pallas_call(
        fetch_kernel,
        out_shape=(
            pltpu.VMEM((width, hidden), jnp.bfloat16),
            pltpu.VMEM((half, width), jnp.bfloat16),
            pltpu.VMEM((half, width), jnp.bfloat16),
        ),
        in_specs=[VMEM, HBM],
        out_specs=(VMEM,) * 3,
        scratch_shapes=[
            pltpu.VMEM((TILE, LANES), jnp.bfloat16),
            pltpu.SemaphoreType.DMA((PIECES,)),
        ],
        cost_estimate=pl.CostEstimate(flops=0, bytes_accessed=2 * moved, transcendentals=0),
        compiler_params=vmem((8 << 20) + 2 * moved + 8 * half * row),
    )(mine, pltpu.with_memory_space_constraint(w_gate, pltpu.HBM))


def my_core():
    return lax.axis_index("dp") % CORES


def row_blocks(rows, step):
    step(0, True)
    if rows > ROWS:
        pl.loop(1, rows // ROWS)(lambda block: step(block, False))


def half_total(gate_delta, up_delta, gate_ref, up_ref, core):
    columns = gate_ref.shape[0] // CORES
    part = pl.ds(pl.multiple_of(core * columns, columns), columns)
    total = lax.dot_general(
        gate_delta, gate_ref[part], CONTRACT_LAST, preferred_element_type=jnp.float32
    )
    return total + lax.dot_general(
        up_delta, up_ref[part], CONTRACT_LAST, preferred_element_type=jnp.float32
    )


def rows_kernel(
    other_ref, my_x_ref, my_dy_ref, gate_ref, up_hbm, down_hbm,
    sent_ref, up_ref, x_ref, dy_ref, gate_delta_ref, up_delta_ref, hidden_ref,
    down_ref, table_ref, sems,
):
    up_copies = copy_pieces(up_hbm, up_ref, sems.at[0])
    down_copies = copy_pieces(down_hbm, down_ref, sems.at[1])
    half = my_x_ref.shape[0]
    x_ref[:half] = my_x_ref[...]
    dy_ref[:half] = my_dy_ref[...]
    lay_out(other_ref, x_ref, dy_ref, table_ref, half)
    depth = up_ref.shape[0] // PIECES

    def step(block, first):
        rows = pl.ds(pl.multiple_of(block * ROWS, ROWS), ROWS)
        x = x_ref[rows]
        pre_gate = jnp.dot(x, gate_ref[...], preferred_element_type=jnp.float32)
        sigmoid_gate = jax.nn.sigmoid(pre_gate)
        activated = pre_gate * sigmoid_gate
        pre_up = None
        for piece, copy in enumerate(up_copies):
            if first:
                copy.wait()
            part = slice(piece * depth, (piece + 1) * depth)
            product = jnp.dot(x[:, part], up_ref[part], preferred_element_type=jnp.float32)
            pre_up = product if pre_up is None else pre_up + product
        hidden_ref[rows] = (activated * pre_up).astype(jnp.bfloat16)
        if first:
            for copy in down_copies:
                copy.wait()
        grad_hidden = lax.dot_general(
            dy_ref[rows], down_ref[...], CONTRACT_LAST, preferred_element_type=jnp.float32
        )
        gate_delta = (
            grad_hidden * pre_up * sigmoid_gate * (1.0 + pre_gate * (1.0 - sigmoid_gate))
        ).astype(jnp.bfloat16)
        up_delta = (grad_hidden * activated).astype(jnp.bfloat16)
        gate_delta_ref[rows] = gate_delta
        up_delta_ref[rows] = up_delta
        sent_ref[rows] = half_total(
            gate_delta, up_delta, gate_ref, up_ref, 1 - my_core()
        ).astype(jnp.bfloat16)

    row_blocks(x_ref.shape[0], step)


def rows_pass(other, my_x, my_dy, gate, w_up, w_down):
    chips, tok_dev, row = other.shape
    width, hidden = gate.shape
    rows = 2 * chips * tok_dev
    bf16 = functools.partial(jax.ShapeDtypeStruct, dtype=jnp.bfloat16)
    moved = (3 * width * hidden + rows * (6 * width + 3 * hidden)) * 2
    up, down = (pltpu.with_memory_space_constraint(w, pltpu.HBM) for w in (w_up, w_down))
    return pl.pallas_call(
        rows_kernel,
        out_shape=(
            bf16((rows, width // CORES)),
            pltpu.VMEM((width, hidden), jnp.bfloat16),
            bf16((rows, width)),
            bf16((rows, width)),
            bf16((rows, hidden)),
            bf16((rows, hidden)),
            bf16((rows, hidden)),
        ),
        in_specs=[VMEM] * 4 + [HBM] * 2,
        out_specs=(VMEM,) * 7,
        scratch_shapes=[
            pltpu.VMEM((hidden, width), jnp.bfloat16),
            pltpu.VMEM((TILE, LANES), jnp.bfloat16),
            pltpu.SemaphoreType.DMA((2, PIECES)),
        ],
        cost_estimate=pl.CostEstimate(
            flops=8 * rows * width * hidden, bytes_accessed=moved, transcendentals=rows * hidden
        ),
        compiler_params=vmem((12 << 20) + 2 * moved),
    )(other, my_x, my_dy, gate, up, down)


def finish_kernel(gate_delta_ref, up_delta_ref, gate_ref, up_ref, total_ref):
    def step(block, first):
        rows = pl.ds(pl.multiple_of(block * ROWS, ROWS), ROWS)
        total_ref[rows] = half_total(
            gate_delta_ref[rows], up_delta_ref[rows], gate_ref, up_ref, my_core()
        )

    row_blocks(total_ref.shape[0], step)


def finish(gate_delta, up_delta, gate, up):
    rows, hidden = gate_delta.shape
    columns = gate.shape[0] // CORES
    moved = 4 * columns * hidden + 4 * rows * (columns + hidden)
    return pl.pallas_call(
        finish_kernel,
        out_shape=jax.ShapeDtypeStruct((rows, columns), jnp.float32),
        in_specs=[VMEM] * 4,
        out_specs=VMEM,
        cost_estimate=pl.CostEstimate(
            flops=4 * rows * columns * hidden, bytes_accessed=moved, transcendentals=0
        ),
        compiler_params=vmem((16 << 20) + 2 * moved),
    )(gate_delta, up_delta, gate, up)


def share_kernel(total_ref, got_ref, shares_ref):
    devices, tok_dev, _ = shares_ref.shape
    chips = devices // CORES
    per_tile = TILE // tok_dev
    tiles = devices // per_tile
    core = my_core()

    def step(tile, carry):
        rows = pl.ds(pl.multiple_of(tile * TILE, TILE), TILE)
        there = pl.ds(pl.multiple_of((tile + tiles // 2) % tiles * TILE, TILE), TILE)
        total = (total_ref[rows] + got_ref[there].astype(jnp.float32)).astype(jnp.bfloat16)
        for j in range(per_tile):
            place = tile * per_tile + j
            owner = jnp.where(place < chips, core, 1 - core)
            shares_ref[(place % chips) * CORES + owner] = total[j * tok_dev : (j + 1) * tok_dev]
        return carry

    lax.fori_loop(0, tiles, step, 0, unroll=tiles <= 4)


def share(total, got, tok_dev):
    rows, columns = total.shape
    return pl.pallas_call(
        share_kernel,
        out_shape=jax.ShapeDtypeStruct((rows // tok_dev, tok_dev, columns), jnp.bfloat16),
        in_specs=[VMEM] * 2,
        out_specs=VMEM,
        compiler_params=vmem((8 << 20) + 32 * rows * columns),
    )(total, got)


def sum_kernel(shares_ref, out_hbm, out_ref, sem):
    devices, tok_dev, columns = shares_ref.shape
    for core in range(CORES):
        zero = jnp.zeros((tok_dev, columns), jnp.float32)
        total = lax.fori_loop(
            0,
            devices // CORES,
            lambda i, acc: acc + shares_ref[i * CORES + core].astype(jnp.float32),
            zero,
            unroll=devices <= 32,
        )
        out_ref[0, :, core * columns : (core + 1) * columns] = total.astype(jnp.bfloat16)
    copy = pltpu.make_async_copy(out_ref, out_hbm, sem)
    copy.start()
    copy.wait()


def sum_shares(shares):
    devices, tok_dev, columns = shares.shape
    out = (1, tok_dev, CORES * columns)
    return pl.pallas_call(
        sum_kernel,
        out_shape=pltpu.HBM(out, jnp.bfloat16),
        in_specs=[VMEM],
        out_specs=HBM,
        scratch_shapes=[pltpu.VMEM(out, jnp.bfloat16), pltpu.SemaphoreType.DMA],
        compiler_params=vmem(16 << 20),
    )(shares)


def local(tokens, out_grad, expert_ids, gate_scores, w_gate, w_up, w_down):
    devices = lax.axis_size("expert") * lax.axis_size("dp")
    chips = devices // CORES
    middle = lax.axis_size("dp") // CORES // 2
    order = [(chip + middle) % chips for chip in range(chips)]
    same_core = [[chip * CORES + core for chip in order] for core in range(CORES)]
    everyone = [[chip * CORES + core for chip in order for core in range(CORES)]]
    core_pairs = [(d, d ^ 1) for d in range(devices)]
    copies = pack(tokens, out_grad, expert_ids, gate_scores, chips)
    mine = lax.all_to_all(copies, BOTH, 0, 0, axis_index_groups=same_core, tiled=True)
    other = lax.ppermute(mine, BOTH, core_pairs)
    gate, my_x, my_dy = fetch(mine, w_gate)
    sent, up, x, dy, gate_delta, up_delta, hidden = rows_pass(
        other, my_x, my_dy, gate, w_up, w_down
    )
    got = lax.ppermute(sent, BOTH, core_pairs)
    total = finish(gate_delta, up_delta, gate, up)
    shares = share(total, got, tokens.shape[1])
    shares = lax.all_to_all(shares, BOTH, 0, 0, axis_index_groups=everyone, tiled=True)
    token_grad = sum_shares(shares)
    grad_down = jnp.dot(hidden.T, dy, preferred_element_type=jnp.float32)
    grad_gate = jnp.dot(x.T, gate_delta, preferred_element_type=jnp.float32)
    grad_up = jnp.dot(x.T, up_delta, preferred_element_type=jnp.float32)
    weight_grads = (grad_gate, grad_up, grad_down)
    return (token_grad,) + tuple(g.astype(jnp.bfloat16)[None] for g in weight_grads)


def solution(mesh):
    return jax.shard_map(
        local,
        mesh=mesh,
        in_specs=(
            P("dp", "expert", None),
            P("dp", "expert", None),
            P("dp", None, None),
            P("dp", None, None),
            P("expert", None, "dp"),
            P("expert", None, "dp"),
            P("expert", "dp", None),
        ),
        out_specs=(
            P("dp", "expert", None),
            P("expert", None, "dp"),
            P("expert", None, "dp"),
            P("expert", "dp", None),
        ),
        check_vma=False,
    )
```

profile of v0, /device:TPU:0, one launch (start us, length us, event | category | flops | bytes accessed | tf_op | source)
XLA Modules:
  0.0 39.4 jit_solution(7928057693251654997)
XLA Ops:
  0.6 0.9 %shard_map.102 = bf16[16,2,4224]{2,1,0:T(2,128)(2,1)S(1)} custom-call(bf16[1,2,2048]{2,1,0:T(2,128)(2,1)} %tokens_hbm.1, bf16[1,2,2048]{2,1,0:T(2,128)(2,1)} %grad_hbm.1, s32[1,2,4]{2,1,0:T(2,128)} %bitcast.14, bf16[1,2,4]{2,1,0:T(2,128)(2,1)} %bitcast.15), custom_call_target="tpu_custom_call" | custom-call | tf_op jit(solution)/shard_map/pallas_call | solution.py:76
  1.5 16.3 %all_to_all.10.mine_ref = bf16[16,2,4224]{2,1,0:T(2,128)(2,1)S(1)} all-to-all(bf16[16,2,4224]{2,1,0:T(2,128)(2,1)S(1)} %shard_map.102), channel_id=1, replica_groups={{8,10,12,14,16,18,20,22,24,26,28,30,0,2,4,6},{9,11,13,15,17,19,21,23,25..., dimensions={0} | all-to-all | bytes 540672 | tf_op jit(solution)/shard_map/all_to_all | solution.py:349
  17.9 0.0 collective-permute-start
  17.9 1.6 %shard_map.103 = (bf16[2048,512]{1,0:T(8,128)(2,1)S(1)}, bf16[32,2048]{1,0:T(8,128)(2,1)S(1)}, bf16[32,2048]{1,0:T(8,128)(2,1)S(1)}) custom-call(bf16[16,2,4224]{2,1,0:T(2,128)(2,1)S(1)} %all_to_all.10.mine_ref, bf16[1,2048,512]{2,1,0:T(8,128)(2,1)} %gate_hbm.1), custom_call_target="tpu_custom_call" | custom-call | bytes 4194304 | tf_op jit(solution)/shard_map/pallas_call | solution.py:136
  19.4 0.0 collective-permute-done.other_ref
  19.4 3.7 %shard_map.104 = (bf16[64,1024]{1,0:T(8,128)(2,1)S(1)}, bf16[2048,512]{1,0:T(8,128)(2,1)S(1)}, bf16[64,2048]{1,0:T(8,128)(2,1)S(1)}, bf16[64,2048]{1,0:T(8,128)(...) custom-call(bf16[16,2,4224]{2,1,0:T(2,128)(2,1)S(1)} %collective-permute-done.other_, ...), custom_call_target="tpu_custom_call" | custom-call | flops 536870912 | bytes 8060928 | tf_op jit(solution)/shard_map/pallas_call | solution.py:228
  23.2 0.6 %collective-permute-start.1 = (bf16[64,1024]{1,0:T(8,128)(2,1)S(1)}, bf16[64,1024]{1,0:T(8,128)(2,1)S(1)}, u32[]{:S(2)}, u32[]{:S(2)}) collective-permute-start(bf16[64,1024]{1,0:T(8,128)(2,1)S(1)} %get-tuple-element.20), channel_id=1, source_target_pairs={{0,1},{1,0},{2,3},{3,2},{4,5},{5,4},{6,7},{7,6},{8,9},{9,8},{10,11... | collective-permute-start | bytes 393224 | tf_op jit(solution)/shard_map/ppermute | solution.py:355
  23.8 0.7 %shard_map.105.total_ref = f32[64,1024]{1,0:T(8,128)S(1)} custom-call(bf16[64,512]{1,0:T(8,128)(2,1)S(1)} %get-tuple-element.17.gate_delta_ref, bf16[64,512]{1,0:T(8,128)(2,1)S(1)} %get-tuple-element.18.up_delta_ref, bf16[2048,512]{1,0:T(8,128)(2,1)S(1)} %get-tuple-element.16.gate_ref, bf16[2048,512]{1,0:T(8,128)(2,1)S(1)} %get-tuple-element.19.up_ref), custom_call_target="tpu_custom_call" | custom-call | flops 134217728 | bytes 2490368 | tf_op jit(solution)/shard_map/pallas_call | solution.py:267
  24.5 2.1 %fusion.1 = bf16[1,2048,512]{2,1,0:T(8,128)(2,1)} fusion(bf16[64,2048]{1,0:T(8,128)(2,1)S(1)} %get-tuple-element.21, bf16[64,512]{1,0:T(8,128)(2,1)S(1)} %get-tuple-element.18.up_delta_ref), kind=kOutput, calls=%fused_computation.4 | convolution fusion | flops 135266304 | bytes 2424832 | tf_op jit(solution)/shard_map/dot_general | solution.py:362
  26.6 0.0 collective-permute-done.1.got_ref
  26.6 0.7 %shard_map.106 = bf16[32,2,1024]{2,1,0:T(2,128)(2,1)} custom-call(f32[64,1024]{1,0:T(8,128)S(1)} %shard_map.105.total_ref, bf16[64,1024]{1,0:T(8,128)(2,1)S(1)} %collective-permute-done.1.got_ref), custom_call_target="tpu_custom_call" | custom-call | tf_op jit(solution)/shard_map/pallas_call | solution.py:301
  27.3 3.3 %all-to-all-start.1 = ((bf16[32,2,1024]{2,1,0:T(2,128)(2,1)}), bf16[32,2,1024]{2,1,0:T(2,128)(2,1)S(1)}, u32[]{:S(2)}, u32[]{:S(2)}) async-start(bf16[32,2,1024]{2,1,0:T(2,128)(2,1)} %shard_map.106), calls=%async_computation.1 | async-start | bytes 262144 | tf_op jit(solution)/shard_map/all_to_all | solution.py:358
  30.6 2.1 %fusion = bf16[1,2048,512]{2,1,0:T(8,128)(2,1)} fusion(bf16[64,2048]{1,0:T(8,128)(2,1)S(1)} %get-tuple-element.21, bf16[64,512]{1,0:T(8,128)(2,1)S(1)} %get-tuple-element.17.gate_delta_ref), kind=kOutput, calls=%fused_computation.3 | convolution fusion | flops 135266304 | bytes 2424832 | tf_op jit(solution)/shard_map/dot_general | solution.py:361
  32.6 2.0 %fusion.2 = bf16[1,512,2048]{2,1,0:T(8,128)(2,1)} fusion(bf16[64,512]{1,0:T(8,128)(2,1)S(1)} %get-tuple-element.22, bf16[64,2048]{1,0:T(8,128)(2,1)S(1)} %get-tuple-element.23), kind=kOutput, calls=%fused_computation.5 | convolution fusion | flops 135266304 | bytes 2424832 | tf_op jit(solution)/shard_map/dot_general | solution.py:360
  34.7 4.1 %all-to-all-done.1.shares_ref = bf16[32,2,1024]{2,1,0:T(2,128)(2,1)S(1)} async-done(((bf16[32,2,1024]{2,1,0:T(2,128)(2,1)}), bf16[32,2,1024]{2,1,0:T(2,128)(2,1)S(1)}, u32[]{:S(2)}, u32[]{:S(2)}) %all-to-all-start.1) | async-done | bytes 131104 | tf_op jit(solution)/shard_map/all_to_all | solution.py:358
  38.8 0.6 %shard_map.107 = bf16[1,2,2048]{2,1,0:T(2,128)(2,1)} custom-call(bf16[32,2,1024]{2,1,0:T(2,128)(2,1)S(1)} %all-to-all-done.1.shares_ref), custom_call_target="tpu_custom_call" | custom-call | tf_op jit(solution)/shard_map/pallas_call | solution.py:330
Async XLA Ops:
  17.9 1.6 %collective-permute-start = (bf16[16,2,4224]{2,1,0:T(2,128)(2,1)S(1)}, bf16[16,2,4224]{2,1,0:T(2,128)(2,1)S(1)}, u32[]{:S(2)}, u32[]{:S(2)}) collective-permute-start(bf16[16,2,4224]{2,1,0:T(2,128)(2,1)S(1)} %all_to_all.10.mine_ref), channel_id=1, source_target_pairs={{0,1},{1,0},{2,3},{3,2},{4,5},{5,4},{6,7},{7,6},{8,9},{9,8},{10,11... | collective-permute-start | bytes 811016 | tf_op jit(solution)/shard_map/ppermute | solution.py:350
  23.2 3.4 %collective-permute-start.1 = (bf16[64,1024]{1,0:T(8,128)(2,1)S(1)}, bf16[64,1024]{1,0:T(8,128)(2,1)S(1)}, u32[]{:S(2)}, u32[]{:S(2)}) collective-permute-start(bf16[64,1024]{1,0:T(8,128)(2,1)S(1)} %get-tuple-element.20), channel_id=1, source_target_pairs={{0,1},{1,0},{2,3},{3,2},{4,5},{5,4},{6,7},{7,6},{8,9},{9,8},{10,11... | collective-permute-start | bytes 393224 | tf_op jit(solution)/shard_map/ppermute | solution.py:355
  27.3 11.5 %all-to-all-start.1 = ((bf16[32,2,1024]{2,1,0:T(2,128)(2,1)}), bf16[32,2,1024]{2,1,0:T(2,128)(2,1)S(1)}, u32[]{:S(2)}, u32[]{:S(2)}) async-start(bf16[32,2,1024]{2,1,0:T(2,128)(2,1)} %shard_map.106), calls=%async_computation.1 | async-start | bytes 262144 | tf_op jit(solution)/shard_map/all_to_all | solution.py:358
where the time goes:
time: 39.7 us; the launch traced here: 39.4 us
  blocking collectives  16.3 us (41%)
  Pallas kernels  8.27 us (21%)
  matrix products  6.17 us (16%)
  waiting for transfers between devices  4.13 us (10%)
  starting transfers between devices  3.85 us (10%)
  between operations  0.68 us (2%)
    all_to_all x1, blocking collectives, local(): lax.all_to_all(copies, BOTH, 0, 0, axis_index_groups=same_core, tiled=True)  16.3 us
    all_to_all x1, waiting for transfers between devices, local(): lax.all_to_all(shares, BOTH, 0, 0, axis_index_groups=everyone, tiled=True)  4.13 us
    pallas_call x1, Pallas kernels, rows_pass(): pl.pallas_call(rows_kernel, out_shape=(bf16((rows, width // CORES)), pltp...  3.75 us
    all_to_all x1, starting transfers between devices, local(): lax.all_to_all(shares, BOTH, 0, 0, axis_index_groups=everyone, tiled=True)  3.27 us
    dot_general x1, matrix products, local(): grad_up = jnp.dot(x.T, up_delta, preferred_element_type=jnp.float32)  2.07 us
    dot_general x1, matrix products, local(): grad_gate = jnp.dot(x.T, gate_delta, preferred_element_type=jnp.float32)  2.05 us
    dot_general x1, matrix products, local(): grad_down = jnp.dot(hidden.T, dy, preferred_element_type=jnp.float32)  2.05 us
    pallas_call x1, Pallas kernels, fetch(): pl.pallas_call(fetch_kernel, out_shape=(pltpu.VMEM((width, hidden), jnp.b...  1.56 us
  transfers between devices with their start and end apart: 3, of which 1 were waited for; matrix products, arithmetic and copies ran while one was open for 16% of the time, Pallas kernels for 6%

commit v1 on v0

--- a/solution.py
+++ b/solution.py
@@ -22,9 +22,14 @@
     return pltpu.CompilerParams(vmem_limit_bytes=min(size, 36 << 20))
 
 
+def chip_at(place):
+    per_expert = lax.axis_size("dp") // CORES
+    return (place + per_expert // 2) % (per_expert * lax.axis_size("expert"))
+
+
 def pack_kernel(
     tokens_hbm, grad_hbm, ids_hbm, scores_hbm, out_ref,
-    tokens_ref, grad_ref, ids_ref, scores_ref, sems,
+    tokens_ref, grad_ref, ids_ref, scores_ref, weighted_ref, sems,
 ):
     copies = [
         pltpu.make_async_copy(src, dst, sems.at[i])
@@ -41,6 +46,7 @@
         copy.wait()
     chips, tok_dev, _ = out_ref.shape
     width = tokens_ref.shape[2]
+    experts = lax.axis_size("expert")
     first = lax.axis_index("expert") * tok_dev
     ids = ids_ref[0]
     scores = scores_ref[0].astype(jnp.float32)
@@ -54,12 +60,13 @@
         score = jnp.sum(jnp.where(mine, scores, 0.0), axis=1, keepdims=True)
         weights = jnp.sum(jnp.where(lane == named, score, 0.0), axis=0, keepdims=True)
         table = jnp.where(row == i, weights, table)
-    table = table.astype(jnp.bfloat16)
-
-    def write(chip, carry):
-        out_ref[chip, :, :width] = tokens_ref[0]
-        out_ref[chip, :, width : 2 * width] = grad_ref[0]
-        out_ref[chip, :, 2 * width :] = table
+    grad = grad_ref[0].astype(jnp.float32)
+    for expert in range(experts):
+        weighted_ref[expert] = (grad * table[:, expert : expert + 1]).astype(jnp.bfloat16)
+
+    def write(place, carry):
+        out_ref[place, :, :width] = tokens_ref[0]
+        out_ref[place, :, width:] = weighted_ref[chip_at(place) // (chips // experts)]
         return carry
 
     lax.fori_loop(0, chips, write, 0, unroll=chips <= 16)
@@ -75,11 +82,14 @@
     ]
     return pl.pallas_call(
         pack_kernel,
-        out_shape=jax.ShapeDtypeStruct((chips, tok_dev, 2 * width + LANES), jnp.bfloat16),
+        out_shape=jax.ShapeDtypeStruct((chips, tok_dev, 2 * width), jnp.bfloat16),
         in_specs=[HBM] * 4,
         out_specs=VMEM,
         scratch_shapes=[pltpu.VMEM(a.shape, a.dtype) for a in operands]
-        + [pltpu.SemaphoreType.DMA((4,))],
+        + [
+            pltpu.VMEM((lax.axis_size("expert"), tok_dev, width), jnp.bfloat16),
+            pltpu.SemaphoreType.DMA((4,)),
+        ],
         compiler_params=vmem(16 << 20),
     )(*operands)
 
@@ -96,34 +106,25 @@
     return copies
 
 
-def lay_out(src_ref, x_ref, dy_ref, table_ref, first):
+def lay_out(src_ref, x_ref, dy_ref, first):
     chips, tok_dev, _ = src_ref.shape
     width = x_ref.shape[1]
-    my_expert = lax.axis_index("expert")
-    lane = lax.broadcasted_iota(jnp.int32, (TILE, LANES), 1)
     per_tile = TILE // tok_dev
 
     def step(tile, carry):
         rows = pl.ds(pl.multiple_of(first + tile * TILE, TILE), TILE)
-        for j in range(per_tile):
-            part = slice(j * tok_dev, (j + 1) * tok_dev)
-            chip = tile * per_tile + j
-            table_ref[part] = src_ref[chip, :, 2 * width :]
-        table = table_ref[...].astype(jnp.float32)
-        weight = jnp.sum(jnp.where(lane == my_expert, table, 0.0), axis=1, keepdims=True)
         blocks = [src_ref[tile * per_tile + j] for j in range(per_tile)]
         x_ref[rows] = jnp.concatenate([b[:, :width] for b in blocks], axis=0)
-        raw = jnp.concatenate([b[:, width : 2 * width] for b in blocks], axis=0)
-        dy_ref[rows] = (raw.astype(jnp.float32) * weight).astype(jnp.bfloat16)
+        dy_ref[rows] = jnp.concatenate([b[:, width:] for b in blocks], axis=0)
         return carry
 
     tiles = chips // per_tile
     lax.fori_loop(0, tiles, step, 0, unroll=tiles <= 2)
 
 
-def fetch_kernel(mine_ref, gate_hbm, gate_ref, x_ref, dy_ref, table_ref, sems):
+def fetch_kernel(mine_ref, gate_hbm, gate_ref, x_ref, dy_ref, sems):
     copies = copy_pieces(gate_hbm, gate_ref, sems)
-    lay_out(mine_ref, x_ref, dy_ref, table_ref, 0)
+    lay_out(mine_ref, x_ref, dy_ref, 0)
     for copy in copies:
         copy.wait()
 
@@ -142,10 +143,7 @@
         ),
         in_specs=[VMEM, HBM],
         out_specs=(VMEM,) * 3,
-        scratch_shapes=[
-            pltpu.VMEM((TILE, LANES), jnp.bfloat16),
-            pltpu.SemaphoreType.DMA((PIECES,)),
-        ],
+        scratch_shapes=[pltpu.SemaphoreType.DMA((PIECES,))],
         cost_estimate=pl.CostEstimate(flops=0, bytes_accessed=2 * moved, transcendentals=0),
         compiler_params=vmem((8 << 20) + 2 * moved + 8 * half * row),
     )(mine, pltpu.with_memory_space_constraint(w_gate, pltpu.HBM))
@@ -172,17 +170,24 @@
     )
 
 
+def store_groups(ref, first, total):
+    rows, columns = total.shape
+    groups = columns // LANES
+    for c in range(groups):
+        ref[pl.ds(first + c, rows, stride=groups)] = total[:, c * LANES : (c + 1) * LANES]
+
+
 def rows_kernel(
     other_ref, my_x_ref, my_dy_ref, gate_ref, up_hbm, down_hbm,
     sent_ref, up_ref, x_ref, dy_ref, gate_delta_ref, up_delta_ref, hidden_ref,
-    down_ref, table_ref, sems,
+    down_ref, total_ref, sems,
 ):
     up_copies = copy_pieces(up_hbm, up_ref, sems.at[0])
     down_copies = copy_pieces(down_hbm, down_ref, sems.at[1])
     half = my_x_ref.shape[0]
     x_ref[:half] = my_x_ref[...]
     dy_ref[:half] = my_dy_ref[...]
-    lay_out(other_ref, x_ref, dy_ref, table_ref, half)
+    lay_out(other_ref, x_ref, dy_ref, half)
     depth = up_ref.shape[0] // PIECES
 
     def step(block, first):
@@ -211,9 +216,11 @@
         up_delta = (grad_hidden * activated).astype(jnp.bfloat16)
         gate_delta_ref[rows] = gate_delta
         up_delta_ref[rows] = up_delta
-        sent_ref[rows] = half_total(
-            gate_delta, up_delta, gate_ref, up_ref, 1 - my_core()
-        ).astype(jnp.bfloat16)
+        total = half_total(gate_delta, up_delta, gate_ref, up_ref, 1 - my_core())
+        store_groups(total_ref, 0, total)
+        size = total_ref.shape[0]
+        part = pl.ds(pl.multiple_of(block * size, size), size)
+        sent_ref[part] = total_ref[...].astype(jnp.bfloat16)
 
     row_blocks(x_ref.shape[0], step)
 
@@ -222,13 +229,14 @@
     chips, tok_dev, row = other.shape
     width, hidden = gate.shape
     rows = 2 * chips * tok_dev
+    groups = width // CORES // LANES
     bf16 = functools.partial(jax.ShapeDtypeStruct, dtype=jnp.bfloat16)
     moved = (3 * width * hidden + rows * (6 * width + 3 * hidden)) * 2
     up, down = (pltpu.with_memory_space_constraint(w, pltpu.HBM) for w in (w_up, w_down))
     return pl.pallas_call(
         rows_kernel,
         out_shape=(
-            bf16((rows, width // CORES)),
+            bf16((rows * groups, LANES)),
             pltpu.VMEM((width, hidden), jnp.bfloat16),
             bf16((rows, width)),
             bf16((rows, width)),
@@ -240,7 +248,7 @@
         out_specs=(VMEM,) * 7,
         scratch_shapes=[
             pltpu.VMEM((hidden, width), jnp.bfloat16),
-            pltpu.VMEM((TILE, LANES), jnp.bfloat16),
+            pltpu.VMEM((ROWS * groups, LANES), jnp.float32),
             pltpu.SemaphoreType.DMA((2, PIECES)),
         ],
         cost_estimate=pl.CostEstimate(
@@ -251,13 +259,17 @@
 
 
 def finish_kernel(gate_delta_ref, up_delta_ref, gate_ref, up_ref, total_ref):
+    rows_all = gate_delta_ref.shape[0]
+    size = total_ref.shape[0] // rows_all * ROWS
+
     def step(block, first):
         rows = pl.ds(pl.multiple_of(block * ROWS, ROWS), ROWS)
-        total_ref[rows] = half_total(
+        total = half_total(
             gate_delta_ref[rows], up_delta_ref[rows], gate_ref, up_ref, my_core()
         )
-
-    row_blocks(total_ref.shape[0], step)
+        store_groups(total_ref, block * size, total)
+
+    row_blocks(rows_all, step)
 
 
 def finish(gate_delta, up_delta, gate, up):
@@ -266,7 +278,7 @@
     moved = 4 * columns * hidden + 4 * rows * (columns + hidden)
     return pl.pallas_call(
         finish_kernel,
-        out_shape=jax.ShapeDtypeStruct((rows, columns), jnp.float32),
+        out_shape=jax.ShapeDtypeStruct((rows * columns // LANES, LANES), jnp.float32),
         in_specs=[VMEM] * 4,
         out_specs=VMEM,
         cost_estimate=pl.CostEstimate(
@@ -277,62 +289,66 @@
 
 
 def share_kernel(total_ref, got_ref, shares_ref):
-    devices, tok_dev, _ = shares_ref.shape
+    devices, size, _ = shares_ref.shape
     chips = devices // CORES
-    per_tile = TILE // tok_dev
-    tiles = devices // per_tile
     core = my_core()
 
-    def step(tile, carry):
-        rows = pl.ds(pl.multiple_of(tile * TILE, TILE), TILE)
-        there = pl.ds(pl.multiple_of((tile + tiles // 2) % tiles * TILE, TILE), TILE)
-        total = (total_ref[rows] + got_ref[there].astype(jnp.float32)).astype(jnp.bfloat16)
-        for j in range(per_tile):
-            place = tile * per_tile + j
-            owner = jnp.where(place < chips, core, 1 - core)
-            shares_ref[(place % chips) * CORES + owner] = total[j * tok_dev : (j + 1) * tok_dev]
+    def step(place, carry):
+        here = pl.ds(pl.multiple_of(place * size, size), size)
+        there = pl.ds(pl.multiple_of((place + chips) % devices * size, size), size)
+        owner = jnp.where(place < chips, core, 1 - core)
+        total = total_ref[here] + got_ref[there].astype(jnp.float32)
+        shares_ref[place % chips * CORES + owner] = total.astype(jnp.bfloat16)
         return carry
 
-    lax.fori_loop(0, tiles, step, 0, unroll=tiles <= 4)
-
-
-def share(total, got, tok_dev):
-    rows, columns = total.shape
+    lax.fori_loop(0, devices, step, 0, unroll=devices <= 32)
+
+
+def share(total, got, devices):
+    size = total.shape[0] // devices
     return pl.pallas_call(
         share_kernel,
-        out_shape=jax.ShapeDtypeStruct((rows // tok_dev, tok_dev, columns), jnp.bfloat16),
+        out_shape=jax.ShapeDtypeStruct((devices, size, LANES), jnp.bfloat16),
         in_specs=[VMEM] * 2,
         out_specs=VMEM,
-        compiler_params=vmem((8 << 20) + 32 * rows * columns),
+        compiler_params=vmem((8 << 20) + 32 * total.size),
     )(total, got)
 
 
-def sum_kernel(shares_ref, out_hbm, out_ref, sem):
-    devices, tok_dev, columns = shares_ref.shape
+def sum_kernel(shares_ref, out_hbm, wide_ref, out_ref, sem):
+    devices, size, _ = shares_ref.shape
+    _, tok_dev, width = out_ref.shape
+    groups = size // tok_dev
     for core in range(CORES):
-        zero = jnp.zeros((tok_dev, columns), jnp.float32)
         total = lax.fori_loop(
             0,
             devices // CORES,
             lambda i, acc: acc + shares_ref[i * CORES + core].astype(jnp.float32),
-            zero,
+            jnp.zeros((size, LANES), jnp.float32),
             unroll=devices <= 32,
         )
-        out_ref[0, :, core * columns : (core + 1) * columns] = total.astype(jnp.bfloat16)
+        for row in range(size):
+            token, lane = row // groups, (core * groups + row % groups) * LANES
+            wide_ref[token : token + 1, lane : lane + LANES] = total[row : row + 1]
+    out_ref[0] = wide_ref[...].astype(jnp.bfloat16)
     copy = pltpu.make_async_copy(out_ref, out_hbm, sem)
     copy.start()
     copy.wait()
 
 
-def sum_shares(shares):
-    devices, tok_dev, columns = shares.shape
-    out = (1, tok_dev, CORES * columns)
+def sum_shares(shares, tok_dev):
+    _, size, _ = shares.shape
+    width = CORES * size // tok_dev * LANES
     return pl.pallas_call(
         sum_kernel,
-        out_shape=pltpu.HBM(out, jnp.bfloat16),
+        out_shape=pltpu.HBM((1, tok_dev, width), jnp.bfloat16),
         in_specs=[VMEM],
         out_specs=HBM,
-        scratch_shapes=[pltpu.VMEM(out, jnp.bfloat16), pltpu.SemaphoreType.DMA],
+        scratch_shapes=[
+            pltpu.VMEM((tok_dev, width), jnp.float32),
+            pltpu.VMEM((1, tok_dev, width), jnp.bfloat16),
+            pltpu.SemaphoreType.DMA,
+        ],
         compiler_params=vmem(16 << 20),
     )(shares)
 
@@ -340,8 +356,7 @@
 def local(tokens, out_grad, expert_ids, gate_scores, w_gate, w_up, w_down):
     devices = lax.axis_size("expert") * lax.axis_size("dp")
     chips = devices // CORES
-    middle = lax.axis_size("dp") // CORES // 2
-    order = [(chip + middle) % chips for chip in range(chips)]
+    order = [chip_at(place) for place in range(chips)]
     same_core = [[chip * CORES + core for chip in order] for core in range(CORES)]
     everyone = [[chip * CORES + core for chip in order for core in range(CORES)]]
     core_pairs = [(d, d ^ 1) for d in range(devices)]
@@ -354,9 +369,12 @@
     )
     got = lax.ppermute(sent, BOTH, core_pairs)
     total = finish(gate_delta, up_delta, gate, up)
-    shares = share(total, got, tokens.shape[1])
+    shares = share(total, got, devices)
+    shares, gate_delta, up_delta, hidden = lax.optimization_barrier(
+        (shares, gate_delta, up_delta, hidden)
+    )
     shares = lax.all_to_all(shares, BOTH, 0, 0, axis_index_groups=everyone, tiled=True)
-    token_grad = sum_shares(shares)
+    token_grad = sum_shares(shares, tokens.shape[1])
     grad_down = jnp.dot(hidden.T, dy, preferred_element_type=jnp.float32)
     grad_gate = jnp.dot(x.T, gate_delta, preferred_element_type=jnp.float32)
     grad_up = jnp.dot(x.T, up_delta, preferred_element_type=jnp.float32)

time: 39.7 us -> 37.9 us (0.955)
  waiting for transfers between devices: 4.13 us -> 2.31 us
    all_to_all x1, waiting for transfers between devices: 4.13 us -> 2.08 us  [local(): lax.all_to_all(shares, BOTH, 0, 0, axis_index_groups=everyone, tiled=True)]
  transfers between devices with their start and end apart: 3 -> 3, of which waited for: 1 -> 2; matrix products, arithmetic and copies ran while one was open for 16% -> 16% of each run, Pallas kernels for 6% -> 6%
where the time goes in v1:
time: 37.9 us; the launch traced here: 37.6 us
  blocking collectives  16.2 us (43%)
  Pallas kernels  8.39 us (22%)
  matrix products  6.15 us (16%)
  starting transfers between devices  3.85 us (10%)
  waiting for transfers between devices  2.31 us (6%)
  between operations  0.68 us (2%)
    all_to_all x1, blocking collectives, local(): lax.all_to_all(copies, BOTH, 0, 0, axis_index_groups=same_core, tiled=True)  16.2 us
    pallas_call x1, Pallas kernels, rows_pass(): pl.pallas_call(rows_kernel, out_shape=(bf16((rows * groups, LANES)), pltp...  3.79 us
    all_to_all x1, starting transfers between devices, local(): lax.all_to_all(shares, BOTH, 0, 0, axis_index_groups=everyone, tiled=True)  3.27 us
    all_to_all x1, waiting for transfers between devices, local(): lax.all_to_all(shares, BOTH, 0, 0, axis_index_groups=everyone, tiled=True)  2.08 us
    dot_general x1, matrix products, local(): grad_up = jnp.dot(x.T, up_delta, preferred_element_type=jnp.float32)  2.06 us
    dot_general x1, matrix products, local(): grad_gate = jnp.dot(x.T, gate_delta, preferred_element_type=jnp.float32)  2.05 us
    dot_general x1, matrix products, local(): grad_down = jnp.dot(hidden.T, dy, preferred_element_type=jnp.float32)  2.04 us
    pallas_call x1, Pallas kernels, fetch(): pl.pallas_call(fetch_kernel, out_shape=(pltpu.VMEM((width, hidden), jnp.b...  1.55 us
  transfers between devices with their start and end apart: 3, of which 2 were waited for; matrix products, arithmetic and copies ran while one was open for 16% of the time, Pallas kernels for 6%

profile of v1, /device:TPU:0, one launch (start us, length us, event | category | flops | bytes accessed | tf_op | source)
XLA Modules:
  0.0 37.6 jit_solution(12505767767620809819)
XLA Ops:
  0.6 1.0 %shard_map.102 = bf16[16,2,4096]{2,1,0:T(2,128)(2,1)S(1)} custom-call(bf16[1,2,2048]{2,1,0:T(2,128)(2,1)} %tokens_hbm.1, bf16[1,2,2048]{2,1,0:T(2,128)(2,1)} %grad_hbm.1, s32[1,2,4]{2,1,0:T(2,128)} %bitcast.14, bf16[1,2,4]{2,1,0:T(2,128)(2,1)} %bitcast.15), custom_call_target="tpu_custom_call" | custom-call | tf_op jit(solution)/shard_map/pallas_call | solution.py:83
  1.6 16.2 %all_to_all.10.mine_ref = bf16[16,2,4096]{2,1,0:T(2,128)(2,1)S(1)} all-to-all(bf16[16,2,4096]{2,1,0:T(2,128)(2,1)S(1)} %shard_map.102), channel_id=1, replica_groups={{8,10,12,14,16,18,20,22,24,26,28,30,0,2,4,6},{9,11,13,15,17,19,21,23,25..., dimensions={0} | all-to-all | bytes 524288 | tf_op jit(solution)/shard_map/all_to_all | solution.py:364
  17.8 0.0 collective-permute-start
  17.8 1.6 %shard_map.103 = (bf16[2048,512]{1,0:T(8,128)(2,1)S(1)}, bf16[32,2048]{1,0:T(8,128)(2,1)S(1)}, bf16[32,2048]{1,0:T(8,128)(2,1)S(1)}) custom-call(bf16[16,2,4096]{2,1,0:T(2,128)(2,1)S(1)} %all_to_all.10.mine_ref, bf16[1,2048,512]{2,1,0:T(8,128)(2,1)} %gate_hbm.1), custom_call_target="tpu_custom_call" | custom-call | bytes 4194304 | tf_op jit(solution)/shard_map/pallas_call | solution.py:137
  19.4 0.0 collective-permute-done.other_ref
  19.4 3.8 %shard_map.104 = (bf16[512,128]{1,0:T(8,128)(2,1)S(1)}, bf16[2048,512]{1,0:T(8,128)(2,1)S(1)}, bf16[64,2048]{1,0:T(8,128)(2,1)S(1)}, bf16[64,2048]{1,0:T(8,128)(...) custom-call(bf16[16,2,4096]{2,1,0:T(2,128)(2,1)S(1)} %collective-permute-done.other_, ...), custom_call_target="tpu_custom_call" | custom-call | flops 536870912 | bytes 8060928 | tf_op jit(solution)/shard_map/pallas_call | solution.py:236
  23.2 0.6 %collective-permute-start.1 = (bf16[512,128]{1,0:T(8,128)(2,1)S(1)}, bf16[512,128]{1,0:T(8,128)(2,1)S(1)}, u32[]{:S(2)}, u32[]{:S(2)}) collective-permute-start(bf16[512,128]{1,0:T(8,128)(2,1)S(1)} %get-tuple-element.24), channel_id=1, source_target_pairs={{0,1},{1,0},{2,3},{3,2},{4,5},{5,4},{6,7},{7,6},{8,9},{9,8},{10,11... | collective-permute-start | bytes 393224 | tf_op jit(solution)/shard_map/ppermute | solution.py:370
  23.7 0.8 %shard_map.105.total_ref = f32[512,128]{1,0:T(8,128)S(1)} custom-call(bf16[64,512]{1,0:T(8,128)(2,1)S(1)} %get-tuple-element.28.gate_delta_ref, bf16[64,512]{1,0:T(8,128)(2,1)S(1)} %get-tuple-element.29.up_delta_ref, bf16[2048,512]{1,0:T(8,128)(2,1)S(1)} %get-tuple-element.20.gate_ref, bf16[2048,512]{1,0:T(8,128)(2,1)S(1)} %get-tuple-element.23.up_ref), custom_call_target="tpu_custom_call" | custom-call | flops 134217728 | bytes 2490368 | tf_op jit(solution)/shard_map/pallas_call | solution.py:279
  24.5 0.2 collective-permute-done.1.got_ref
  24.7 0.7 %shard_map.106 = bf16[32,16,128]{2,1,0:T(8,128)(2,1)} custom-call(f32[512,128]{1,0:T(8,128)S(1)} %shard_map.105.total_ref, bf16[512,128]{1,0:T(8,128)(2,1)S(1)} %collective-permute-done.1.got_ref), custom_call_target="tpu_custom_call" | custom-call | tf_op jit(solution)/shard_map/pallas_call | solution.py:309
  25.4 3.3 %all-to-all-start.1 = ((bf16[32,16,128]{2,1,0:T(8,128)(2,1)}), bf16[32,16,128]{2,1,0:T(8,128)(2,1)S(1)}, u32[]{:S(2)}, u32[]{:S(2)}) async-start(bf16[32,16,128]{2,1,0:T(8,128)(2,1)} %shard_map.106), calls=%async_computation.1 | async-start | bytes 262144 | tf_op jit(solution)/shard_map/all_to_all | solution.py:376
  28.7 2.1 %fusion = bf16[1,2048,512]{2,1,0:T(8,128)(2,1)} fusion(bf16[64,2048]{1,0:T(8,128)(2,1)S(1)} %get-tuple-element.27, bf16[64,512]{1,0:T(8,128)(2,1)S(1)} %get-tuple-element.28.gate_delta_ref), kind=kOutput, calls=%fused_computation.3 | convolution fusion | flops 135266304 | bytes 2424832 | tf_op jit(solution)/shard_map/dot_general | solution.py:379
  30.7 2.1 %fusion.1 = bf16[1,2048,512]{2,1,0:T(8,128)(2,1)} fusion(bf16[64,2048]{1,0:T(8,128)(2,1)S(1)} %get-tuple-element.27, bf16[64,512]{1,0:T(8,128)(2,1)S(1)} %get-tuple-element.29.up_delta_ref), kind=kOutput, calls=%fused_computation.4 | convolution fusion | flops 135266304 | bytes 2424832 | tf_op jit(solution)/shard_map/dot_general | solution.py:380
  32.8 2.0 %fusion.2 = bf16[1,512,2048]{2,1,0:T(8,128)(2,1)} fusion(bf16[64,512]{1,0:T(8,128)(2,1)S(1)} %get-tuple-element.30, bf16[64,2048]{1,0:T(8,128)(2,1)S(1)} %get-tuple-element.31), kind=kOutput, calls=%fused_computation.5 | convolution fusion | flops 135266304 | bytes 2424832 | tf_op jit(solution)/shard_map/dot_general | solution.py:378
  34.8 2.1 %all-to-all-done.1.shares_ref = bf16[32,16,128]{2,1,0:T(8,128)(2,1)S(1)} async-done(((bf16[32,16,128]{2,1,0:T(8,128)(2,1)}), bf16[32,16,128]{2,1,0:T(8,128)(2,1)S(1)}, u32[]{:S(2)}, u32[]{:S(2)}) %all-to-all-start.1) | async-done | bytes 131104 | tf_op jit(solution)/shard_map/all_to_all | solution.py:376
  36.9 0.6 %shard_map.107 = bf16[1,2,2048]{2,1,0:T(2,128)(2,1)} custom-call(bf16[32,16,128]{2,1,0:T(8,128)(2,1)S(1)} %all-to-all-done.1.shares_ref), custom_call_target="tpu_custom_call" | custom-call | tf_op jit(solution)/shard_map/pallas_call | solution.py:342
Async XLA Ops:
  17.8 1.6 %collective-permute-start = (bf16[16,2,4096]{2,1,0:T(2,128)(2,1)S(1)}, bf16[16,2,4096]{2,1,0:T(2,128)(2,1)S(1)}, u32[]{:S(2)}, u32[]{:S(2)}) collective-permute-start(bf16[16,2,4096]{2,1,0:T(2,128)(2,1)S(1)} %all_to_all.10.mine_ref), channel_id=1, source_target_pairs={{0,1},{1,0},{2,3},{3,2},{4,5},{5,4},{6,7},{7,6},{8,9},{9,8},{10,11... | collective-permute-start | bytes 786440 | tf_op jit(solution)/shard_map/ppermute | solution.py:365
  23.2 1.6 %collective-permute-start.1 = (bf16[512,128]{1,0:T(8,128)(2,1)S(1)}, bf16[512,128]{1,0:T(8,128)(2,1)S(1)}, u32[]{:S(2)}, u32[]{:S(2)}) collective-permute-start(bf16[512,128]{1,0:T(8,128)(2,1)S(1)} %get-tuple-element.24), channel_id=1, source_target_pairs={{0,1},{1,0},{2,3},{3,2},{4,5},{5,4},{6,7},{7,6},{8,9},{9,8},{10,11... | collective-permute-start | bytes 393224 | tf_op jit(solution)/shard_map/ppermute | solution.py:370
  25.4 11.5 %all-to-all-start.1 = ((bf16[32,16,128]{2,1,0:T(8,128)(2,1)}), bf16[32,16,128]{2,1,0:T(8,128)(2,1)S(1)}, u32[]{:S(2)}, u32[]{:S(2)}) async-start(bf16[32,16,128]{2,1,0:T(8,128)(2,1)} %shard_map.106), calls=%async_computation.1 | async-start | bytes 262144 | tf_op jit(solution)/shard_map/all_to_all | solution.py:376

commit v2 on v1

--- a/solution.py
+++ b/solution.py
@@ -23,8 +23,12 @@
 
 
 def chip_at(place):
+    experts = lax.axis_size("expert")
     per_expert = lax.axis_size("dp") // CORES
-    return (place + per_expert // 2) % (per_expert * lax.axis_size("expert"))
+    upper = 1 - place % 2
+    rank = place // 2 // experts
+    within = per_expert // 2 + upper * rank - (1 - upper) * (1 + rank)
+    return place // 2 % experts * per_expert + within
 
 
 def pack_kernel(
@@ -308,7 +312,7 @@
     size = total.shape[0] // devices
     return pl.pallas_call(
         share_kernel,
-        out_shape=jax.ShapeDtypeStruct((devices, size, LANES), jnp.bfloat16),
+        out_shape=pltpu.VMEM((devices, size, LANES), jnp.bfloat16),
         in_specs=[VMEM] * 2,
         out_specs=VMEM,
         compiler_params=vmem((8 << 20) + 32 * total.size),

time: 37.9 us -> 37.6 us (level)
  transfers between devices with their start and end apart: 3 -> 3, of which waited for: 2 -> 2; matrix products, arithmetic and copies ran while one was open for 16% -> 17% of each run, Pallas kernels for 6% -> 6%
where the time goes in v2:
time: 37.6 us; the launch traced here: 37.2 us
  blocking collectives  16.2 us (43%)
  Pallas kernels  8.39 us (22%)
  matrix products  6.15 us (16%)
  starting transfers between devices  3.81 us (10%)
  waiting for transfers between devices  2 us (5%)
  between operations  0.68 us (2%)
    all_to_all x1, blocking collectives, local(): lax.all_to_all(copies, BOTH, 0, 0, axis_index_groups=same_core, tiled=True)  16.2 us
    pallas_call x1, Pallas kernels, rows_pass(): pl.pallas_call(rows_kernel, out_shape=(bf16((rows * groups, LANES)), pltp...  3.79 us
    all_to_all x1, starting transfers between devices, local(): lax.all_to_all(shares, BOTH, 0, 0, axis_index_groups=everyone, tiled=True)  3.23 us
    dot_general x1, matrix products, local(): grad_up = jnp.dot(x.T, up_delta, preferred_element_type=jnp.float32)  2.06 us
    dot_general x1, matrix products, local(): grad_gate = jnp.dot(x.T, gate_delta, preferred_element_type=jnp.float32)  2.05 us
    dot_general x1, matrix products, local(): grad_down = jnp.dot(hidden.T, dy, preferred_element_type=jnp.float32)  2.04 us
    all_to_all x1, waiting for transfers between devices, local(): lax.all_to_all(shares, BOTH, 0, 0, axis_index_groups=everyone, tiled=True)  1.76 us
    pallas_call x1, Pallas kernels, fetch(): pl.pallas_call(fetch_kernel, out_shape=(pltpu.VMEM((width, hidden), jnp.b...  1.55 us
  transfers between devices with their start and end apart: 3, of which 2 were waited for; matrix products, arithmetic and copies ran while one was open for 17% of the time, Pallas kernels for 6%

profile of v2, /device:TPU:0, one launch (start us, length us, event | category | flops | bytes accessed | tf_op | source)
XLA Modules:
  0.0 37.2 jit_solution(7653359325155934487)
XLA Ops:
  0.6 1.0 %shard_map.102 = bf16[16,2,4096]{2,1,0:T(2,128)(2,1)S(1)} custom-call(bf16[1,2,2048]{2,1,0:T(2,128)(2,1)} %tokens_hbm.1, bf16[1,2,2048]{2,1,0:T(2,128)(2,1)} %grad_hbm.1, s32[1,2,4]{2,1,0:T(2,128)} %bitcast.14, bf16[1,2,4]{2,1,0:T(2,128)(2,1)} %bitcast.15), custom_call_target="tpu_custom_call" | custom-call | tf_op jit(solution)/shard_map/pallas_call | solution.py:87
  1.6 16.2 %all_to_all.10.mine_ref = bf16[16,2,4096]{2,1,0:T(2,128)(2,1)S(1)} all-to-all(bf16[16,2,4096]{2,1,0:T(2,128)(2,1)S(1)} %shard_map.102), channel_id=1, replica_groups={{8,6,24,22,10,4,26,20,12,2,28,18,14,0,30,16},{9,7,25,23,11,5,27,21,13,3..., dimensions={0} | all-to-all | bytes 524288 | tf_op jit(solution)/shard_map/all_to_all | solution.py:368
  17.8 0.0 collective-permute-start
  17.8 1.6 %shard_map.103 = (bf16[2048,512]{1,0:T(8,128)(2,1)S(1)}, bf16[32,2048]{1,0:T(8,128)(2,1)S(1)}, bf16[32,2048]{1,0:T(8,128)(2,1)S(1)}) custom-call(bf16[16,2,4096]{2,1,0:T(2,128)(2,1)S(1)} %all_to_all.10.mine_ref, bf16[1,2048,512]{2,1,0:T(8,128)(2,1)} %gate_hbm.1), custom_call_target="tpu_custom_call" | custom-call | bytes 4194304 | tf_op jit(solution)/shard_map/pallas_call | solution.py:141
  19.4 0.0 collective-permute-done.other_ref
  19.4 3.8 %shard_map.104 = (bf16[512,128]{1,0:T(8,128)(2,1)S(1)}, bf16[2048,512]{1,0:T(8,128)(2,1)S(1)}, bf16[64,2048]{1,0:T(8,128)(2,1)S(1)}, bf16[64,2048]{1,0:T(8,128)(...) custom-call(bf16[16,2,4096]{2,1,0:T(2,128)(2,1)S(1)} %collective-permute-done.other_, ...), custom_call_target="tpu_custom_call" | custom-call | flops 536870912 | bytes 8060928 | tf_op jit(solution)/shard_map/pallas_call | solution.py:240
  23.2 0.6 %collective-permute-start.1 = (bf16[512,128]{1,0:T(8,128)(2,1)S(1)}, bf16[512,128]{1,0:T(8,128)(2,1)S(1)}, u32[]{:S(2)}, u32[]{:S(2)}) collective-permute-start(bf16[512,128]{1,0:T(8,128)(2,1)S(1)} %get-tuple-element.24), channel_id=1, source_target_pairs={{0,1},{1,0},{2,3},{3,2},{4,5},{5,4},{6,7},{7,6},{8,9},{9,8},{10,11... | collective-permute-start | bytes 393224 | tf_op jit(solution)/shard_map/ppermute | solution.py:374
  23.8 0.8 %shard_map.105.total_ref = f32[512,128]{1,0:T(8,128)S(1)} custom-call(bf16[64,512]{1,0:T(8,128)(2,1)S(1)} %get-tuple-element.28.gate_delta_ref, bf16[64,512]{1,0:T(8,128)(2,1)S(1)} %get-tuple-element.29.up_delta_ref, bf16[2048,512]{1,0:T(8,128)(2,1)S(1)} %get-tuple-element.20.gate_ref, bf16[2048,512]{1,0:T(8,128)(2,1)S(1)} %get-tuple-element.23.up_ref), custom_call_target="tpu_custom_call" | custom-call | flops 134217728 | bytes 2490368 | tf_op jit(solution)/shard_map/pallas_call | solution.py:283
  24.5 0.2 collective-permute-done.1.got_ref
  24.8 0.7 %shard_map.106 = bf16[32,16,128]{2,1,0:T(8,128)(2,1)} custom-call(f32[512,128]{1,0:T(8,128)S(1)} %shard_map.105.total_ref, bf16[512,128]{1,0:T(8,128)(2,1)S(1)} %collective-permute-done.1.got_ref), custom_call_target="tpu_custom_call" | custom-call | tf_op jit(solution)/shard_map/pallas_call | solution.py:313
  25.4 3.2 %all-to-all-start.1 = ((bf16[32,16,128]{2,1,0:T(8,128)(2,1)}), bf16[32,16,128]{2,1,0:T(8,128)(2,1)S(1)}, u32[]{:S(2)}, u32[]{:S(2)}) async-start(bf16[32,16,128]{2,1,0:T(8,128)(2,1)} %shard_map.106), calls=%async_computation.1 | async-start | bytes 262144 | tf_op jit(solution)/shard_map/all_to_all | solution.py:380
  28.7 2.0 %fusion = bf16[1,2048,512]{2,1,0:T(8,128)(2,1)} fusion(bf16[64,2048]{1,0:T(8,128)(2,1)S(1)} %get-tuple-element.27, bf16[64,512]{1,0:T(8,128)(2,1)S(1)} %get-tuple-element.28.gate_delta_ref), kind=kOutput, calls=%fused_computation.3 | convolution fusion | flops 135266304 | bytes 2424832 | tf_op jit(solution)/shard_map/dot_general | solution.py:383
  30.7 2.1 %fusion.1 = bf16[1,2048,512]{2,1,0:T(8,128)(2,1)} fusion(bf16[64,2048]{1,0:T(8,128)(2,1)S(1)} %get-tuple-element.27, bf16[64,512]{1,0:T(8,128)(2,1)S(1)} %get-tuple-element.29.up_delta_ref), kind=kOutput, calls=%fused_computation.4 | convolution fusion | flops 135266304 | bytes 2424832 | tf_op jit(solution)/shard_map/dot_general | solution.py:384
  32.8 2.0 %fusion.2 = bf16[1,512,2048]{2,1,0:T(8,128)(2,1)} fusion(bf16[64,512]{1,0:T(8,128)(2,1)S(1)} %get-tuple-element.30, bf16[64,2048]{1,0:T(8,128)(2,1)S(1)} %get-tuple-element.31), kind=kOutput, calls=%fused_computation.5 | convolution fusion | flops 135266304 | bytes 2424832 | tf_op jit(solution)/shard_map/dot_general | solution.py:382
  34.8 1.8 %all-to-all-done.1.shares_ref = bf16[32,16,128]{2,1,0:T(8,128)(2,1)S(1)} async-done(((bf16[32,16,128]{2,1,0:T(8,128)(2,1)}), bf16[32,16,128]{2,1,0:T(8,128)(2,1)S(1)}, u32[]{:S(2)}, u32[]{:S(2)}) %all-to-all-start.1) | async-done | bytes 131104 | tf_op jit(solution)/shard_map/all_to_all | solution.py:380
  36.6 0.6 %shard_map.107 = bf16[1,2,2048]{2,1,0:T(2,128)(2,1)} custom-call(bf16[32,16,128]{2,1,0:T(8,128)(2,1)S(1)} %all-to-all-done.1.shares_ref), custom_call_target="tpu_custom_call" | custom-call | tf_op jit(solution)/shard_map/pallas_call | solution.py:346
Async XLA Ops:
  17.8 1.6 %collective-permute-start = (bf16[16,2,4096]{2,1,0:T(2,128)(2,1)S(1)}, bf16[16,2,4096]{2,1,0:T(2,128)(2,1)S(1)}, u32[]{:S(2)}, u32[]{:S(2)}) collective-permute-start(bf16[16,2,4096]{2,1,0:T(2,128)(2,1)S(1)} %all_to_all.10.mine_ref), channel_id=1, source_target_pairs={{0,1},{1,0},{2,3},{3,2},{4,5},{5,4},{6,7},{7,6},{8,9},{9,8},{10,11... | collective-permute-start | bytes 786440 | tf_op jit(solution)/shard_map/ppermute | solution.py:369
  23.2 1.6 %collective-permute-start.1 = (bf16[512,128]{1,0:T(8,128)(2,1)S(1)}, bf16[512,128]{1,0:T(8,128)(2,1)S(1)}, u32[]{:S(2)}, u32[]{:S(2)}) collective-permute-start(bf16[512,128]{1,0:T(8,128)(2,1)S(1)} %get-tuple-element.24), channel_id=1, source_target_pairs={{0,1},{1,0},{2,3},{3,2},{4,5},{5,4},{6,7},{7,6},{8,9},{9,8},{10,11... | collective-permute-start | bytes 393224 | tf_op jit(solution)/shard_map/ppermute | solution.py:374
  25.4 11.2 %all-to-all-start.1 = ((bf16[32,16,128]{2,1,0:T(8,128)(2,1)}), bf16[32,16,128]{2,1,0:T(8,128)(2,1)S(1)}, u32[]{:S(2)}, u32[]{:S(2)}) async-start(bf16[32,16,128]{2,1,0:T(8,128)(2,1)} %shard_map.106), calls=%async_computation.1 | async-start | bytes 262144 | tf_op jit(solution)/shard_map/all_to_all | solution.py:380

commit v3 on v2

--- a/solution.py
+++ b/solution.py
@@ -186,8 +186,8 @@
     sent_ref, up_ref, x_ref, dy_ref, gate_delta_ref, up_delta_ref, hidden_ref,
     down_ref, total_ref, sems,
 ):
-    up_copies = copy_pieces(up_hbm, up_ref, sems.at[0])
-    down_copies = copy_pieces(down_hbm, down_ref, sems.at[1])
+    down_copies = copy_pieces(down_hbm, down_ref, sems.at[0])
+    up_copies = copy_pieces(up_hbm, up_ref, sems.at[1])
     half = my_x_ref.shape[0]
     x_ref[:half] = my_x_ref[...]
     dy_ref[:half] = my_dy_ref[...]
@@ -200,6 +200,13 @@
         pre_gate = jnp.dot(x, gate_ref[...], preferred_element_type=jnp.float32)
         sigmoid_gate = jax.nn.sigmoid(pre_gate)
         activated = pre_gate * sigmoid_gate
+        slope = sigmoid_gate * (1.0 + pre_gate * (1.0 - sigmoid_gate))
+        if first:
+            for copy in down_copies:
+                copy.wait()
+        grad_hidden = lax.dot_general(
+            dy_ref[rows], down_ref[...], CONTRACT_LAST, preferred_element_type=jnp.float32
+        )
         pre_up = None
         for piece, copy in enumerate(up_copies):
             if first:
@@ -208,15 +215,7 @@
             product = jnp.dot(x[:, part], up_ref[part], preferred_element_type=jnp.float32)
             pre_up = product if pre_up is None else pre_up + product
         hidden_ref[rows] = (activated * pre_up).astype(jnp.bfloat16)
-        if first:
-            for copy in down_copies:
-                copy.wait()
-        grad_hidden = lax.dot_general(
-            dy_ref[rows], down_ref[...], CONTRACT_LAST, preferred_element_type=jnp.float32
-        )
-        gate_delta = (
-            grad_hidden * pre_up * sigmoid_gate * (1.0 + pre_gate * (1.0 - sigmoid_gate))
-        ).astype(jnp.bfloat16)
+        gate_delta = (grad_hidden * pre_up * slope).astype(jnp.bfloat16)
         up_delta = (grad_hidden * activated).astype(jnp.bfloat16)
         gate_delta_ref[rows] = gate_delta
         up_delta_ref[rows] = up_delta
@@ -302,7 +301,7 @@
         there = pl.ds(pl.multiple_of((place + chips) % devices * size, size), size)
         owner = jnp.where(place < chips, core, 1 - core)
         total = total_ref[here] + got_ref[there].astype(jnp.float32)
-        shares_ref[place % chips * CORES + owner] = total.astype(jnp.bfloat16)
+        shares_ref[chip_at(place % chips) * CORES + owner] = total.astype(jnp.bfloat16)
         return carry
 
     lax.fori_loop(0, devices, step, 0, unroll=devices <= 32)
@@ -362,7 +361,6 @@
     chips = devices // CORES
     order = [chip_at(place) for place in range(chips)]
     same_core = [[chip * CORES + core for chip in order] for core in range(CORES)]
-    everyone = [[chip * CORES + core for chip in order for core in range(CORES)]]
     core_pairs = [(d, d ^ 1) for d in range(devices)]
     copies = pack(tokens, out_grad, expert_ids, gate_scores, chips)
     mine = lax.all_to_all(copies, BOTH, 0, 0, axis_index_groups=same_core, tiled=True)
@@ -377,7 +375,7 @@
     shares, gate_delta, up_delta, hidden = lax.optimization_barrier(
         (shares, gate_delta, up_delta, hidden)
     )
-    shares = lax.all_to_all(shares, BOTH, 0, 0, axis_index_groups=everyone, tiled=True)
+    shares = lax.all_to_all(shares, BOTH, 0, 0, tiled=True)
     token_grad = sum_shares(shares, tokens.shape[1])
     grad_down = jnp.dot(hidden.T, dy, preferred_element_type=jnp.float32)
     grad_gate = jnp.dot(x.T, gate_delta, preferred_element_type=jnp.float32)

time: 37.6 us -> 38 us (1.011)
  transfers between devices with their start and end apart: 3 -> 3, of which waited for: 2 -> 2; matrix products, arithmetic and copies ran while one was open for 17% -> 16% of each run, Pallas kernels for 6% -> 6%
where the time goes in v3:
time: 38 us; the launch traced here: 37.7 us
  blocking collectives  16.2 us (43%)
  Pallas kernels  8.57 us (23%)
  matrix products  6.15 us (16%)
  starting transfers between devices  3.81 us (10%)
  waiting for transfers between devices  2.31 us (6%)
  between operations  0.68 us (2%)
    all_to_all x1, blocking collectives, local(): lax.all_to_all(copies, BOTH, 0, 0, axis_index_groups=same_core, tiled=True)  16.2 us
    pallas_call x1, Pallas kernels, rows_pass(): pl.pallas_call(rows_kernel, out_shape=(bf16((rows * groups, LANES)), pltp...  3.97 us
    all_to_all x1, starting transfers between devices, local(): shares = lax.all_to_all(shares, BOTH, 0, 0, tiled=True)  3.23 us
    all_to_all x1, waiting for transfers between devices, local(): shares = lax.all_to_all(shares, BOTH, 0, 0, tiled=True)  2.08 us
    dot_general x1, matrix products, local(): grad_up = jnp.dot(x.T, up_delta, preferred_element_type=jnp.float32)  2.06 us
    dot_general x1, matrix products, local(): grad_gate = jnp.dot(x.T, gate_delta, preferred_element_type=jnp.float32)  2.05 us
    dot_general x1, matrix products, local(): grad_down = jnp.dot(hidden.T, dy, preferred_element_type=jnp.float32)  2.04 us
    pallas_call x1, Pallas kernels, fetch(): pl.pallas_call(fetch_kernel, out_shape=(pltpu.VMEM((width, hidden), jnp.b...  1.55 us
  transfers between devices with their start and end apart: 3, of which 2 were waited for; matrix products, arithmetic and copies ran while one was open for 16% of the time, Pallas kernels for 6%

profile of v3, /device:TPU:0, one launch (start us, length us, event | category | flops | bytes accessed | tf_op | source)
XLA Modules:
  0.0 37.7 jit_solution(2927286523030961311)
XLA Ops:
  0.6 1.0 %shard_map.102 = bf16[16,2,4096]{2,1,0:T(2,128)(2,1)S(1)} custom-call(bf16[1,2,2048]{2,1,0:T(2,128)(2,1)} %tokens_hbm.1, bf16[1,2,2048]{2,1,0:T(2,128)(2,1)} %grad_hbm.1, s32[1,2,4]{2,1,0:T(2,128)} %bitcast.14, bf16[1,2,4]{2,1,0:T(2,128)(2,1)} %bitcast.15), custom_call_target="tpu_custom_call" | custom-call | tf_op jit(solution)/shard_map/pallas_call | solution.py:87
  1.6 16.2 %all_to_all.10.mine_ref = bf16[16,2,4096]{2,1,0:T(2,128)(2,1)S(1)} all-to-all(bf16[16,2,4096]{2,1,0:T(2,128)(2,1)S(1)} %shard_map.102), channel_id=1, replica_groups={{8,6,24,22,10,4,26,20,12,2,28,18,14,0,30,16},{9,7,25,23,11,5,27,21,13,3..., dimensions={0} | all-to-all | bytes 524288 | tf_op jit(solution)/shard_map/all_to_all | solution.py:366
  17.8 0.0 collective-permute-start
  17.8 1.6 %shard_map.103 = (bf16[2048,512]{1,0:T(8,128)(2,1)S(1)}, bf16[32,2048]{1,0:T(8,128)(2,1)S(1)}, bf16[32,2048]{1,0:T(8,128)(2,1)S(1)}) custom-call(bf16[16,2,4096]{2,1,0:T(2,128)(2,1)S(1)} %all_to_all.10.mine_ref, bf16[1,2048,512]{2,1,0:T(8,128)(2,1)} %gate_hbm.1), custom_call_target="tpu_custom_call" | custom-call | bytes 4194304 | tf_op jit(solution)/shard_map/pallas_call | solution.py:141
  19.4 0.0 collective-permute-done.other_ref
  19.4 4.0 %shard_map.104 = (bf16[512,128]{1,0:T(8,128)(2,1)S(1)}, bf16[2048,512]{1,0:T(8,128)(2,1)S(1)}, bf16[64,2048]{1,0:T(8,128)(2,1)S(1)}, bf16[64,2048]{1,0:T(8,128)(...) custom-call(bf16[16,2,4096]{2,1,0:T(2,128)(2,1)S(1)} %collective-permute-done.other_, ...), custom_call_target="tpu_custom_call" | custom-call | flops 536870912 | bytes 8060928 | tf_op jit(solution)/shard_map/pallas_call | solution.py:239
  23.4 0.6 %collective-permute-start.1 = (bf16[512,128]{1,0:T(8,128)(2,1)S(1)}, bf16[512,128]{1,0:T(8,128)(2,1)S(1)}, u32[]{:S(2)}, u32[]{:S(2)}) collective-permute-start(bf16[512,128]{1,0:T(8,128)(2,1)S(1)} %get-tuple-element.24), channel_id=1, source_target_pairs={{0,1},{1,0},{2,3},{3,2},{4,5},{5,4},{6,7},{7,6},{8,9},{9,8},{10,11... | collective-permute-start | bytes 393224 | tf_op jit(solution)/shard_map/ppermute | solution.py:372
  24.0 0.8 %shard_map.105.total_ref = f32[512,128]{1,0:T(8,128)S(1)} custom-call(bf16[64,512]{1,0:T(8,128)(2,1)S(1)} %get-tuple-element.28.gate_delta_ref, bf16[64,512]{1,0:T(8,128)(2,1)S(1)} %get-tuple-element.29.up_delta_ref, bf16[2048,512]{1,0:T(8,128)(2,1)S(1)} %get-tuple-element.20.gate_ref, bf16[2048,512]{1,0:T(8,128)(2,1)S(1)} %get-tuple-element.23.up_ref), custom_call_target="tpu_custom_call" | custom-call | flops 134217728 | bytes 2490368 | tf_op jit(solution)/shard_map/pallas_call | solution.py:282
  24.7 0.2 collective-permute-done.1.got_ref
  25.0 0.7 %shard_map.106 = bf16[32,16,128]{2,1,0:T(8,128)(2,1)} custom-call(f32[512,128]{1,0:T(8,128)S(1)} %shard_map.105.total_ref, bf16[512,128]{1,0:T(8,128)(2,1)S(1)} %collective-permute-done.1.got_ref), custom_call_target="tpu_custom_call" | custom-call | tf_op jit(solution)/shard_map/pallas_call | solution.py:312
  25.6 3.2 %all-to-all-start.1 = ((bf16[32,16,128]{2,1,0:T(8,128)(2,1)}), bf16[32,16,128]{2,1,0:T(8,128)(2,1)S(1)}, u32[]{:S(2)}, u32[]{:S(2)}) async-start(bf16[32,16,128]{2,1,0:T(8,128)(2,1)} %shard_map.106), calls=%async_computation.1 | async-start | bytes 262144 | tf_op jit(solution)/shard_map/all_to_all | solution.py:378
  28.9 2.0 %fusion = bf16[1,2048,512]{2,1,0:T(8,128)(2,1)} fusion(bf16[64,2048]{1,0:T(8,128)(2,1)S(1)} %get-tuple-element.27, bf16[64,512]{1,0:T(8,128)(2,1)S(1)} %get-tuple-element.28.gate_delta_ref), kind=kOutput, calls=%fused_computation.3 | convolution fusion | flops 135266304 | bytes 2424832 | tf_op jit(solution)/shard_map/dot_general | solution.py:381
  30.9 2.1 %fusion.1 = bf16[1,2048,512]{2,1,0:T(8,128)(2,1)} fusion(bf16[64,2048]{1,0:T(8,128)(2,1)S(1)} %get-tuple-element.27, bf16[64,512]{1,0:T(8,128)(2,1)S(1)} %get-tuple-element.29.up_delta_ref), kind=kOutput, calls=%fused_computation.4 | convolution fusion | flops 135266304 | bytes 2424832 | tf_op jit(solution)/shard_map/dot_general | solution.py:382
  33.0 2.0 %fusion.2 = bf16[1,512,2048]{2,1,0:T(8,128)(2,1)} fusion(bf16[64,512]{1,0:T(8,128)(2,1)S(1)} %get-tuple-element.30, bf16[64,2048]{1,0:T(8,128)(2,1)S(1)} %get-tuple-element.31), kind=kOutput, calls=%fused_computation.5 | convolution fusion | flops 135266304 | bytes 2424832 | tf_op jit(solution)/shard_map/dot_general | solution.py:380
  35.0 2.1 %all-to-all-done.1.shares_ref = bf16[32,16,128]{2,1,0:T(8,128)(2,1)S(1)} async-done(((bf16[32,16,128]{2,1,0:T(8,128)(2,1)}), bf16[32,16,128]{2,1,0:T(8,128)(2,1)S(1)}, u32[]{:S(2)}, u32[]{:S(2)}) %all-to-all-start.1) | async-done | bytes 131104 | tf_op jit(solution)/shard_map/all_to_all | solution.py:378
  37.1 0.6 %shard_map.107 = bf16[1,2,2048]{2,1,0:T(2,128)(2,1)} custom-call(bf16[32,16,128]{2,1,0:T(8,128)(2,1)S(1)} %all-to-all-done.1.shares_ref), custom_call_target="tpu_custom_call" | custom-call | tf_op jit(solution)/shard_map/pallas_call | solution.py:345
Async XLA Ops:
  17.8 1.6 %collective-permute-start = (bf16[16,2,4096]{2,1,0:T(2,128)(2,1)S(1)}, bf16[16,2,4096]{2,1,0:T(2,128)(2,1)S(1)}, u32[]{:S(2)}, u32[]{:S(2)}) collective-permute-start(bf16[16,2,4096]{2,1,0:T(2,128)(2,1)S(1)} %all_to_all.10.mine_ref), channel_id=1, source_target_pairs={{0,1},{1,0},{2,3},{3,2},{4,5},{5,4},{6,7},{7,6},{8,9},{9,8},{10,11... | collective-permute-start | bytes 786440 | tf_op jit(solution)/shard_map/ppermute | solution.py:367
  23.4 1.6 %collective-permute-start.1 = (bf16[512,128]{1,0:T(8,128)(2,1)S(1)}, bf16[512,128]{1,0:T(8,128)(2,1)S(1)}, u32[]{:S(2)}, u32[]{:S(2)}) collective-permute-start(bf16[512,128]{1,0:T(8,128)(2,1)S(1)} %get-tuple-element.24), channel_id=1, source_target_pairs={{0,1},{1,0},{2,3},{3,2},{4,5},{5,4},{6,7},{7,6},{8,9},{9,8},{10,11... | collective-permute-start | bytes 393224 | tf_op jit(solution)/shard_map/ppermute | solution.py:372
  25.6 11.5 %all-to-all-start.1 = ((bf16[32,16,128]{2,1,0:T(8,128)(2,1)}), bf16[32,16,128]{2,1,0:T(8,128)(2,1)S(1)}, u32[]{:S(2)}, u32[]{:S(2)}) async-start(bf16[32,16,128]{2,1,0:T(8,128)(2,1)} %shard_map.106), calls=%async_computation.1 | async-start | bytes 262144 | tf_op jit(solution)/shard_map/all_to_all | solution.py:378

commit v4 on v3

--- a/solution.py
+++ b/solution.py
@@ -33,7 +33,7 @@
 
 def pack_kernel(
     tokens_hbm, grad_hbm, ids_hbm, scores_hbm, out_ref,
-    tokens_ref, grad_ref, ids_ref, scores_ref, weighted_ref, sems,
+    tokens_ref, grad_ref, ids_ref, scores_ref, wide_ref, block_ref, sems,
 ):
     copies = [
         pltpu.make_async_copy(src, dst, sems.at[i])
@@ -48,8 +48,8 @@
         copy.start()
     for copy in copies:
         copy.wait()
-    chips, tok_dev, _ = out_ref.shape
-    width = tokens_ref.shape[2]
+    chips, size, _ = out_ref.shape
+    _, tok_dev, width = tokens_ref.shape
     experts = lax.axis_size("expert")
     first = lax.axis_index("expert") * tok_dev
     ids = ids_ref[0]
@@ -64,20 +64,26 @@
         score = jnp.sum(jnp.where(mine, scores, 0.0), axis=1, keepdims=True)
         weights = jnp.sum(jnp.where(lane == named, score, 0.0), axis=0, keepdims=True)
         table = jnp.where(row == i, weights, table)
+    def put(first, value):
+        for c in range(width // LANES):
+            at = first + c * tok_dev
+            wide_ref[at : at + tok_dev] = value[:, c * LANES : (c + 1) * LANES]
+
+    put(0, tokens_ref[0].astype(jnp.float32))
     grad = grad_ref[0].astype(jnp.float32)
     for expert in range(experts):
-        weighted_ref[expert] = (grad * table[:, expert : expert + 1]).astype(jnp.bfloat16)
+        put(size // 2, grad * table[:, expert : expert + 1])
+        block_ref[expert] = wide_ref[...].astype(jnp.bfloat16)
 
     def write(place, carry):
-        out_ref[place, :, :width] = tokens_ref[0]
-        out_ref[place, :, width:] = weighted_ref[chip_at(place) // (chips // experts)]
+        out_ref[place] = block_ref[chip_at(place) // (chips // experts)]
         return carry
 
     lax.fori_loop(0, chips, write, 0, unroll=chips <= 16)
 
 
 def pack(tokens, out_grad, expert_ids, gate_scores, chips):
-    _, tok_dev, width = tokens.shape
+    size = 2 * tokens.size // LANES
     operands = [
         pltpu.with_memory_space_constraint(a, pltpu.HBM)
         for a in (
@@ -86,12 +92,13 @@
     ]
     return pl.pallas_call(
         pack_kernel,
-        out_shape=jax.ShapeDtypeStruct((chips, tok_dev, 2 * width), jnp.bfloat16),
+        out_shape=jax.ShapeDtypeStruct((chips, size, LANES), jnp.bfloat16),
         in_specs=[HBM] * 4,
         out_specs=VMEM,
         scratch_shapes=[pltpu.VMEM(a.shape, a.dtype) for a in operands]
         + [
-            pltpu.VMEM((lax.axis_size("expert"), tok_dev, width), jnp.bfloat16),
+            pltpu.VMEM((size, LANES), jnp.float32),
+            pltpu.VMEM((lax.axis_size("expert"), size, LANES), jnp.bfloat16),
             pltpu.SemaphoreType.DMA((4,)),
         ],
         compiler_params=vmem(16 << 20),
@@ -110,33 +117,43 @@
     return copies
 
 
-def lay_out(src_ref, x_ref, dy_ref, first):
-    chips, tok_dev, _ = src_ref.shape
-    width = x_ref.shape[1]
-    per_tile = TILE // tok_dev
+def lay_out(src_ref, x_ref, dy_ref, wide_ref, first):
+    chips, size, _ = src_ref.shape
+    groups = x_ref.shape[1] // LANES
+    tok_dev = size // 2 // groups
 
     def step(tile, carry):
-        rows = pl.ds(pl.multiple_of(first + tile * TILE, TILE), TILE)
-        blocks = [src_ref[tile * per_tile + j] for j in range(per_tile)]
-        x_ref[rows] = jnp.concatenate([b[:, :width] for b in blocks], axis=0)
-        dy_ref[rows] = jnp.concatenate([b[:, width:] for b in blocks], axis=0)
+        for j in range(TILE):
+            wide_ref[j * size : (j + 1) * size] = src_ref[tile * TILE + j].astype(jnp.float32)
+        for t in range(tok_dev):
+            rows = pl.ds(pl.multiple_of(first + t * chips + tile * TILE, TILE), TILE)
+            for c in range(groups):
+                lanes = slice(c * LANES, (c + 1) * LANES)
+                for half, ref in enumerate((x_ref, dy_ref)):
+                    at = half * size // 2 + c * tok_dev + t
+                    ref[rows, lanes] = wide_ref[pl.ds(at, TILE, stride=size)].astype(
+                        jnp.bfloat16
+                    )
         return carry
 
-    tiles = chips // per_tile
-    lax.fori_loop(0, tiles, step, 0, unroll=tiles <= 2)
-
-
-def fetch_kernel(mine_ref, gate_hbm, gate_ref, x_ref, dy_ref, sems):
+    tiles = chips // TILE
+    if tiles == 1:
+        step(0, 0)
+    else:
+        lax.fori_loop(0, tiles, step, 0)
+
+
+def fetch_kernel(mine_ref, gate_hbm, gate_ref, x_ref, dy_ref, wide_ref, sems):
     copies = copy_pieces(gate_hbm, gate_ref, sems)
-    lay_out(mine_ref, x_ref, dy_ref, 0)
+    lay_out(mine_ref, x_ref, dy_ref, wide_ref, 0)
     for copy in copies:
         copy.wait()
 
 
 def fetch(mine, w_gate):
-    chips, tok_dev, row = mine.shape
+    chips, size, _ = mine.shape
     _, width, hidden = w_gate.shape
-    half = chips * tok_dev
+    half = chips * size * LANES // 2 // width
     moved = 2 * width * hidden
     return pl.pallas_call(
         fetch_kernel,
@@ -147,9 +164,12 @@
         ),
         in_specs=[VMEM, HBM],
         out_specs=(VMEM,) * 3,
-        scratch_shapes=[pltpu.SemaphoreType.DMA((PIECES,))],
+        scratch_shapes=[
+            pltpu.VMEM((TILE * size, LANES), jnp.float32),
+            pltpu.SemaphoreType.DMA((PIECES,)),
+        ],
         cost_estimate=pl.CostEstimate(flops=0, bytes_accessed=2 * moved, transcendentals=0),
-        compiler_params=vmem((8 << 20) + 2 * moved + 8 * half * row),
+        compiler_params=vmem((8 << 20) + 2 * moved + 8 * mine.size),
     )(mine, pltpu.with_memory_space_constraint(w_gate, pltpu.HBM))
 
 
@@ -174,24 +194,35 @@
     )
 
 
-def store_groups(ref, first, total):
+def store_groups(ref, block, total):
     rows, columns = total.shape
     groups = columns // LANES
-    for c in range(groups):
-        ref[pl.ds(first + c, rows, stride=groups)] = total[:, c * LANES : (c + 1) * LANES]
+    chips = lax.axis_size("expert") * lax.axis_size("dp") // CORES
+    half = ref.shape[0] // groups // CORES
+    tok_dev = half // chips
+    for tile in range(rows // TILE):
+        row = block * rows + tile * TILE
+        token = row % half // chips
+        device = row // half * chips + row % chips
+        first = (device * tok_dev + token) * groups
+        part = total[tile * TILE : (tile + 1) * TILE]
+        for c in range(groups):
+            ref[pl.ds(first + c, TILE, stride=tok_dev * groups)] = part[
+                :, c * LANES : (c + 1) * LANES
+            ]
 
 
 def rows_kernel(
     other_ref, my_x_ref, my_dy_ref, gate_ref, up_hbm, down_hbm,
     sent_ref, up_ref, x_ref, dy_ref, gate_delta_ref, up_delta_ref, hidden_ref,
-    down_ref, total_ref, sems,
+    down_ref, wide_ref, total_ref, sems,
 ):
     down_copies = copy_pieces(down_hbm, down_ref, sems.at[0])
     up_copies = copy_pieces(up_hbm, up_ref, sems.at[1])
     half = my_x_ref.shape[0]
     x_ref[:half] = my_x_ref[...]
     dy_ref[:half] = my_dy_ref[...]
-    lay_out(other_ref, x_ref, dy_ref, half)
+    lay_out(other_ref, x_ref, dy_ref, wide_ref, half)
     depth = up_ref.shape[0] // PIECES
 
     def step(block, first):
@@ -220,18 +251,16 @@
         gate_delta_ref[rows] = gate_delta
         up_delta_ref[rows] = up_delta
         total = half_total(gate_delta, up_delta, gate_ref, up_ref, 1 - my_core())
-        store_groups(total_ref, 0, total)
-        size = total_ref.shape[0]
-        part = pl.ds(pl.multiple_of(block * size, size), size)
-        sent_ref[part] = total_ref[...].astype(jnp.bfloat16)
+        store_groups(total_ref, block, total)
 
     row_blocks(x_ref.shape[0], step)
+    sent_ref[...] = total_ref[...].astype(jnp.bfloat16)
 
 
 def rows_pass(other, my_x, my_dy, gate, w_up, w_down):
-    chips, tok_dev, row = other.shape
+    chips, size, _ = other.shape
     width, hidden = gate.shape
-    rows = 2 * chips * tok_dev
+    rows = CORES * my_x.shape[0]
     groups = width // CORES // LANES
     bf16 = functools.partial(jax.ShapeDtypeStruct, dtype=jnp.bfloat16)
     moved = (3 * width * hidden + rows * (6 * width + 3 * hidden)) * 2
@@ -251,7 +280,8 @@
         out_specs=(VMEM,) * 7,
         scratch_shapes=[
             pltpu.VMEM((hidden, width), jnp.bfloat16),
-            pltpu.VMEM((ROWS * groups, LANES), jnp.float32),
+            pltpu.VMEM((TILE * size, LANES), jnp.float32),
+            pltpu.VMEM((rows * groups, LANES), jnp.float32),
             pltpu.SemaphoreType.DMA((2, PIECES)),
         ],
         cost_estimate=pl.CostEstimate(
@@ -262,17 +292,14 @@
 
 
 def finish_kernel(gate_delta_ref, up_delta_ref, gate_ref, up_ref, total_ref):
-    rows_all = gate_delta_ref.shape[0]
-    size = total_ref.shape[0] // rows_all * ROWS
-
     def step(block, first):
         rows = pl.ds(pl.multiple_of(block * ROWS, ROWS), ROWS)
         total = half_total(
             gate_delta_ref[rows], up_delta_ref[rows], gate_ref, up_ref, my_core()
         )
-        store_groups(total_ref, block * size, total)
-
-    row_blocks(rows_all, step)
+        store_groups(total_ref, block, total)
+
+    row_blocks(gate_delta_ref.shape[0], step)
 
 
 def finish(gate_delta, up_delta, gate, up):

time: 38 us -> 38.1 us (level)
  no operation moved by 1% of the time
where the time goes in v4:
time: 38.1 us; the launch traced here: 37.8 us
  blocking collectives  16.2 us (43%)
  Pallas kernels  8.67 us (23%)
  matrix products  6.15 us (16%)
  starting transfers between devices  3.81 us (10%)
  waiting for transfers between devices  2.29 us (6%)
  between operations  0.68 us (2%)
    all_to_all x1, blocking collectives, local(): lax.all_to_all(copies, BOTH, 0, 0, axis_index_groups=same_core, tiled=True)  16.2 us
    pallas_call x1, Pallas kernels, rows_pass(): pl.pallas_call(rows_kernel, out_shape=(bf16((rows * groups, LANES)), pltp...  4.04 us
    all_to_all x1, starting transfers between devices, local(): shares = lax.all_to_all(shares, BOTH, 0, 0, tiled=True)  3.24 us
    all_to_all x1, waiting for transfers between devices, local(): shares = lax.all_to_all(shares, BOTH, 0, 0, tiled=True)  2.07 us
    dot_general x1, matrix products, local(): grad_up = jnp.dot(x.T, up_delta, preferred_element_type=jnp.float32)  2.06 us
    dot_general x1, matrix products, local(): grad_gate = jnp.dot(x.T, gate_delta, preferred_element_type=jnp.float32)  2.05 us
    dot_general x1, matrix products, local(): grad_down = jnp.dot(hidden.T, dy, preferred_element_type=jnp.float32)  2.04 us
    pallas_call x1, Pallas kernels, fetch(): pl.pallas_call(fetch_kernel, out_shape=(pltpu.VMEM((width, hidden), jnp.b...  1.55 us
  transfers between devices with their start and end apart: 3, of which 2 were waited for; matrix products, arithmetic and copies ran while one was open for 16% of the time, Pallas kernels for 6%

profile of v4, /device:TPU:0, one launch (start us, length us, event | category | flops | bytes accessed | tf_op | source)
XLA Modules:
  0.0 37.8 jit_solution(11114032857322158996)
XLA Ops:
  0.6 1.0 %shard_map.102 = bf16[16,64,128]{2,1,0:T(8,128)(2,1)S(1)} custom-call(bf16[1,2,2048]{2,1,0:T(2,128)(2,1)} %tokens_hbm.1, bf16[1,2,2048]{2,1,0:T(2,128)(2,1)} %grad_hbm.1, s32[1,2,4]{2,1,0:T(2,128)} %bitcast.14, bf16[1,2,4]{2,1,0:T(2,128)(2,1)} %bitcast.15), custom_call_target="tpu_custom_call" | custom-call | tf_op jit(solution)/shard_map/pallas_call | solution.py:93
  1.6 16.2 %all_to_all.10.mine_ref = bf16[16,64,128]{2,1,0:T(8,128)(2,1)S(1)} all-to-all(bf16[16,64,128]{2,1,0:T(8,128)(2,1)S(1)} %shard_map.102), channel_id=1, replica_groups={{8,6,24,22,10,4,26,20,12,2,28,18,14,0,30,16},{9,7,25,23,11,5,27,21,13,3..., dimensions={0} | all-to-all | bytes 524288 | tf_op jit(solution)/shard_map/all_to_all | solution.py:393
  17.9 0.0 collective-permute-start
  17.9 1.6 %shard_map.103 = (bf16[2048,512]{1,0:T(8,128)(2,1)S(1)}, bf16[32,2048]{1,0:T(8,128)(2,1)S(1)}, bf16[32,2048]{1,0:T(8,128)(2,1)S(1)}) custom-call(bf16[16,64,128]{2,1,0:T(8,128)(2,1)S(1)} %all_to_all.10.mine_ref, bf16[1,2048,512]{2,1,0:T(8,128)(2,1)} %gate_hbm.1), custom_call_target="tpu_custom_call" | custom-call | bytes 4194304 | tf_op jit(solution)/shard_map/pallas_call | solution.py:158
  19.4 0.0 collective-permute-done.other_ref
  19.4 4.0 %shard_map.104 = (bf16[512,128]{1,0:T(8,128)(2,1)S(1)}, bf16[2048,512]{1,0:T(8,128)(2,1)S(1)}, bf16[64,2048]{1,0:T(8,128)(2,1)S(1)}, bf16[64,2048]{1,0:T(8,128)(...) custom-call(bf16[16,64,128]{2,1,0:T(8,128)(2,1)S(1)} %collective-permute-done.other_, ...), custom_call_target="tpu_custom_call" | custom-call | flops 536870912 | bytes 8060928 | tf_op jit(solution)/shard_map/pallas_call | solution.py:268
  23.5 0.6 %collective-permute-start.1 = (bf16[512,128]{1,0:T(8,128)(2,1)S(1)}, bf16[512,128]{1,0:T(8,128)(2,1)S(1)}, u32[]{:S(2)}, u32[]{:S(2)}) collective-permute-start(bf16[512,128]{1,0:T(8,128)(2,1)S(1)} %get-tuple-element.24), channel_id=1, source_target_pairs={{0,1},{1,0},{2,3},{3,2},{4,5},{5,4},{6,7},{7,6},{8,9},{9,8},{10,11... | collective-permute-start | bytes 393224 | tf_op jit(solution)/shard_map/ppermute | solution.py:399
  24.1 0.8 %shard_map.105.total_ref = f32[512,128]{1,0:T(8,128)S(1)} custom-call(bf16[64,512]{1,0:T(8,128)(2,1)S(1)} %get-tuple-element.28.gate_delta_ref, bf16[64,512]{1,0:T(8,128)(2,1)S(1)} %get-tuple-element.29.up_delta_ref, bf16[2048,512]{1,0:T(8,128)(2,1)S(1)} %get-tuple-element.20.gate_ref, bf16[2048,512]{1,0:T(8,128)(2,1)S(1)} %get-tuple-element.23.up_ref), custom_call_target="tpu_custom_call" | custom-call | flops 134217728 | bytes 2490368 | tf_op jit(solution)/shard_map/pallas_call | solution.py:309
  24.8 0.2 collective-permute-done.1.got_ref
  25.0 0.7 %shard_map.106 = bf16[32,16,128]{2,1,0:T(8,128)(2,1)} custom-call(f32[512,128]{1,0:T(8,128)S(1)} %shard_map.105.total_ref, bf16[512,128]{1,0:T(8,128)(2,1)S(1)} %collective-permute-done.1.got_ref), custom_call_target="tpu_custom_call" | custom-call | tf_op jit(solution)/shard_map/pallas_call | solution.py:339
  25.7 3.2 %all-to-all-start.1 = ((bf16[32,16,128]{2,1,0:T(8,128)(2,1)}), bf16[32,16,128]{2,1,0:T(8,128)(2,1)S(1)}, u32[]{:S(2)}, u32[]{:S(2)}) async-start(bf16[32,16,128]{2,1,0:T(8,128)(2,1)} %shard_map.106), calls=%async_computation.1 | async-start | bytes 262144 | tf_op jit(solution)/shard_map/all_to_all | solution.py:405
  29.0 2.1 %fusion = bf16[1,2048,512]{2,1,0:T(8,128)(2,1)} fusion(bf16[64,2048]{1,0:T(8,128)(2,1)S(1)} %get-tuple-element.27, bf16[64,512]{1,0:T(8,128)(2,1)S(1)} %get-tuple-element.28.gate_delta_ref), kind=kOutput, calls=%fused_computation.3 | convolution fusion | flops 135266304 | bytes 2424832 | tf_op jit(solution)/shard_map/dot_general | solution.py:408
  31.0 2.1 %fusion.1 = bf16[1,2048,512]{2,1,0:T(8,128)(2,1)} fusion(bf16[64,2048]{1,0:T(8,128)(2,1)S(1)} %get-tuple-element.27, bf16[64,512]{1,0:T(8,128)(2,1)S(1)} %get-tuple-element.29.up_delta_ref), kind=kOutput, calls=%fused_computation.4 | convolution fusion | flops 135266304 | bytes 2424832 | tf_op jit(solution)/shard_map/dot_general | solution.py:409
  33.1 2.0 %fusion.2 = bf16[1,512,2048]{2,1,0:T(8,128)(2,1)} fusion(bf16[64,512]{1,0:T(8,128)(2,1)S(1)} %get-tuple-element.30, bf16[64,2048]{1,0:T(8,128)(2,1)S(1)} %get-tuple-element.31), kind=kOutput, calls=%fused_computation.5 | convolution fusion | flops 135266304 | bytes 2424832 | tf_op jit(solution)/shard_map/dot_general | solution.py:407
  35.1 2.1 %all-to-all-done.1.shares_ref = bf16[32,16,128]{2,1,0:T(8,128)(2,1)S(1)} async-done(((bf16[32,16,128]{2,1,0:T(8,128)(2,1)}), bf16[32,16,128]{2,1,0:T(8,128)(2,1)S(1)}, u32[]{:S(2)}, u32[]{:S(2)}) %all-to-all-start.1) | async-done | bytes 131104 | tf_op jit(solution)/shard_map/all_to_all | solution.py:405
  37.2 0.6 %shard_map.107 = bf16[1,2,2048]{2,1,0:T(2,128)(2,1)} custom-call(bf16[32,16,128]{2,1,0:T(8,128)(2,1)S(1)} %all-to-all-done.1.shares_ref), custom_call_target="tpu_custom_call" | custom-call | tf_op jit(solution)/shard_map/pallas_call | solution.py:372
Async XLA Ops:
  17.9 1.6 %collective-permute-start = (bf16[16,64,128]{2,1,0:T(8,128)(2,1)S(1)}, bf16[16,64,128]{2,1,0:T(8,128)(2,1)S(1)}, u32[]{:S(2)}, u32[]{:S(2)}) collective-permute-start(bf16[16,64,128]{2,1,0:T(8,128)(2,1)S(1)} %all_to_all.10.mine_ref), channel_id=1, source_target_pairs={{0,1},{1,0},{2,3},{3,2},{4,5},{5,4},{6,7},{7,6},{8,9},{9,8},{10,11... | collective-permute-start | bytes 786440 | tf_op jit(solution)/shard_map/ppermute | solution.py:394
  23.5 1.6 %collective-permute-start.1 = (bf16[512,128]{1,0:T(8,128)(2,1)S(1)}, bf16[512,128]{1,0:T(8,128)(2,1)S(1)}, u32[]{:S(2)}, u32[]{:S(2)}) collective-permute-start(bf16[512,128]{1,0:T(8,128)(2,1)S(1)} %get-tuple-element.24), channel_id=1, source_target_pairs={{0,1},{1,0},{2,3},{3,2},{4,5},{5,4},{6,7},{7,6},{8,9},{9,8},{10,11... | collective-permute-start | bytes 393224 | tf_op jit(solution)/shard_map/ppermute | solution.py:399
  25.7 11.5 %all-to-all-start.1 = ((bf16[32,16,128]{2,1,0:T(8,128)(2,1)}), bf16[32,16,128]{2,1,0:T(8,128)(2,1)S(1)}, u32[]{:S(2)}, u32[]{:S(2)}) async-start(bf16[32,16,128]{2,1,0:T(8,128)(2,1)} %shard_map.106), calls=%async_computation.1 | async-start | bytes 262144 | tf_op jit(solution)/shard_map/all_to_all | solution.py:405

commit v5 on v3

--- a/solution.py
+++ b/solution.py
@@ -191,7 +191,8 @@
     half = my_x_ref.shape[0]
     x_ref[:half] = my_x_ref[...]
     dy_ref[:half] = my_dy_ref[...]
-    lay_out(other_ref, x_ref, dy_ref, half)
+    x_ref[half:] = other_ref[:, : x_ref.shape[1]]
+    dy_ref[half:] = other_ref[:, x_ref.shape[1] :]
     depth = up_ref.shape[0] // PIECES
 
     def step(block, first):
@@ -229,9 +230,8 @@
 
 
 def rows_pass(other, my_x, my_dy, gate, w_up, w_down):
-    chips, tok_dev, row = other.shape
     width, hidden = gate.shape
-    rows = 2 * chips * tok_dev
+    rows = CORES * other.shape[0]
     groups = width // CORES // LANES
     bf16 = functools.partial(jax.ShapeDtypeStruct, dtype=jnp.bfloat16)
     moved = (3 * width * hidden + rows * (6 * width + 3 * hidden)) * 2
@@ -367,7 +367,7 @@
     other = lax.ppermute(mine, BOTH, core_pairs)
     gate, my_x, my_dy = fetch(mine, w_gate)
     sent, up, x, dy, gate_delta, up_delta, hidden = rows_pass(
-        other, my_x, my_dy, gate, w_up, w_down
+        other.reshape(my_x.shape[0], -1), my_x, my_dy, gate, w_up, w_down
     )
     got = lax.ppermute(sent, BOTH, core_pairs)
     total = finish(gate_delta, up_delta, gate, up)

time: 38 us -> 38 us (level)
  no operation moved by 1% of the time
where the time goes in v5:
time: 38 us; the launch traced here: 37.7 us
  blocking collectives  16.2 us (43%)
  Pallas kernels  8.41 us (22%)
  matrix products  6.15 us (16%)
  starting transfers between devices  3.81 us (10%)
  waiting for transfers between devices  2.31 us (6%)
  between operations  0.68 us (2%)
    all_to_all x1, blocking collectives, local(): lax.all_to_all(copies, BOTH, 0, 0, axis_index_groups=same_core, tiled=True)  16.2 us
    pallas_call x1, Pallas kernels, rows_pass(): pl.pallas_call(rows_kernel, out_shape=(bf16((rows * groups, LANES)), pltp...  3.81 us
    all_to_all x1, starting transfers between devices, local(): shares = lax.all_to_all(shares, BOTH, 0, 0, tiled=True)  3.24 us
    all_to_all x1, waiting for transfers between devices, local(): shares = lax.all_to_all(shares, BOTH, 0, 0, tiled=True)  2.08 us
    dot_general x1, matrix products, local(): grad_up = jnp.dot(x.T, up_delta, preferred_element_type=jnp.float32)  2.06 us
    dot_general x1, matrix products, local(): grad_gate = jnp.dot(x.T, gate_delta, preferred_element_type=jnp.float32)  2.05 us
    dot_general x1, matrix products, local(): grad_down = jnp.dot(hidden.T, dy, preferred_element_type=jnp.float32)  2.04 us
    pallas_call x1, Pallas kernels, fetch(): pl.pallas_call(fetch_kernel, out_shape=(pltpu.VMEM((width, hidden), jnp.b...  1.55 us
  transfers between devices with their start and end apart: 3, of which 2 were waited for; matrix products, arithmetic and copies ran while one was open for 16% of the time, Pallas kernels for 6%

profile of v5, /device:TPU:0, one launch (start us, length us, event | category | flops | bytes accessed | tf_op | source)
XLA Modules:
  0.0 37.7 jit_solution(170021009924780828)
XLA Ops:
  0.6 1.0 %shard_map.102 = bf16[16,2,4096]{2,1,0:T(2,128)(2,1)S(1)} custom-call(bf16[1,2,2048]{2,1,0:T(2,128)(2,1)} %tokens_hbm.1, bf16[1,2,2048]{2,1,0:T(2,128)(2,1)} %grad_hbm.1, s32[1,2,4]{2,1,0:T(2,128)} %bitcast.14, bf16[1,2,4]{2,1,0:T(2,128)(2,1)} %bitcast.15), custom_call_target="tpu_custom_call" | custom-call | tf_op jit(solution)/shard_map/pallas_call | solution.py:87
  1.6 16.2 %all_to_all.10.mine_ref = bf16[16,2,4096]{2,1,0:T(2,128)(2,1)S(1)} all-to-all(bf16[16,2,4096]{2,1,0:T(2,128)(2,1)S(1)} %shard_map.102), channel_id=1, replica_groups={{8,6,24,22,10,4,26,20,12,2,28,18,14,0,30,16},{9,7,25,23,11,5,27,21,13,3..., dimensions={0} | all-to-all | bytes 524288 | tf_op jit(solution)/shard_map/all_to_all | solution.py:366
  17.8 0.0 collective-permute-start
  17.8 1.6 %shard_map.103 = (bf16[2048,512]{1,0:T(8,128)(2,1)S(1)}, bf16[32,2048]{1,0:T(8,128)(2,1)S(1)}, bf16[32,2048]{1,0:T(8,128)(2,1)S(1)}) custom-call(bf16[16,2,4096]{2,1,0:T(2,128)(2,1)S(1)} %all_to_all.10.mine_ref, bf16[1,2048,512]{2,1,0:T(8,128)(2,1)} %gate_hbm.1), custom_call_target="tpu_custom_call" | custom-call | bytes 4194304 | tf_op jit(solution)/shard_map/pallas_call | solution.py:141
  19.4 0.0 collective-permute-done
  19.4 0.1 reshape.11.other_ref
  19.5 3.8 %shard_map.104 = (bf16[512,128]{1,0:T(8,128)(2,1)S(1)}, bf16[2048,512]{1,0:T(8,128)(2,1)S(1)}, bf16[64,2048]{1,0:T(8,128)(2,1)S(1)}, bf16[64,2048]{1,0:T(8,128)(...) custom-call(bf16[32,4096]{1,0:T(8,128)(2,1)S(1)} %reshape.11.other_ref, ...), custom_call_target="tpu_custom_call" | custom-call | flops 536870912 | bytes 8060928 | tf_op jit(solution)/shard_map/pallas_call | solution.py:239
  23.3 0.6 %collective-permute-start.1 = (bf16[512,128]{1,0:T(8,128)(2,1)S(1)}, bf16[512,128]{1,0:T(8,128)(2,1)S(1)}, u32[]{:S(2)}, u32[]{:S(2)}) collective-permute-start(bf16[512,128]{1,0:T(8,128)(2,1)S(1)} %get-tuple-element.24), channel_id=1, source_target_pairs={{0,1},{1,0},{2,3},{3,2},{4,5},{5,4},{6,7},{7,6},{8,9},{9,8},{10,11... | collective-permute-start | bytes 393224 | tf_op jit(solution)/shard_map/ppermute | solution.py:372
  23.9 0.8 %shard_map.105.total_ref = f32[512,128]{1,0:T(8,128)S(1)} custom-call(bf16[64,512]{1,0:T(8,128)(2,1)S(1)} %get-tuple-element.28.gate_delta_ref, bf16[64,512]{1,0:T(8,128)(2,1)S(1)} %get-tuple-element.29.up_delta_ref, bf16[2048,512]{1,0:T(8,128)(2,1)S(1)} %get-tuple-element.20.gate_ref, bf16[2048,512]{1,0:T(8,128)(2,1)S(1)} %get-tuple-element.23.up_ref), custom_call_target="tpu_custom_call" | custom-call | flops 134217728 | bytes 2490368 | tf_op jit(solution)/shard_map/pallas_call | solution.py:282
  24.7 0.2 collective-permute-done.1.got_ref
  24.9 0.7 %shard_map.106 = bf16[32,16,128]{2,1,0:T(8,128)(2,1)} custom-call(f32[512,128]{1,0:T(8,128)S(1)} %shard_map.105.total_ref, bf16[512,128]{1,0:T(8,128)(2,1)S(1)} %collective-permute-done.1.got_ref), custom_call_target="tpu_custom_call" | custom-call | tf_op jit(solution)/shard_map/pallas_call | solution.py:312
  25.6 3.2 %all-to-all-start.1 = ((bf16[32,16,128]{2,1,0:T(8,128)(2,1)}), bf16[32,16,128]{2,1,0:T(8,128)(2,1)S(1)}, u32[]{:S(2)}, u32[]{:S(2)}) async-start(bf16[32,16,128]{2,1,0:T(8,128)(2,1)} %shard_map.106), calls=%async_computation.1 | async-start | bytes 262144 | tf_op jit(solution)/shard_map/all_to_all | solution.py:378
  28.8 2.1 %fusion = bf16[1,2048,512]{2,1,0:T(8,128)(2,1)} fusion(bf16[64,2048]{1,0:T(8,128)(2,1)S(1)} %get-tuple-element.27, bf16[64,512]{1,0:T(8,128)(2,1)S(1)} %get-tuple-element.28.gate_delta_ref), kind=kOutput, calls=%fused_computation.3 | convolution fusion | flops 135266304 | bytes 2424832 | tf_op jit(solution)/shard_map/dot_general | solution.py:381
  30.9 2.1 %fusion.1 = bf16[1,2048,512]{2,1,0:T(8,128)(2,1)} fusion(bf16[64,2048]{1,0:T(8,128)(2,1)S(1)} %get-tuple-element.27, bf16[64,512]{1,0:T(8,128)(2,1)S(1)} %get-tuple-element.29.up_delta_ref), kind=kOutput, calls=%fused_computation.4 | convolution fusion | flops 135266304 | bytes 2424832 | tf_op jit(solution)/shard_map/dot_general | solution.py:382
  32.9 2.0 %fusion.2 = bf16[1,512,2048]{2,1,0:T(8,128)(2,1)} fusion(bf16[64,512]{1,0:T(8,128)(2,1)S(1)} %get-tuple-element.30, bf16[64,2048]{1,0:T(8,128)(2,1)S(1)} %get-tuple-element.31), kind=kOutput, calls=%fused_computation.5 | convolution fusion | flops 135266304 | bytes 2424832 | tf_op jit(solution)/shard_map/dot_general | solution.py:380
  35.0 2.1 %all-to-all-done.1.shares_ref = bf16[32,16,128]{2,1,0:T(8,128)(2,1)S(1)} async-done(((bf16[32,16,128]{2,1,0:T(8,128)(2,1)}), bf16[32,16,128]{2,1,0:T(8,128)(2,1)S(1)}, u32[]{:S(2)}, u32[]{:S(2)}) %all-to-all-start.1) | async-done | bytes 131104 | tf_op jit(solution)/shard_map/all_to_all | solution.py:378
  37.0 0.6 %shard_map.107 = bf16[1,2,2048]{2,1,0:T(2,128)(2,1)} custom-call(bf16[32,16,128]{2,1,0:T(8,128)(2,1)S(1)} %all-to-all-done.1.shares_ref), custom_call_target="tpu_custom_call" | custom-call | tf_op jit(solution)/shard_map/pallas_call | solution.py:345
Async XLA Ops:
  17.8 1.6 %collective-permute-start = (bf16[16,2,4096]{2,1,0:T(2,128)(2,1)S(1)}, bf16[16,2,4096]{2,1,0:T(2,128)(2,1)S(1)}, u32[]{:S(2)}, u32[]{:S(2)}) collective-permute-start(bf16[16,2,4096]{2,1,0:T(2,128)(2,1)S(1)} %all_to_all.10.mine_ref), channel_id=1, source_target_pairs={{0,1},{1,0},{2,3},{3,2},{4,5},{5,4},{6,7},{7,6},{8,9},{9,8},{10,11... | collective-permute-start | bytes 786440 | tf_op jit(solution)/shard_map/ppermute | solution.py:367
  23.3 1.6 %collective-permute-start.1 = (bf16[512,128]{1,0:T(8,128)(2,1)S(1)}, bf16[512,128]{1,0:T(8,128)(2,1)S(1)}, u32[]{:S(2)}, u32[]{:S(2)}) collective-permute-start(bf16[512,128]{1,0:T(8,128)(2,1)S(1)} %get-tuple-element.24), channel_id=1, source_target_pairs={{0,1},{1,0},{2,3},{3,2},{4,5},{5,4},{6,7},{7,6},{8,9},{9,8},{10,11... | collective-permute-start | bytes 393224 | tf_op jit(solution)/shard_map/ppermute | solution.py:372
  25.6 11.5 %all-to-all-start.1 = ((bf16[32,16,128]{2,1,0:T(8,128)(2,1)}), bf16[32,16,128]{2,1,0:T(8,128)(2,1)S(1)}, u32[]{:S(2)}, u32[]{:S(2)}) async-start(bf16[32,16,128]{2,1,0:T(8,128)(2,1)} %shard_map.106), calls=%async_computation.1 | async-start | bytes 262144 | tf_op jit(solution)/shard_map/all_to_all | solution.py:378

commit v6 on v1

--- a/solution.py
+++ b/solution.py
@@ -23,8 +23,7 @@
 
 
 def chip_at(place):
-    per_expert = lax.axis_size("dp") // CORES
-    return (place + per_expert // 2) % (per_expert * lax.axis_size("expert"))
+    return lax.axis_size("expert") * lax.axis_size("dp") // CORES - 1 - place
 
 
 def pack_kernel(
@@ -308,7 +307,7 @@
     size = total.shape[0] // devices
     return pl.pallas_call(
         share_kernel,
-        out_shape=jax.ShapeDtypeStruct((devices, size, LANES), jnp.bfloat16),
+        out_shape=pltpu.VMEM((devices, size, LANES), jnp.bfloat16),
         in_specs=[VMEM] * 2,
         out_specs=VMEM,
         compiler_params=vmem((8 << 20) + 32 * total.size),

time: 37.9 us -> 38.1 us (level)
  starting transfers between devices: 3.85 us -> 4.84 us
  blocking collectives: 16.2 us -> 15.8 us
    all_to_all x1, starting transfers between devices: 3.27 us -> 4.27 us  [local(): lax.all_to_all(shares, BOTH, 0, 0, axis_index_groups=everyone, tiled=True)]
    all_to_all x1, blocking collectives: 16.2 us -> 15.8 us  [local(): lax.all_to_all(copies, BOTH, 0, 0, axis_index_groups=same_core, tiled=True)]
where the time goes in v6:
time: 38.1 us; the launch traced here: 37.8 us
  blocking collectives  15.8 us (41%)
  Pallas kernels  8.39 us (22%)
  matrix products  6.15 us (16%)
  starting transfers between devices  4.84 us (13%)
  waiting for transfers between devices  2 us (5%)
  between operations  0.68 us (2%)
    all_to_all x1, blocking collectives, local(): lax.all_to_all(copies, BOTH, 0, 0, axis_index_groups=same_core, tiled=True)  15.8 us
    all_to_all x1, starting transfers between devices, local(): lax.all_to_all(shares, BOTH, 0, 0, axis_index_groups=everyone, tiled=True)  4.27 us
    pallas_call x1, Pallas kernels, rows_pass(): pl.pallas_call(rows_kernel, out_shape=(bf16((rows * groups, LANES)), pltp...  3.79 us
    dot_general x1, matrix products, local(): grad_gate = jnp.dot(x.T, gate_delta, preferred_element_type=jnp.float32)  2.05 us
    dot_general x1, matrix products, local(): grad_up = jnp.dot(x.T, up_delta, preferred_element_type=jnp.float32)  2.05 us
    dot_general x1, matrix products, local(): grad_down = jnp.dot(hidden.T, dy, preferred_element_type=jnp.float32)  2.05 us
    all_to_all x1, waiting for transfers between devices, local(): lax.all_to_all(shares, BOTH, 0, 0, axis_index_groups=everyone, tiled=True)  1.76 us
    pallas_call x1, Pallas kernels, fetch(): pl.pallas_call(fetch_kernel, out_shape=(pltpu.VMEM((width, hidden), jnp.b...  1.55 us
  transfers between devices with their start and end apart: 3, of which 2 were waited for; matrix products, arithmetic and copies ran while one was open for 16% of the time, Pallas kernels for 6%

profile of v6, /device:TPU:0, one launch (start us, length us, event | category | flops | bytes accessed | tf_op | source)
XLA Modules:
  0.0 37.8 jit_solution(14822560415126067761)
XLA Ops:
  0.6 1.0 %shard_map.102 = bf16[16,2,4096]{2,1,0:T(2,128)(2,1)S(1)} custom-call(bf16[1,2,2048]{2,1,0:T(2,128)(2,1)} %tokens_hbm.1, bf16[1,2,2048]{2,1,0:T(2,128)(2,1)} %grad_hbm.1, s32[1,2,4]{2,1,0:T(2,128)} %bitcast.14, bf16[1,2,4]{2,1,0:T(2,128)(2,1)} %bitcast.15), custom_call_target="tpu_custom_call" | custom-call | tf_op jit(solution)/shard_map/pallas_call | solution.py:82
  1.6 15.8 %all_to_all.10.mine_ref = bf16[16,2,4096]{2,1,0:T(2,128)(2,1)S(1)} all-to-all(bf16[16,2,4096]{2,1,0:T(2,128)(2,1)S(1)} %shard_map.102), channel_id=1, replica_groups={{30,28,26,24,22,20,18,16,14,12,10,8,6,4,2,0},{31,29,27,25,23,21,19,17,1..., dimensions={0} | all-to-all | bytes 524288 | tf_op jit(solution)/shard_map/all_to_all | solution.py:363
  17.4 0.0 collective-permute-start
  17.4 1.6 %shard_map.103 = (bf16[2048,512]{1,0:T(8,128)(2,1)S(1)}, bf16[32,2048]{1,0:T(8,128)(2,1)S(1)}, bf16[32,2048]{1,0:T(8,128)(2,1)S(1)}) custom-call(bf16[16,2,4096]{2,1,0:T(2,128)(2,1)S(1)} %all_to_all.10.mine_ref, bf16[1,2048,512]{2,1,0:T(8,128)(2,1)} %gate_hbm.1), custom_call_target="tpu_custom_call" | custom-call | bytes 4194304 | tf_op jit(solution)/shard_map/pallas_call | solution.py:136
  19.0 0.0 collective-permute-done.other_ref
  19.0 3.8 %shard_map.104 = (bf16[512,128]{1,0:T(8,128)(2,1)S(1)}, bf16[2048,512]{1,0:T(8,128)(2,1)S(1)}, bf16[64,2048]{1,0:T(8,128)(2,1)S(1)}, bf16[64,2048]{1,0:T(8,128)(...) custom-call(bf16[16,2,4096]{2,1,0:T(2,128)(2,1)S(1)} %collective-permute-done.other_, ...), custom_call_target="tpu_custom_call" | custom-call | flops 536870912 | bytes 8060928 | tf_op jit(solution)/shard_map/pallas_call | solution.py:235
  22.8 0.6 %collective-permute-start.1 = (bf16[512,128]{1,0:T(8,128)(2,1)S(1)}, bf16[512,128]{1,0:T(8,128)(2,1)S(1)}, u32[]{:S(2)}, u32[]{:S(2)}) collective-permute-start(bf16[512,128]{1,0:T(8,128)(2,1)S(1)} %get-tuple-element.24), channel_id=1, source_target_pairs={{0,1},{1,0},{2,3},{3,2},{4,5},{5,4},{6,7},{7,6},{8,9},{9,8},{10,11... | collective-permute-start | bytes 393224 | tf_op jit(solution)/shard_map/ppermute | solution.py:369
  23.3 0.8 %shard_map.105.total_ref = f32[512,128]{1,0:T(8,128)S(1)} custom-call(bf16[64,512]{1,0:T(8,128)(2,1)S(1)} %get-tuple-element.28.gate_delta_ref, bf16[64,512]{1,0:T(8,128)(2,1)S(1)} %get-tuple-element.29.up_delta_ref, bf16[2048,512]{1,0:T(8,128)(2,1)S(1)} %get-tuple-element.20.gate_ref, bf16[2048,512]{1,0:T(8,128)(2,1)S(1)} %get-tuple-element.23.up_ref), custom_call_target="tpu_custom_call" | custom-call | flops 134217728 | bytes 2490368 | tf_op jit(solution)/shard_map/pallas_call | solution.py:278
  24.1 0.2 collective-permute-done.1.got_ref
  24.3 0.7 %shard_map.106 = bf16[32,16,128]{2,1,0:T(8,128)(2,1)} custom-call(f32[512,128]{1,0:T(8,128)S(1)} %shard_map.105.total_ref, bf16[512,128]{1,0:T(8,128)(2,1)S(1)} %collective-permute-done.1.got_ref), custom_call_target="tpu_custom_call" | custom-call | tf_op jit(solution)/shard_map/pallas_call | solution.py:308
  25.0 4.3 %all-to-all-start.1 = ((bf16[32,16,128]{2,1,0:T(8,128)(2,1)}), bf16[32,16,128]{2,1,0:T(8,128)(2,1)S(1)}, u32[]{:S(2)}, u32[]{:S(2)}) async-start(bf16[32,16,128]{2,1,0:T(8,128)(2,1)} %shard_map.106), calls=%async_computation.1 | async-start | bytes 262144 | tf_op jit(solution)/shard_map/all_to_all | solution.py:375
  29.3 2.1 %fusion = bf16[1,2048,512]{2,1,0:T(8,128)(2,1)} fusion(bf16[64,2048]{1,0:T(8,128)(2,1)S(1)} %get-tuple-element.27, bf16[64,512]{1,0:T(8,128)(2,1)S(1)} %get-tuple-element.28.gate_delta_ref), kind=kOutput, calls=%fused_computation.3 | convolution fusion | flops 135266304 | bytes 2424832 | tf_op jit(solution)/shard_map/dot_general | solution.py:378
  31.3 2.0 %fusion.1 = bf16[1,2048,512]{2,1,0:T(8,128)(2,1)} fusion(bf16[64,2048]{1,0:T(8,128)(2,1)S(1)} %get-tuple-element.27, bf16[64,512]{1,0:T(8,128)(2,1)S(1)} %get-tuple-element.29.up_delta_ref), kind=kOutput, calls=%fused_computation.4 | convolution fusion | flops 135266304 | bytes 2424832 | tf_op jit(solution)/shard_map/dot_general | solution.py:379
  33.4 2.0 %fusion.2 = bf16[1,512,2048]{2,1,0:T(8,128)(2,1)} fusion(bf16[64,512]{1,0:T(8,128)(2,1)S(1)} %get-tuple-element.30, bf16[64,2048]{1,0:T(8,128)(2,1)S(1)} %get-tuple-element.31), kind=kOutput, calls=%fused_computation.5 | convolution fusion | flops 135266304 | bytes 2424832 | tf_op jit(solution)/shard_map/dot_general | solution.py:377
  35.4 1.8 %all-to-all-done.1.shares_ref = bf16[32,16,128]{2,1,0:T(8,128)(2,1)S(1)} async-done(((bf16[32,16,128]{2,1,0:T(8,128)(2,1)}), bf16[32,16,128]{2,1,0:T(8,128)(2,1)S(1)}, u32[]{:S(2)}, u32[]{:S(2)}) %all-to-all-start.1) | async-done | bytes 131104 | tf_op jit(solution)/shard_map/all_to_all | solution.py:375
  37.2 0.6 %shard_map.107 = bf16[1,2,2048]{2,1,0:T(2,128)(2,1)} custom-call(bf16[32,16,128]{2,1,0:T(8,128)(2,1)S(1)} %all-to-all-done.1.shares_ref), custom_call_target="tpu_custom_call" | custom-call | tf_op jit(solution)/shard_map/pallas_call | solution.py:341
Async XLA Ops:
  17.4 1.6 %collective-permute-start = (bf16[16,2,4096]{2,1,0:T(2,128)(2,1)S(1)}, bf16[16,2,4096]{2,1,0:T(2,128)(2,1)S(1)}, u32[]{:S(2)}, u32[]{:S(2)}) collective-permute-start(bf16[16,2,4096]{2,1,0:T(2,128)(2,1)S(1)} %all_to_all.10.mine_ref), channel_id=1, source_target_pairs={{0,1},{1,0},{2,3},{3,2},{4,5},{5,4},{6,7},{7,6},{8,9},{9,8},{10,11... | collective-permute-start | bytes 786440 | tf_op jit(solution)/shard_map/ppermute | solution.py:364
  22.8 1.6 %collective-permute-start.1 = (bf16[512,128]{1,0:T(8,128)(2,1)S(1)}, bf16[512,128]{1,0:T(8,128)(2,1)S(1)}, u32[]{:S(2)}, u32[]{:S(2)}) collective-permute-start(bf16[512,128]{1,0:T(8,128)(2,1)S(1)} %get-tuple-element.24), channel_id=1, source_target_pairs={{0,1},{1,0},{2,3},{3,2},{4,5},{5,4},{6,7},{7,6},{8,9},{9,8},{10,11... | collective-permute-start | bytes 393224 | tf_op jit(solution)/shard_map/ppermute | solution.py:369
  25.0 12.2 %all-to-all-start.1 = ((bf16[32,16,128]{2,1,0:T(8,128)(2,1)}), bf16[32,16,128]{2,1,0:T(8,128)(2,1)S(1)}, u32[]{:S(2)}, u32[]{:S(2)}) async-start(bf16[32,16,128]{2,1,0:T(8,128)(2,1)} %shard_map.106), calls=%async_computation.1 | async-start | bytes 262144 | tf_op jit(solution)/shard_map/all_to_all | solution.py:375

commit v7 on v5

--- a/solution.py
+++ b/solution.py
@@ -22,13 +22,26 @@
     return pltpu.CompilerParams(vmem_limit_bytes=min(size, 36 << 20))
 
 
-def chip_at(place):
-    experts = lax.axis_size("expert")
-    per_expert = lax.axis_size("dp") // CORES
-    upper = 1 - place % 2
-    rank = place // 2 // experts
-    within = per_expert // 2 + upper * rank - (1 - upper) * (1 + rank)
-    return place // 2 % experts * per_expert + within
+def sizes():
+    dp = lax.axis_size("dp")
+    along_y = 1
+    while (2 * along_y) ** 2 <= dp // CORES:
+        along_y *= 2
+    return lax.axis_size("expert"), dp // CORES // along_y, along_y, CORES
+
+
+def device_at(expert, z, y, core):
+    _, along_z, along_y, _ = sizes()
+    return ((expert * along_z + z) * along_y + y) * CORES + core
+
+
+def place_at(place):
+    experts, along_z, _, _ = sizes()
+    return place % experts, (place // experts + along_z // 2) % along_z
+
+
+def my_y():
+    return lax.axis_index("dp") // CORES % sizes()[2]
 
 
 def pack_kernel(
@@ -48,7 +61,7 @@
         copy.start()
     for copy in copies:
         copy.wait()
-    chips, tok_dev, _ = out_ref.shape
+    places, tok_dev, _ = out_ref.shape
     width = tokens_ref.shape[2]
     experts = lax.axis_size("expert")
     first = lax.axis_index("expert") * tok_dev
@@ -70,13 +83,13 @@
 
     def write(place, carry):
         out_ref[place, :, :width] = tokens_ref[0]
-        out_ref[place, :, width:] = weighted_ref[chip_at(place) // (chips // experts)]
+        out_ref[place, :, width:] = weighted_ref[place_at(place)[0]]
         return carry
 
-    lax.fori_loop(0, chips, write, 0, unroll=chips <= 16)
-
-
-def pack(tokens, out_grad, expert_ids, gate_scores, chips):
+    lax.fori_loop(0, places, write, 0, unroll=places <= 16)
+
+
+def pack(tokens, out_grad, expert_ids, gate_scores, places):
     _, tok_dev, width = tokens.shape
     operands = [
         pltpu.with_memory_space_constraint(a, pltpu.HBM)
@@ -86,7 +99,7 @@
     ]
     return pl.pallas_call(
         pack_kernel,
-        out_shape=jax.ShapeDtypeStruct((chips, tok_dev, 2 * width), jnp.bfloat16),
+        out_shape=jax.ShapeDtypeStruct((places, tok_dev, 2 * width), jnp.bfloat16),
         in_specs=[HBM] * 4,
         out_specs=VMEM,
         scratch_shapes=[pltpu.VMEM(a.shape, a.dtype) for a in operands]
@@ -101,13 +114,10 @@
 def copy_pieces(src, dst, sems):
     rows = dst.shape[0] // PIECES
     parts = [pl.ds(piece * rows, rows) for piece in range(PIECES)]
-    copies = [
+    return [
         pltpu.make_async_copy(src.at[0, part], dst.at[part], sems.at[piece])
         for piece, part in enumerate(parts)
     ]
-    for copy in copies:
-        copy.start()
-    return copies
 
 
 def lay_out(src_ref, x_ref, dy_ref, first):
@@ -126,31 +136,55 @@
     lax.fori_loop(0, tiles, step, 0, unroll=tiles <= 2)
 
 
-def fetch_kernel(mine_ref, gate_hbm, gate_ref, x_ref, dy_ref, sems):
-    copies = copy_pieces(gate_hbm, gate_ref, sems)
+def fetch_kernel(
+    mine_ref, gate_hbm, up_hbm, down_hbm, gate_ref, up_ref, down_ref, x_ref, dy_ref, sems
+):
+    copies = copy_pieces(gate_hbm, gate_ref, sems.at[0])
+    copies += copy_pieces(up_hbm, up_ref, sems.at[1])
+    copies += copy_pieces(down_hbm, down_ref, sems.at[2])
+    for copy in copies:
+        copy.start()
     lay_out(mine_ref, x_ref, dy_ref, 0)
     for copy in copies:
         copy.wait()
 
 
-def fetch(mine, w_gate):
-    chips, tok_dev, row = mine.shape
-    _, width, hidden = w_gate.shape
-    half = chips * tok_dev
-    moved = 2 * width * hidden
+def fetch(mine, *weights):
+    places, tok_dev, row = mine.shape
+    rows = (places * tok_dev, row // 2)
+    moved = sum(2 * w.size for w in weights)
+    weights = [pltpu.with_memory_space_constraint(w, pltpu.HBM) for w in weights]
     return pl.pallas_call(
         fetch_kernel,
-        out_shape=(
-            pltpu.VMEM((width, hidden), jnp.bfloat16),
-            pltpu.VMEM((half, width), jnp.bfloat16),
-            pltpu.VMEM((half, width), jnp.bfloat16),
-        ),
-        in_specs=[VMEM, HBM],
-        out_specs=(VMEM,) * 3,
-        scratch_shapes=[pltpu.SemaphoreType.DMA((PIECES,))],
+        out_shape=tuple(pltpu.VMEM(w.shape[1:], w.dtype) for w in weights)
+        + (pltpu.VMEM(rows, jnp.bfloat16), pltpu.VMEM(rows, jnp.bfloat16)),
+        in_specs=[VMEM] + [HBM] * 3,
+        out_specs=(VMEM,) * 5,
+        scratch_shapes=[pltpu.SemaphoreType.DMA((3, PIECES))],
         cost_estimate=pl.CostEstimate(flops=0, bytes_accessed=2 * moved, transcendentals=0),
-        compiler_params=vmem((8 << 20) + 2 * moved + 8 * half * row),
-    )(mine, pltpu.with_memory_space_constraint(w_gate, pltpu.HBM))
+        compiler_params=vmem((4 << 20) + 2 * moved + 8 * mine.size),
+    )(mine, *weights)
+
+
+def lay_kernel(*refs):
+    *src_refs, x_ref, dy_ref = refs
+    for i, src_ref in enumerate(src_refs):
+        lay_out(src_ref, x_ref, dy_ref, i * (x_ref.shape[0] // len(src_refs)))
+
+
+def lay(*blocks):
+    places, tok_dev, row = blocks[0].shape
+    rows = (len(blocks) * places * tok_dev, row // 2)
+    return pl.pallas_call(
+        lay_kernel,
+        out_shape=(pltpu.VMEM(rows, jnp.bfloat16), pltpu.VMEM(rows, jnp.bfloat16)),
+        in_specs=[VMEM] * len(blocks),
+        out_specs=(VMEM,) * 2,
+        cost_estimate=pl.CostEstimate(
+            flops=0, bytes_accessed=8 * len(blocks) * blocks[0].size, transcendentals=0
+        ),
+        compiler_params=vmem((8 << 20) + 8 * len(blocks) * blocks[0].size),
+    )(*blocks)
 
 
 def my_core():
@@ -181,41 +215,33 @@
         ref[pl.ds(first + c, rows, stride=groups)] = total[:, c * LANES : (c + 1) * LANES]
 
 
-def rows_kernel(
-    other_ref, my_x_ref, my_dy_ref, gate_ref, up_hbm, down_hbm,
-    sent_ref, up_ref, x_ref, dy_ref, gate_delta_ref, up_delta_ref, hidden_ref,
-    down_ref, total_ref, sems,
-):
-    down_copies = copy_pieces(down_hbm, down_ref, sems.at[0])
-    up_copies = copy_pieces(up_hbm, up_ref, sems.at[1])
-    half = my_x_ref.shape[0]
-    x_ref[:half] = my_x_ref[...]
-    dy_ref[:half] = my_dy_ref[...]
-    x_ref[half:] = other_ref[:, : x_ref.shape[1]]
-    dy_ref[half:] = other_ref[:, x_ref.shape[1] :]
-    depth = up_ref.shape[0] // PIECES
+def rows_kernel(*refs):
+    along_y = sizes()[2]
+    other_refs, refs = refs[: along_y - 1], refs[along_y - 1 :]
+    my_x_ref, my_dy_ref, laid_x_ref, laid_dy_ref, gate_ref, up_ref, down_ref, *refs = refs
+    sent_ref, x_ref, dy_ref, gate_delta_ref, up_delta_ref, hidden_ref, total_ref = refs
+    size = my_x_ref.shape[0]
+    x_ref[:size] = my_x_ref[...]
+    dy_ref[:size] = my_dy_ref[...]
+    for i in range(along_y):
+        there = pl.ds(size if i == 0 else 2 * i * size, size)
+        x_ref[there] = laid_x_ref[i * size : (i + 1) * size]
+        dy_ref[there] = laid_dy_ref[i * size : (i + 1) * size]
+    for i, other_ref in enumerate(other_refs):
+        lay_out(other_ref, x_ref, dy_ref, (2 * i + 3) * size)
 
     def step(block, first):
         rows = pl.ds(pl.multiple_of(block * ROWS, ROWS), ROWS)
         x = x_ref[rows]
         pre_gate = jnp.dot(x, gate_ref[...], preferred_element_type=jnp.float32)
+        pre_up = jnp.dot(x, up_ref[...], preferred_element_type=jnp.float32)
         sigmoid_gate = jax.nn.sigmoid(pre_gate)
         activated = pre_gate * sigmoid_gate
         slope = sigmoid_gate * (1.0 + pre_gate * (1.0 - sigmoid_gate))
-        if first:
-            for copy in down_copies:
-                copy.wait()
+        hidden_ref[rows] = (activated * pre_up).astype(jnp.bfloat16)
         grad_hidden = lax.dot_general(
             dy_ref[rows], down_ref[...], CONTRACT_LAST, preferred_element_type=jnp.float32
         )
-        pre_up = None
-        for piece, copy in enumerate(up_copies):
-            if first:
-                copy.wait()
-            part = slice(piece * depth, (piece + 1) * depth)
-            product = jnp.dot(x[:, part], up_ref[part], preferred_element_type=jnp.float32)
-            pre_up = product if pre_up is None else pre_up + product
-        hidden_ref[rows] = (activated * pre_up).astype(jnp.bfloat16)
         gate_delta = (grad_hidden * pre_up * slope).astype(jnp.bfloat16)
         up_delta = (grad_hidden * activated).astype(jnp.bfloat16)
         gate_delta_ref[rows] = gate_delta
@@ -229,36 +255,30 @@
     row_blocks(x_ref.shape[0], step)
 
 
-def rows_pass(other, my_x, my_dy, gate, w_up, w_down):
+def rows_pass(others, my_x, my_dy, laid_x, laid_dy, gate, up, down):
     width, hidden = gate.shape
-    rows = CORES * other.shape[0]
+    rows = CORES * laid_x.shape[0]
     groups = width // CORES // LANES
     bf16 = functools.partial(jax.ShapeDtypeStruct, dtype=jnp.bfloat16)
-    moved = (3 * width * hidden + rows * (6 * width + 3 * hidden)) * 2
-    up, down = (pltpu.with_memory_space_constraint(w, pltpu.HBM) for w in (w_up, w_down))
+    moved = rows * (6 * width + 3 * hidden) * 2
     return pl.pallas_call(
         rows_kernel,
         out_shape=(
             bf16((rows * groups, LANES)),
-            pltpu.VMEM((width, hidden), jnp.bfloat16),
             bf16((rows, width)),
             bf16((rows, width)),
             bf16((rows, hidden)),
             bf16((rows, hidden)),
             bf16((rows, hidden)),
         ),
-        in_specs=[VMEM] * 4 + [HBM] * 2,
-        out_specs=(VMEM,) * 7,
-        scratch_shapes=[
-            pltpu.VMEM((hidden, width), jnp.bfloat16),
-            pltpu.VMEM((ROWS * groups, LANES), jnp.float32),
-            pltpu.SemaphoreType.DMA((2, PIECES)),
-        ],
+        in_specs=[VMEM] * (len(others) + 7),
+        out_specs=(VMEM,) * 6,
+        scratch_shapes=[pltpu.VMEM((ROWS * groups, LANES), jnp.float32)],
         cost_estimate=pl.CostEstimate(
             flops=8 * rows * width * hidden, bytes_accessed=moved, transcendentals=rows * hidden
         ),
         compiler_params=vmem((12 << 20) + 2 * moved),
-    )(other, my_x, my_dy, gate, up, down)
+    )(*others, my_x, my_dy, laid_x, laid_dy, gate, up, down)
 
 
 def finish_kernel(gate_delta_ref, up_delta_ref, gate_ref, up_ref, total_ref):
@@ -293,15 +313,19 @@
 
 def share_kernel(total_ref, got_ref, shares_ref):
     devices, size, _ = shares_ref.shape
-    chips = devices // CORES
-    core = my_core()
-
-    def step(place, carry):
-        here = pl.ds(pl.multiple_of(place * size, size), size)
-        there = pl.ds(pl.multiple_of((place + chips) % devices * size, size), size)
-        owner = jnp.where(place < chips, core, 1 - core)
+    experts, along_z, along_y, _ = sizes()
+    places = experts * along_z
+    y, core = my_y(), my_core()
+
+    def step(row, carry):
+        shift, half, place = row // (CORES * places), row // places % CORES, row % places
+        got_row = row + (1 - 2 * half) * places
+        here = pl.ds(pl.multiple_of(row * size, size), size)
+        there = pl.ds(pl.multiple_of(got_row * size, size), size)
+        expert, z = place_at(place)
+        owner = device_at(expert, z, (y + shift) % along_y, (core + half) % CORES)
         total = total_ref[here] + got_ref[there].astype(jnp.float32)
-        shares_ref[chip_at(place % chips) * CORES + owner] = total.astype(jnp.bfloat16)
+        shares_ref[owner] = total.astype(jnp.bfloat16)
         return carry
 
     lax.fori_loop(0, devices, step, 0, unroll=devices <= 32)
@@ -357,17 +381,35 @@
 
 
 def local(tokens, out_grad, expert_ids, gate_scores, w_gate, w_up, w_down):
-    devices = lax.axis_size("expert") * lax.axis_size("dp")
-    chips = devices // CORES
-    order = [chip_at(place) for place in range(chips)]
-    same_core = [[chip * CORES + core for chip in order] for core in range(CORES)]
+    experts, along_z, along_y, _ = sizes()
+    places = experts * along_z
+    devices = places * along_y * CORES
+    groups = [
+        [device_at(expert, z, y, core) for expert, z in map(place_at, range(places))]
+        for y in range(along_y)
+        for core in range(CORES)
+    ]
     core_pairs = [(d, d ^ 1) for d in range(devices)]
-    copies = pack(tokens, out_grad, expert_ids, gate_scores, chips)
-    mine = lax.all_to_all(copies, BOTH, 0, 0, axis_index_groups=same_core, tiled=True)
+
+    def from_y(shift):
+        return [
+            (device_at(e, z, (y + shift) % along_y, c), device_at(e, z, y, c))
+            for e in range(experts)
+            for z in range(along_z)
+            for y in range(along_y)
+            for c in range(CORES)
+        ]
+
+    copies = pack(tokens, out_grad, expert_ids, gate_scores, places)
+    mine = lax.all_to_all(copies, BOTH, 0, 0, axis_index_groups=groups, tiled=True)
+    beside = [lax.ppermute(mine, BOTH, from_y(shift)) for shift in range(1, along_y)]
     other = lax.ppermute(mine, BOTH, core_pairs)
-    gate, my_x, my_dy = fetch(mine, w_gate)
-    sent, up, x, dy, gate_delta, up_delta, hidden = rows_pass(
-        other.reshape(my_x.shape[0], -1), my_x, my_dy, gate, w_up, w_down
+    gate, up, down, my_x, my_dy = fetch(mine, w_gate, w_up, w_down)
+    *beside, my_x = lax.optimization_barrier((*beside, my_x))
+    others = [lax.ppermute(piece, BOTH, core_pairs) for piece in beside]
+    laid_x, laid_dy = lay(other, *beside)
+    sent, x, dy, gate_delta, up_delta, hidden = rows_pass(
+        others, my_x, my_dy, laid_x, laid_dy, gate, up, down
     )
     got = lax.ppermute(sent, BOTH, core_pairs)
     total = finish(gate_delta, up_delta, gate, up)

time: 38 us -> 37.5 us (0.987)
  blocking collectives: 16.2 us -> 12.6 us
  waiting for transfers between devices: 2.31 us -> 4.21 us
  starting transfers between devices: 3.81 us -> 5.26 us
    all_to_all x1, blocking collectives: 16.2 us -> 12.6 us  [local(): lax.all_to_all(copies, BOTH, 0, 0, axis_index_groups=groups, tiled=True)]
    ppermute x0 -> x2, waiting for transfers between devices: none -> 1.69 us  [the longest x1 1.13 us: local(): others = [lax.ppermute(piece, BOTH, core_pairs) for piece in beside]]
    ppermute x0 -> x2, starting transfers between devices: none -> 1.54 us  [the longest x1 1.52 us: local(): lax.ppermute(mine, BOTH, from_y(shift))]
    pallas_call x3 -> x4, Pallas kernels: 6.33 us -> 6.21 us  [the longest x1 2.88 us: fetch(): pl.pallas_call(fetch_kernel, out_shape=tuple((pltpu.VMEM(w.shape[1:], w.d...]
  transfers between devices with their start and end apart: 3 -> 5, of which waited for: 2 -> 4; matrix products, arithmetic and copies ran while one was open for 16% -> 17% of each run, Pallas kernels for 6% -> 10%
where the time goes in v7:
time: 37.5 us; the launch traced here: 37.2 us
  blocking collectives  12.6 us (34%)
  Pallas kernels  8.29 us (22%)
  matrix products  6.16 us (16%)
  starting transfers between devices  5.26 us (14%)
  waiting for transfers between devices  4.21 us (11%)
  between operations  0.67 us (2%)
    all_to_all x1, blocking collectives, local(): lax.all_to_all(copies, BOTH, 0, 0, axis_index_groups=groups, tiled=True)  12.6 us
    all_to_all x1, starting transfers between devices, local(): shares = lax.all_to_all(shares, BOTH, 0, 0, tiled=True)  3.5 us
    pallas_call x1, Pallas kernels, fetch(): pl.pallas_call(fetch_kernel, out_shape=tuple((pltpu.VMEM(w.shape[1:], w.d...  2.88 us
    pallas_call x1, Pallas kernels, rows_pass(): pl.pallas_call(rows_kernel, out_shape=(bf16((rows * groups, LANES)), bf16...  2.18 us
    all_to_all x1, waiting for transfers between devices, local(): shares = lax.all_to_all(shares, BOTH, 0, 0, tiled=True)  2.07 us
    dot_general x1, matrix products, local(): grad_gate = jnp.dot(x.T, gate_delta, preferred_element_type=jnp.float32)  2.06 us
    dot_general x1, matrix products, local(): grad_up = jnp.dot(x.T, up_delta, preferred_element_type=jnp.float32)  2.05 us
    dot_general x1, matrix products, local(): grad_down = jnp.dot(hidden.T, dy, preferred_element_type=jnp.float32)  2.05 us
  transfers between devices with their start and end apart: 5, of which 4 were waited for; matrix products, arithmetic and copies ran while one was open for 17% of the time, Pallas kernels for 10%

profile of v7, /device:TPU:0, one launch (start us, length us, event | category | flops | bytes accessed | tf_op | source)
XLA Modules:
  0.0 37.2 jit_solution(675262470805745366)
XLA Ops:
  0.6 1.0 %shard_map.102 = bf16[8,2,4096]{2,1,0:T(2,128)(2,1)S(1)} custom-call(bf16[1,2,2048]{2,1,0:T(2,128)(2,1)} %tokens_hbm.1, bf16[1,2,2048]{2,1,0:T(2,128)(2,1)} %grad_hbm.1, s32[1,2,4]{2,1,0:T(2,128)} %bitcast.14, bf16[1,2,4]{2,1,0:T(2,128)(2,1)} %bitcast.15), custom_call_target="tpu_custom_call" | custom-call | tf_op jit(solution)/shard_map/pallas_call | solution.py:100
  1.6 12.6 %all_to_all.10.mine_ref = bf16[8,2,4096]{2,1,0:T(2,128)(2,1)S(1)} all-to-all(bf16[8,2,4096]{2,1,0:T(2,128)(2,1)S(1)} %shard_map.102), channel_id=1, replica_groups={{8,24,12,28,0,16,4,20},{9,25,13,29,1,17,5,21},{10,26,14,30,2,18,6,22},{..., dimensions={0} | all-to-all | bytes 262144 | tf_op jit(solution)/shard_map/all_to_all | solution.py:404
  14.2 1.5 %collective-permute-start = (bf16[8,2,4096]{2,1,0:T(2,128)(2,1)S(1)}, bf16[8,2,4096]{2,1,0:T(2,128)(2,1)S(1)}, u32[]{:S(2)}, u32[]{:S(2)}) collective-permute-start(bf16[8,2,4096]{2,1,0:T(2,128)(2,1)S(1)} %all_to_all.10.mine_ref), channel_id=1, source_target_pairs={{2,0},{3,1},{0,2},{1,3},{6,4},{7,5},{4,6},{5,7},{10,8},{11,9},{8,1... | collective-permute-start | bytes 393224 | tf_op jit(solution)/shard_map/ppermute | solution.py:405
  15.7 0.0 collective-permute-start.2
  15.7 2.9 %shard_map.103 = (bf16[2048,512]{1,0:T(8,128)(2,1)S(1)}, bf16[2048,512]{1,0:T(8,128)(2,1)S(1)}, bf16[512,2048]{1,0:T(8,128)(2,1)S(1)}, bf16[16,2048]{1,0:T(8,128)(2,1)S(1)}, bf16[16,2048]{1,0:T(8,128)(2,1)S(1)}) custom-call(bf16[8,2,4096]{2,1,0:T(2,128)(2,1)S(1)} %all_to_all.10.mine_ref, bf16[1,2048,512]{2,1,0:T(8,128)(2,1)} %gate_hbm.1, ...), custom_call_target="tpu_custom_call" | custom-call | bytes 12582912 | tf_op jit(solution)/shard_map/pallas_call | solution.py:157
  18.6 0.6 %collective-permute-done.refs_1_ = bf16[8,2,4096]{2,1,0:T(2,128)(2,1)S(1)} collective-permute-done((bf16[8,2,4096]{2,1,0:T(2,128)(2,1)S(1)}, bf16[8,2,4096]{2,1,0:T(2,128)(2,1)S(1)}, u32[]{:S(2)}, u32[]{:S(2)}) %collective-permute-start) | collective-permute-done | bytes 131104 | tf_op jit(solution)/shard_map/ppermute | solution.py:405
  19.2 0.0 collective-permute-start.1
  19.2 0.0 collective-permute-done.2.refs_0_
  19.2 0.2 shard_map.104
  19.4 1.1 %collective-permute-done.1.refs_0_ = bf16[8,2,4096]{2,1,0:T(2,128)(2,1)S(1)} collective-permute-done((bf16[8,2,4096]{2,1,0:T(2,128)(2,1)S(1)}, bf16[8,2,4096]{2,1,0:T(2,128)(2,1)S(1)}, u32[]{:S(2)}, u32[]{:S(2)}) %collective-permute-start.1) | collective-permute-done | bytes 131104 | tf_op jit(solution)/shard_map/ppermute | solution.py:409
  20.5 2.2 %shard_map.105 = (bf16[512,128]{1,0:T(8,128)(2,1)S(1)}, bf16[64,2048]{1,0:T(8,128)(2,1)S(1)}, bf16[64,2048]{1,0:T(8,128)(2,1)S(1)}, bf16[64,512]{1,0:T(8,128)(2,...) custom-call(bf16[8,2,4096]{2,1,0:T(2,128)(2,1)S(1)} %collective-permute-done.1.refs_0_, ...), custom_call_target="tpu_custom_call" | custom-call | flops 536870912 | bytes 1769472 | tf_op jit(solution)/shard_map/pallas_call | solution.py:264
  22.7 0.2 collective-permute-start.3
  22.9 0.8 %shard_map.106.total_ref = f32[512,128]{1,0:T(8,128)S(1)} custom-call(bf16[64,512]{1,0:T(8,128)(2,1)S(1)} %get-tuple-element.38.gate_delta_ref, bf16[64,512]{1,0:T(8,128)(2,1)S(1)} %get-tuple-element.39.up_delta_ref, bf16[2048,512]{1,0:T(8,128)(2,1)S(1)} %get-tuple-element.29.refs_5_.gate_ref, bf16[2048,512]{1,0:T(8,128)(2,1)S(1)} %get-tuple-element.30.refs_6_.up_ref), custom_call_target="tpu_custom_call" | custom-call | flops 134217728 | bytes 2490368 | tf_op jit(solution)/shard_map/pallas_call | solution.py:302
  23.7 0.4 %collective-permute-done.3.got_ref = bf16[512,128]{1,0:T(8,128)(2,1)S(1)} collective-permute-done((bf16[512,128]{1,0:T(8,128)(2,1)S(1)}, bf16[512,128]{1,0:T(8,128)(2,1)S(1)}, u32[]{:S(2)}, u32[]{:S(2)}) %collective-permute-start.3) | collective-permute-done | bytes 131104 | tf_op jit(solution)/shard_map/ppermute | solution.py:414
  24.1 0.7 %shard_map.107 = bf16[32,16,128]{2,1,0:T(8,128)(2,1)} custom-call(f32[512,128]{1,0:T(8,128)S(1)} %shard_map.106.total_ref, bf16[512,128]{1,0:T(8,128)(2,1)S(1)} %collective-permute-done.3.got_ref), custom_call_target="tpu_custom_call" | custom-call | tf_op jit(solution)/shard_map/pallas_call | solution.py:336
  24.8 3.5 %all-to-all-start.1 = ((bf16[32,16,128]{2,1,0:T(8,128)(2,1)}), bf16[32,16,128]{2,1,0:T(8,128)(2,1)S(1)}, u32[]{:S(2)}, u32[]{:S(2)}) async-start(bf16[32,16,128]{2,1,0:T(8,128)(2,1)} %shard_map.107), calls=%async_computation.1 | async-start | bytes 262144 | tf_op jit(solution)/shard_map/all_to_all | solution.py:420
  28.3 2.1 %fusion = bf16[1,2048,512]{2,1,0:T(8,128)(2,1)} fusion(bf16[64,2048]{1,0:T(8,128)(2,1)S(1)} %get-tuple-element.37, bf16[64,512]{1,0:T(8,128)(2,1)S(1)} %get-tuple-element.38.gate_delta_ref), kind=kOutput, calls=%fused_computation.3 | convolution fusion | flops 135266304 | bytes 2424832 | tf_op jit(solution)/shard_map/dot_general | solution.py:423
  30.4 2.1 %fusion.1 = bf16[1,2048,512]{2,1,0:T(8,128)(2,1)} fusion(bf16[64,2048]{1,0:T(8,128)(2,1)S(1)} %get-tuple-element.37, bf16[64,512]{1,0:T(8,128)(2,1)S(1)} %get-tuple-element.39.up_delta_ref), kind=kOutput, calls=%fused_computation.4 | convolution fusion | flops 135266304 | bytes 2424832 | tf_op jit(solution)/shard_map/dot_general | solution.py:424
  32.4 2.0 %fusion.2 = bf16[1,512,2048]{2,1,0:T(8,128)(2,1)} fusion(bf16[64,512]{1,0:T(8,128)(2,1)S(1)} %get-tuple-element.40, bf16[64,2048]{1,0:T(8,128)(2,1)S(1)} %get-tuple-element.41), kind=kOutput, calls=%fused_computation.5 | convolution fusion | flops 135266304 | bytes 2424832 | tf_op jit(solution)/shard_map/dot_general | solution.py:422
  34.5 2.1 %all-to-all-done.1.shares_ref = bf16[32,16,128]{2,1,0:T(8,128)(2,1)S(1)} async-done(((bf16[32,16,128]{2,1,0:T(8,128)(2,1)}), bf16[32,16,128]{2,1,0:T(8,128)(2,1)S(1)}, u32[]{:S(2)}, u32[]{:S(2)}) %all-to-all-start.1) | async-done | bytes 131104 | tf_op jit(solution)/shard_map/all_to_all | solution.py:420
  36.5 0.6 %shard_map.108 = bf16[1,2,2048]{2,1,0:T(2,128)(2,1)} custom-call(bf16[32,16,128]{2,1,0:T(8,128)(2,1)S(1)} %all-to-all-done.1.shares_ref), custom_call_target="tpu_custom_call" | custom-call | tf_op jit(solution)/shard_map/pallas_call | solution.py:369
Async XLA Ops:
  14.2 5.0 %collective-permute-start = (bf16[8,2,4096]{2,1,0:T(2,128)(2,1)S(1)}, bf16[8,2,4096]{2,1,0:T(2,128)(2,1)S(1)}, u32[]{:S(2)}, u32[]{:S(2)}) collective-permute-start(bf16[8,2,4096]{2,1,0:T(2,128)(2,1)S(1)} %all_to_all.10.mine_ref), channel_id=1, source_target_pairs={{2,0},{3,1},{0,2},{1,3},{6,4},{7,5},{4,6},{5,7},{10,8},{11,9},{8,1... | collective-permute-start | bytes 393224 | tf_op jit(solution)/shard_map/ppermute | solution.py:405
  15.7 3.5 %collective-permute-start.2 = (bf16[8,2,4096]{2,1,0:T(2,128)(2,1)S(1)}, bf16[8,2,4096]{2,1,0:T(2,128)(2,1)S(1)}, u32[]{:S(2)}, u32[]{:S(2)}) collective-permute-start(bf16[8,2,4096]{2,1,0:T(2,128)(2,1)S(1)} %all_to_all.10.mine_ref), channel_id=1, source_target_pairs={{0,1},{1,0},{2,3},{3,2},{4,5},{5,4},{6,7},{7,6},{8,9},{9,8},{10,11... | collective-permute-start | bytes 393224 | tf_op jit(solution)/shard_map/ppermute | solution.py:406
  19.2 1.3 %collective-permute-start.1 = (bf16[8,2,4096]{2,1,0:T(2,128)(2,1)S(1)}, bf16[8,2,4096]{2,1,0:T(2,128)(2,1)S(1)}, u32[]{:S(2)}, u32[]{:S(2)}) collective-permute-start(bf16[8,2,4096]{2,1,0:T(2,128)(2,1)S(1)} %collective-permute-done.refs_1_), channel_id=1, source_target_pairs={{0,1},{1,0},{2,3},{3,2},{4,5},{5,4},{6,7},{7,6},{8,9},{9,8},{10,11... | collective-permute-start | bytes 393224 | tf_op jit(solution)/shard_map/ppermute | solution.py:409
  22.7 1.4 %collective-permute-start.3 = (bf16[512,128]{1,0:T(8,128)(2,1)S(1)}, bf16[512,128]{1,0:T(8,128)(2,1)S(1)}, u32[]{:S(2)}, u32[]{:S(2)}) collective-permute-start(bf16[512,128]{1,0:T(8,128)(2,1)S(1)} %get-tuple-element.34), channel_id=1, source_target_pairs={{0,1},{1,0},{2,3},{3,2},{4,5},{5,4},{6,7},{7,6},{8,9},{9,8},{10,11... | collective-permute-start | bytes 393224 | tf_op jit(solution)/shard_map/ppermute | solution.py:414
  24.8 11.7 %all-to-all-start.1 = ((bf16[32,16,128]{2,1,0:T(8,128)(2,1)}), bf16[32,16,128]{2,1,0:T(8,128)(2,1)S(1)}, u32[]{:S(2)}, u32[]{:S(2)}) async-start(bf16[32,16,128]{2,1,0:T(8,128)(2,1)} %shard_map.107), calls=%async_computation.1 | async-start | bytes 262144 | tf_op jit(solution)/shard_map/all_to_all | solution.py:420

commit v8 on v7

--- a/solution.py
+++ b/solution.py
@@ -35,9 +35,30 @@
     return ((expert * along_z + z) * along_y + y) * CORES + core
 
 
+def z_at(step):
+    upper = 1 - step % 2
+    return sizes()[1] // 2 + upper * (step // 2) - (1 - upper) * (1 + step // 2)
+
+
 def place_at(place):
-    experts, along_z, _, _ = sizes()
-    return place % experts, (place // experts + along_z // 2) % along_z
+    experts = sizes()[0]
+    pair = place // 2
+    return pair % experts, z_at(place % 2 + 2 * (pair // experts))
+
+
+def order_at(place):
+    experts, _, along_y, _ = sizes()
+    place, core = place // CORES, place % CORES
+    place, turn = place // 2, place % 2
+    place, expert = place // experts, place % experts
+    return device_at(expert, z_at(turn + 2 * (place // along_y)), place % along_y, core)
+
+
+def order_of(expert, z, y, core):
+    experts, along_z, along_y, _ = sizes()
+    upper = (z >= along_z // 2) * 1
+    step = upper * (z - along_z // 2) + (1 - upper) * (along_z // 2 - 1 - z)
+    return (((step * along_y + y) * experts + expert) * 2 + 1 - upper) * CORES + core
 
 
 def my_y():
@@ -323,7 +344,7 @@
         here = pl.ds(pl.multiple_of(row * size, size), size)
         there = pl.ds(pl.multiple_of(got_row * size, size), size)
         expert, z = place_at(place)
-        owner = device_at(expert, z, (y + shift) % along_y, (core + half) % CORES)
+        owner = order_of(expert, z, (y + shift) % along_y, (core + half) % CORES)
         total = total_ref[here] + got_ref[there].astype(jnp.float32)
         shares_ref[owner] = total.astype(jnp.bfloat16)
         return carry
@@ -417,7 +438,8 @@
     shares, gate_delta, up_delta, hidden = lax.optimization_barrier(
         (shares, gate_delta, up_delta, hidden)
     )
-    shares = lax.all_to_all(shares, BOTH, 0, 0, tiled=True)
+    everyone = [[order_at(place) for place in range(devices)]]
+    shares = lax.all_to_all(shares, BOTH, 0, 0, axis_index_groups=everyone, tiled=True)
     token_grad = sum_shares(shares, tokens.shape[1])
     grad_down = jnp.dot(hidden.T, dy, preferred_element_type=jnp.float32)
     grad_gate = jnp.dot(x.T, gate_delta, preferred_element_type=jnp.float32)

time: 37.5 us -> 37.5 us (level)
  starting transfers between devices: 5.26 us -> 6.11 us
  blocking collectives: 12.6 us -> 11.9 us
    all_to_all x1, starting transfers between devices: 3.5 us -> 4.35 us  [local(): lax.all_to_all(shares, BOTH, 0, 0, axis_index_groups=everyone, tiled=True)]
    all_to_all x1, blocking collectives: 12.6 us -> 11.9 us  [local(): lax.all_to_all(copies, BOTH, 0, 0, axis_index_groups=groups, tiled=True)]
where the time goes in v8:
time: 37.5 us; the launch traced here: 37.1 us
  blocking collectives  11.9 us (32%)
  Pallas kernels  8.29 us (22%)
  matrix products  6.15 us (16%)
  starting transfers between devices  6.11 us (16%)
  waiting for transfers between devices  4 us (11%)
  between operations  0.67 us (2%)
    all_to_all x1, blocking collectives, local(): lax.all_to_all(copies, BOTH, 0, 0, axis_index_groups=groups, tiled=True)  11.9 us
    all_to_all x1, starting transfers between devices, local(): lax.all_to_all(shares, BOTH, 0, 0, axis_index_groups=everyone, tiled=True)  4.35 us
    pallas_call x1, Pallas kernels, fetch(): pl.pallas_call(fetch_kernel, out_shape=tuple((pltpu.VMEM(w.shape[1:], w.d...  2.88 us
    pallas_call x1, Pallas kernels, rows_pass(): pl.pallas_call(rows_kernel, out_shape=(bf16((rows * groups, LANES)), bf16...  2.18 us
    dot_general x1, matrix products, local(): grad_gate = jnp.dot(x.T, gate_delta, preferred_element_type=jnp.float32)  2.05 us
    dot_general x1, matrix products, local(): grad_up = jnp.dot(x.T, up_delta, preferred_element_type=jnp.float32)  2.05 us
    dot_general x1, matrix products, local(): grad_down = jnp.dot(hidden.T, dy, preferred_element_type=jnp.float32)  2.05 us
    all_to_all x1, waiting for transfers between devices, local(): lax.all_to_all(shares, BOTH, 0, 0, axis_index_groups=everyone, tiled=True)  1.86 us
  transfers between devices with their start and end apart: 5, of which 4 were waited for; matrix products, arithmetic and copies ran while one was open for 17% of the time, Pallas kernels for 10%

profile of v8, /device:TPU:0, one launch (start us, length us, event | category | flops | bytes accessed | tf_op | source)
XLA Modules:
  0.0 37.1 jit_solution(9793028412626151148)
XLA Ops:
  0.6 1.0 %shard_map.102 = bf16[8,2,4096]{2,1,0:T(2,128)(2,1)S(1)} custom-call(bf16[1,2,2048]{2,1,0:T(2,128)(2,1)} %tokens_hbm.1, bf16[1,2,2048]{2,1,0:T(2,128)(2,1)} %grad_hbm.1, s32[1,2,4]{2,1,0:T(2,128)} %bitcast.14, bf16[1,2,4]{2,1,0:T(2,128)(2,1)} %bitcast.15), custom_call_target="tpu_custom_call" | custom-call | tf_op jit(solution)/shard_map/pallas_call | solution.py:121
  1.6 11.9 %all_to_all.10.mine_ref = bf16[8,2,4096]{2,1,0:T(2,128)(2,1)S(1)} all-to-all(bf16[8,2,4096]{2,1,0:T(2,128)(2,1)S(1)} %shard_map.102), channel_id=1, replica_groups={{8,4,24,20,12,0,28,16},{9,5,25,21,13,1,29,17},{10,6,26,22,14,2,30,18},{..., dimensions={0} | all-to-all | bytes 262144 | tf_op jit(solution)/shard_map/all_to_all | solution.py:425
  13.5 1.5 %collective-permute-start = (bf16[8,2,4096]{2,1,0:T(2,128)(2,1)S(1)}, bf16[8,2,4096]{2,1,0:T(2,128)(2,1)S(1)}, u32[]{:S(2)}, u32[]{:S(2)}) collective-permute-start(bf16[8,2,4096]{2,1,0:T(2,128)(2,1)S(1)} %all_to_all.10.mine_ref), channel_id=1, source_target_pairs={{2,0},{3,1},{0,2},{1,3},{6,4},{7,5},{4,6},{5,7},{10,8},{11,9},{8,1... | collective-permute-start | bytes 393224 | tf_op jit(solution)/shard_map/ppermute | solution.py:426
  15.0 0.0 collective-permute-start.2
  15.1 2.9 %shard_map.103 = (bf16[2048,512]{1,0:T(8,128)(2,1)S(1)}, bf16[2048,512]{1,0:T(8,128)(2,1)S(1)}, bf16[512,2048]{1,0:T(8,128)(2,1)S(1)}, bf16[16,2048]{1,0:T(8,128)(2,1)S(1)}, bf16[16,2048]{1,0:T(8,128)(2,1)S(1)}) custom-call(bf16[8,2,4096]{2,1,0:T(2,128)(2,1)S(1)} %all_to_all.10.mine_ref, bf16[1,2048,512]{2,1,0:T(8,128)(2,1)} %gate_hbm.1, ...), custom_call_target="tpu_custom_call" | custom-call | bytes 12582912 | tf_op jit(solution)/shard_map/pallas_call | solution.py:178
  17.9 0.6 %collective-permute-done.refs_1_ = bf16[8,2,4096]{2,1,0:T(2,128)(2,1)S(1)} collective-permute-done((bf16[8,2,4096]{2,1,0:T(2,128)(2,1)S(1)}, bf16[8,2,4096]{2,1,0:T(2,128)(2,1)S(1)}, u32[]{:S(2)}, u32[]{:S(2)}) %collective-permute-start) | collective-permute-done | bytes 131104 | tf_op jit(solution)/shard_map/ppermute | solution.py:426
  18.5 0.0 collective-permute-start.1
  18.5 0.0 collective-permute-done.2.refs_0_
  18.5 0.2 shard_map.104
  18.7 1.1 %collective-permute-done.1.refs_0_ = bf16[8,2,4096]{2,1,0:T(2,128)(2,1)S(1)} collective-permute-done((bf16[8,2,4096]{2,1,0:T(2,128)(2,1)S(1)}, bf16[8,2,4096]{2,1,0:T(2,128)(2,1)S(1)}, u32[]{:S(2)}, u32[]{:S(2)}) %collective-permute-start.1) | collective-permute-done | bytes 131104 | tf_op jit(solution)/shard_map/ppermute | solution.py:430
  19.8 2.2 %shard_map.105 = (bf16[512,128]{1,0:T(8,128)(2,1)S(1)}, bf16[64,2048]{1,0:T(8,128)(2,1)S(1)}, bf16[64,2048]{1,0:T(8,128)(2,1)S(1)}, bf16[64,512]{1,0:T(8,128)(2,...) custom-call(bf16[8,2,4096]{2,1,0:T(2,128)(2,1)S(1)} %collective-permute-done.1.refs_0_, ...), custom_call_target="tpu_custom_call" | custom-call | flops 536870912 | bytes 1769472 | tf_op jit(solution)/shard_map/pallas_call | solution.py:285
  22.0 0.2 collective-permute-start.3
  22.2 0.8 %shard_map.106.total_ref = f32[512,128]{1,0:T(8,128)S(1)} custom-call(bf16[64,512]{1,0:T(8,128)(2,1)S(1)} %get-tuple-element.38.gate_delta_ref, bf16[64,512]{1,0:T(8,128)(2,1)S(1)} %get-tuple-element.39.up_delta_ref, bf16[2048,512]{1,0:T(8,128)(2,1)S(1)} %get-tuple-element.29.refs_5_.gate_ref, bf16[2048,512]{1,0:T(8,128)(2,1)S(1)} %get-tuple-element.30.refs_6_.up_ref), custom_call_target="tpu_custom_call" | custom-call | flops 134217728 | bytes 2490368 | tf_op jit(solution)/shard_map/pallas_call | solution.py:323
  23.0 0.4 %collective-permute-done.3.got_ref = bf16[512,128]{1,0:T(8,128)(2,1)S(1)} collective-permute-done((bf16[512,128]{1,0:T(8,128)(2,1)S(1)}, bf16[512,128]{1,0:T(8,128)(2,1)S(1)}, u32[]{:S(2)}, u32[]{:S(2)}) %collective-permute-start.3) | collective-permute-done | bytes 131104 | tf_op jit(solution)/shard_map/ppermute | solution.py:435
  23.4 0.7 %shard_map.107 = bf16[32,16,128]{2,1,0:T(8,128)(2,1)} custom-call(f32[512,128]{1,0:T(8,128)S(1)} %shard_map.106.total_ref, bf16[512,128]{1,0:T(8,128)(2,1)S(1)} %collective-permute-done.3.got_ref), custom_call_target="tpu_custom_call" | custom-call | tf_op jit(solution)/shard_map/pallas_call | solution.py:357
  24.1 4.4 %all-to-all-start.1 = ((bf16[32,16,128]{2,1,0:T(8,128)(2,1)}), bf16[32,16,128]{2,1,0:T(8,128)(2,1)S(1)}, u32[]{:S(2)}, u32[]{:S(2)}) async-start(bf16[32,16,128]{2,1,0:T(8,128)(2,1)} %shard_map.107), calls=%async_computation.1 | async-start | bytes 262144 | tf_op jit(solution)/shard_map/all_to_all | solution.py:442
  28.5 2.1 %fusion = bf16[1,2048,512]{2,1,0:T(8,128)(2,1)} fusion(bf16[64,2048]{1,0:T(8,128)(2,1)S(1)} %get-tuple-element.37, bf16[64,512]{1,0:T(8,128)(2,1)S(1)} %get-tuple-element.38.gate_delta_ref), kind=kOutput, calls=%fused_computation.3 | convolution fusion | flops 135266304 | bytes 2424832 | tf_op jit(solution)/shard_map/dot_general | solution.py:445
  30.5 2.0 %fusion.1 = bf16[1,2048,512]{2,1,0:T(8,128)(2,1)} fusion(bf16[64,2048]{1,0:T(8,128)(2,1)S(1)} %get-tuple-element.37, bf16[64,512]{1,0:T(8,128)(2,1)S(1)} %get-tuple-element.39.up_delta_ref), kind=kOutput, calls=%fused_computation.4 | convolution fusion | flops 135266304 | bytes 2424832 | tf_op jit(solution)/shard_map/dot_general | solution.py:446
  32.6 2.0 %fusion.2 = bf16[1,512,2048]{2,1,0:T(8,128)(2,1)} fusion(bf16[64,512]{1,0:T(8,128)(2,1)S(1)} %get-tuple-element.40, bf16[64,2048]{1,0:T(8,128)(2,1)S(1)} %get-tuple-element.41), kind=kOutput, calls=%fused_computation.5 | convolution fusion | flops 135266304 | bytes 2424832 | tf_op jit(solution)/shard_map/dot_general | solution.py:444
  34.6 1.9 %all-to-all-done.1.shares_ref = bf16[32,16,128]{2,1,0:T(8,128)(2,1)S(1)} async-done(((bf16[32,16,128]{2,1,0:T(8,128)(2,1)}), bf16[32,16,128]{2,1,0:T(8,128)(2,1)S(1)}, u32[]{:S(2)}, u32[]{:S(2)}) %all-to-all-start.1) | async-done | bytes 131104 | tf_op jit(solution)/shard_map/all_to_all | solution.py:442
  36.5 0.6 %shard_map.108 = bf16[1,2,2048]{2,1,0:T(2,128)(2,1)} custom-call(bf16[32,16,128]{2,1,0:T(8,128)(2,1)S(1)} %all-to-all-done.1.shares_ref), custom_call_target="tpu_custom_call" | custom-call | tf_op jit(solution)/shard_map/pallas_call | solution.py:390
Async XLA Ops:
  13.5 5.0 %collective-permute-start = (bf16[8,2,4096]{2,1,0:T(2,128)(2,1)S(1)}, bf16[8,2,4096]{2,1,0:T(2,128)(2,1)S(1)}, u32[]{:S(2)}, u32[]{:S(2)}) collective-permute-start(bf16[8,2,4096]{2,1,0:T(2,128)(2,1)S(1)} %all_to_all.10.mine_ref), channel_id=1, source_target_pairs={{2,0},{3,1},{0,2},{1,3},{6,4},{7,5},{4,6},{5,7},{10,8},{11,9},{8,1... | collective-permute-start | bytes 393224 | tf_op jit(solution)/shard_map/ppermute | solution.py:426
  15.0 3.5 %collective-permute-start.2 = (bf16[8,2,4096]{2,1,0:T(2,128)(2,1)S(1)}, bf16[8,2,4096]{2,1,0:T(2,128)(2,1)S(1)}, u32[]{:S(2)}, u32[]{:S(2)}) collective-permute-start(bf16[8,2,4096]{2,1,0:T(2,128)(2,1)S(1)} %all_to_all.10.mine_ref), channel_id=1, source_target_pairs={{0,1},{1,0},{2,3},{3,2},{4,5},{5,4},{6,7},{7,6},{8,9},{9,8},{10,11... | collective-permute-start | bytes 393224 | tf_op jit(solution)/shard_map/ppermute | solution.py:427
  18.5 1.3 %collective-permute-start.1 = (bf16[8,2,4096]{2,1,0:T(2,128)(2,1)S(1)}, bf16[8,2,4096]{2,1,0:T(2,128)(2,1)S(1)}, u32[]{:S(2)}, u32[]{:S(2)}) collective-permute-start(bf16[8,2,4096]{2,1,0:T(2,128)(2,1)S(1)} %collective-permute-done.refs_1_), channel_id=1, source_target_pairs={{0,1},{1,0},{2,3},{3,2},{4,5},{5,4},{6,7},{7,6},{8,9},{9,8},{10,11... | collective-permute-start | bytes 393224 | tf_op jit(solution)/shard_map/ppermute | solution.py:430
  22.0 1.4 %collective-permute-start.3 = (bf16[512,128]{1,0:T(8,128)(2,1)S(1)}, bf16[512,128]{1,0:T(8,128)(2,1)S(1)}, u32[]{:S(2)}, u32[]{:S(2)}) collective-permute-start(bf16[512,128]{1,0:T(8,128)(2,1)S(1)} %get-tuple-element.34), channel_id=1, source_target_pairs={{0,1},{1,0},{2,3},{3,2},{4,5},{5,4},{6,7},{7,6},{8,9},{9,8},{10,11... | collective-permute-start | bytes 393224 | tf_op jit(solution)/shard_map/ppermute | solution.py:435
  24.1 12.4 %all-to-all-start.1 = ((bf16[32,16,128]{2,1,0:T(8,128)(2,1)}), bf16[32,16,128]{2,1,0:T(8,128)(2,1)S(1)}, u32[]{:S(2)}, u32[]{:S(2)}) async-start(bf16[32,16,128]{2,1,0:T(8,128)(2,1)} %shard_map.107), calls=%async_computation.1 | async-start | bytes 262144 | tf_op jit(solution)/shard_map/all_to_all | solution.py:442

commit v9 on v8

--- a/solution.py
+++ b/solution.py
@@ -141,16 +141,20 @@
     ]
 
 
-def lay_out(src_ref, x_ref, dy_ref, first):
-    chips, tok_dev, _ = src_ref.shape
-    width = x_ref.shape[1]
+def halves(ref):
+    width = ref.shape[2] // 2
+    return ref.at[:, :, pl.ds(0, width)], ref.at[:, :, pl.ds(width, width)]
+
+
+def lay_out(src_refs, dst_refs, first):
+    chips, tok_dev, _ = src_refs[0].shape
     per_tile = TILE // tok_dev
 
     def step(tile, carry):
         rows = pl.ds(pl.multiple_of(first + tile * TILE, TILE), TILE)
-        blocks = [src_ref[tile * per_tile + j] for j in range(per_tile)]
-        x_ref[rows] = jnp.concatenate([b[:, :width] for b in blocks], axis=0)
-        dy_ref[rows] = jnp.concatenate([b[:, width:] for b in blocks], axis=0)
+        for src_ref, dst_ref in zip(src_refs, dst_refs):
+            blocks = [src_ref[tile * per_tile + j] for j in range(per_tile)]
+            dst_ref[rows] = jnp.concatenate(blocks, axis=0)
         return carry
 
     tiles = chips // per_tile
@@ -165,7 +169,7 @@
     copies += copy_pieces(down_hbm, down_ref, sems.at[2])
     for copy in copies:
         copy.start()
-    lay_out(mine_ref, x_ref, dy_ref, 0)
+    lay_out(halves(mine_ref), (x_ref, dy_ref), 0)
     for copy in copies:
         copy.wait()
 
@@ -187,25 +191,27 @@
     )(mine, *weights)
 
 
-def lay_kernel(*refs):
+def lay_kernel(other_ref, *refs):
     *src_refs, x_ref, dy_ref = refs
-    for i, src_ref in enumerate(src_refs):
-        lay_out(src_ref, x_ref, dy_ref, i * (x_ref.shape[0] // len(src_refs)))
-
-
-def lay(*blocks):
-    places, tok_dev, row = blocks[0].shape
-    rows = (len(blocks) * places * tok_dev, row // 2)
+    pairs = [halves(other_ref), *zip(src_refs[::2], src_refs[1::2])]
+    for i, pair in enumerate(pairs):
+        lay_out(pair, (x_ref, dy_ref), i * (x_ref.shape[0] // len(pairs)))
+
+
+def lay(other, beside):
+    places, tok_dev, row = other.shape
+    blocks = 1 + len(beside)
+    rows = (blocks * places * tok_dev, row // 2)
     return pl.pallas_call(
         lay_kernel,
         out_shape=(pltpu.VMEM(rows, jnp.bfloat16), pltpu.VMEM(rows, jnp.bfloat16)),
-        in_specs=[VMEM] * len(blocks),
+        in_specs=[VMEM] * (2 * blocks - 1),
         out_specs=(VMEM,) * 2,
         cost_estimate=pl.CostEstimate(
-            flops=0, bytes_accessed=8 * len(blocks) * blocks[0].size, transcendentals=0
-        ),
-        compiler_params=vmem((8 << 20) + 8 * len(blocks) * blocks[0].size),
-    )(*blocks)
+            flops=0, bytes_accessed=8 * blocks * other.size, transcendentals=0
+        ),
+        compiler_params=vmem((8 << 20) + 8 * blocks * other.size),
+    )(other, *(part for pair in beside for part in pair))
 
 
 def my_core():
@@ -238,7 +244,7 @@
 
 def rows_kernel(*refs):
     along_y = sizes()[2]
-    other_refs, refs = refs[: along_y - 1], refs[along_y - 1 :]
+    other_refs, refs = refs[: 2 * along_y - 2], refs[2 * along_y - 2 :]
     my_x_ref, my_dy_ref, laid_x_ref, laid_dy_ref, gate_ref, up_ref, down_ref, *refs = refs
     sent_ref, x_ref, dy_ref, gate_delta_ref, up_delta_ref, hidden_ref, total_ref = refs
     size = my_x_ref.shape[0]
@@ -248,8 +254,8 @@
         there = pl.ds(size if i == 0 else 2 * i * size, size)
         x_ref[there] = laid_x_ref[i * size : (i + 1) * size]
         dy_ref[there] = laid_dy_ref[i * size : (i + 1) * size]
-    for i, other_ref in enumerate(other_refs):
-        lay_out(other_ref, x_ref, dy_ref, (2 * i + 3) * size)
+    for i, pair in enumerate(zip(other_refs[::2], other_refs[1::2])):
+        lay_out(pair, (x_ref, dy_ref), (2 * i + 3) * size)
 
     def step(block, first):
         rows = pl.ds(pl.multiple_of(block * ROWS, ROWS), ROWS)
@@ -292,14 +298,14 @@
             bf16((rows, hidden)),
             bf16((rows, hidden)),
         ),
-        in_specs=[VMEM] * (len(others) + 7),
+        in_specs=[VMEM] * (2 * len(others) + 7),
         out_specs=(VMEM,) * 6,
         scratch_shapes=[pltpu.VMEM((ROWS * groups, LANES), jnp.float32)],
         cost_estimate=pl.CostEstimate(
             flops=8 * rows * width * hidden, bytes_accessed=moved, transcendentals=rows * hidden
         ),
         compiler_params=vmem((12 << 20) + 2 * moved),
-    )(*others, my_x, my_dy, laid_x, laid_dy, gate, up, down)
+    )(*(part for pair in others for part in pair), my_x, my_dy, laid_x, laid_dy, gate, up, down)
 
 
 def finish_kernel(gate_delta_ref, up_delta_ref, gate_ref, up_ref, total_ref):
@@ -423,12 +429,17 @@
 
     copies = pack(tokens, out_grad, expert_ids, gate_scores, places)
     mine = lax.all_to_all(copies, BOTH, 0, 0, axis_index_groups=groups, tiled=True)
-    beside = [lax.ppermute(mine, BOTH, from_y(shift)) for shift in range(1, along_y)]
+    width = mine.shape[2] // 2
+    parts = (mine[:, :, :width], mine[:, :, width:])
+    beside = [
+        [lax.ppermute(part, BOTH, from_y(shift)) for part in parts]
+        for shift in range(1, along_y)
+    ]
     other = lax.ppermute(mine, BOTH, core_pairs)
     gate, up, down, my_x, my_dy = fetch(mine, w_gate, w_up, w_down)
-    *beside, my_x = lax.optimization_barrier((*beside, my_x))
-    others = [lax.ppermute(piece, BOTH, core_pairs) for piece in beside]
-    laid_x, laid_dy = lay(other, *beside)
+    beside, my_x = lax.optimization_barrier((beside, my_x))
+    others = [[lax.ppermute(part, BOTH, core_pairs) for part in pair] for pair in beside]
+    laid_x, laid_dy = lay(other, beside)
     sent, x, dy, gate_delta, up_delta, hidden = rows_pass(
         others, my_x, my_dy, laid_x, laid_dy, gate, up, down
     )

time: 37.5 us -> 38.1 us (1.016)
  starting transfers between devices: 6.11 us -> 6.95 us
    ppermute x2 -> x4, starting transfers between devices: 1.54 us -> 2.6 us  [the longest x2 2.09 us: local(): lax.ppermute(part, BOTH, from_y(shift))]
    all_to_all x1, starting transfers between devices: 4.35 us -> 3.93 us  [local(): lax.all_to_all(shares, BOTH, 0, 0, axis_index_groups=everyone, tiled=True)]
    ppermute x2 -> x4, waiting for transfers between devices: 1.69 us -> 1.57 us  [the longest x2 0.86 us: local(): lax.ppermute(part, BOTH, from_y(shift))]
  transfers between devices with their start and end apart: 5 -> 7, of which waited for: 4 -> 5; matrix products, arithmetic and copies ran while one was open for 17% -> 16% of each run, Pallas kernels for 10% -> 10%
where the time goes in v9:
time: 38.1 us; the launch traced here: 37.8 us
  blocking collectives  11.9 us (31%)
  Pallas kernels  8.28 us (22%)
  starting transfers between devices  6.95 us (18%)
  matrix products  6.15 us (16%)
  waiting for transfers between devices  3.68 us (10%)
  between operations  0.69 us (2%)
    all_to_all x1, blocking collectives, local(): lax.all_to_all(copies, BOTH, 0, 0, axis_index_groups=groups, tiled=True)  11.9 us
    all_to_all x1, starting transfers between devices, local(): lax.all_to_all(shares, BOTH, 0, 0, axis_index_groups=everyone, tiled=True)  3.93 us
    pallas_call x1, Pallas kernels, fetch(): pl.pallas_call(fetch_kernel, out_shape=tuple((pltpu.VMEM(w.shape[1:], w.d...  2.88 us
    pallas_call x1, Pallas kernels, rows_pass(): pl.pallas_call(rows_kernel, out_shape=(bf16((rows * groups, LANES)), bf16...  2.18 us
    ppermute x2, starting transfers between devices, local(): lax.ppermute(part, BOTH, from_y(shift))  2.09 us
    dot_general x1, matrix products, local(): grad_gate = jnp.dot(x.T, gate_delta, preferred_element_type=jnp.float32)  2.05 us
    dot_general x1, matrix products, local(): grad_up = jnp.dot(x.T, up_delta, preferred_element_type=jnp.float32)  2.05 us
    dot_general x1, matrix products, local(): grad_down = jnp.dot(hidden.T, dy, preferred_element_type=jnp.float32)  2.05 us
  transfers between devices with their start and end apart: 7, of which 5 were waited for; matrix products, arithmetic and copies ran while one was open for 16% of the time, Pallas kernels for 10%

profile of v9, /device:TPU:0, one launch (start us, length us, event | category | flops | bytes accessed | tf_op | source)
XLA Modules:
  0.0 37.8 jit_solution(2992377495281332991)
XLA Ops:
  0.6 1.0 %shard_map.102 = bf16[8,2,4096]{2,1,0:T(2,128)(2,1)S(1)} custom-call(bf16[1,2,2048]{2,1,0:T(2,128)(2,1)} %tokens_hbm.1, bf16[1,2,2048]{2,1,0:T(2,128)(2,1)} %grad_hbm.1, s32[1,2,4]{2,1,0:T(2,128)} %bitcast.14, bf16[1,2,4]{2,1,0:T(2,128)(2,1)} %bitcast.15), custom_call_target="tpu_custom_call" | custom-call | tf_op jit(solution)/shard_map/pallas_call | solution.py:121
  1.6 11.9 %all_to_all.10.mine_ref = bf16[8,2,4096]{2,1,0:T(2,128)(2,1)S(1)} all-to-all(bf16[8,2,4096]{2,1,0:T(2,128)(2,1)S(1)} %shard_map.102), channel_id=1, replica_groups={{8,4,24,20,12,0,28,16},{9,5,25,21,13,1,29,17},{10,6,26,22,14,2,30,18},{..., dimensions={0} | all-to-all | bytes 262144 | tf_op jit(solution)/shard_map/all_to_all | solution.py:431
  13.5 0.1 fusion.3
  13.6 1.6 %collective-permute-start.1 = (bf16[8,2,2048]{2,1,0:T(2,128)(2,1)S(1)}, bf16[8,2,2048]{2,1,0:T(2,128)(2,1)S(1)}, u32[]{:S(2)}, u32[]{:S(2)}) collective-permute-start(bf16[8,2,2048]{2,1,0:T(2,128)(2,1)S(1)} %get-tuple-element.44), channel_id=1, source_target_pairs={{2,0},{3,1},{0,2},{1,3},{6,4},{7,5},{4,6},{5,7},{10,8},{11,9},{8,1... | collective-permute-start | bytes 196616 | tf_op jit(solution)/shard_map/ppermute | solution.py:435
  15.2 0.5 %collective-permute-start = (bf16[8,2,2048]{2,1,0:T(2,128)(2,1)S(1)}, bf16[8,2,2048]{2,1,0:T(2,128)(2,1)S(1)}, u32[]{:S(2)}, u32[]{:S(2)}) collective-permute-start(bf16[8,2,2048]{2,1,0:T(2,128)(2,1)S(1)} %get-tuple-element.45), channel_id=1, source_target_pairs={{2,0},{3,1},{0,2},{1,3},{6,4},{7,5},{4,6},{5,7},{10,8},{11,9},{8,1... | collective-permute-start | bytes 196616 | tf_op jit(solution)/shard_map/ppermute | solution.py:435
  15.7 0.0 collective-permute-start.4
  15.7 2.9 %shard_map.103 = (bf16[2048,512]{1,0:T(8,128)(2,1)S(1)}, bf16[2048,512]{1,0:T(8,128)(2,1)S(1)}, bf16[512,2048]{1,0:T(8,128)(2,1)S(1)}, bf16[16,2048]{1,0:T(8,128)(2,1)S(1)}, bf16[16,2048]{1,0:T(8,128)(2,1)S(1)}) custom-call(bf16[8,2,4096]{2,1,0:T(2,128)(2,1)S(1)} %all_to_all.10.mine_ref, bf16[1,2048,512]{2,1,0:T(8,128)(2,1)} %gate_hbm.1, ...), custom_call_target="tpu_custom_call" | custom-call | bytes 12582912 | tf_op jit(solution)/shard_map/pallas_call | solution.py:182
  18.6 0.0 collective-permute-done.1.refs_1_
  18.6 0.9 %collective-permute-done.refs_0_ = bf16[8,2,2048]{2,1,0:T(2,128)(2,1)S(1)} collective-permute-done((bf16[8,2,2048]{2,1,0:T(2,128)(2,1)S(1)}, bf16[8,2,2048]{2,1,0:T(2,128)(2,1)S(1)}, u32[]{:S(2)}, u32[]{:S(2)}) %collective-permute-start) | collective-permute-done | bytes 65568 | tf_op jit(solution)/shard_map/ppermute | solution.py:435
  19.5 0.0 collective-permute-start.2
  19.5 0.5 %collective-permute-start.3 = (bf16[8,2,2048]{2,1,0:T(2,128)(2,1)S(1)}, bf16[8,2,2048]{2,1,0:T(2,128)(2,1)S(1)}, u32[]{:S(2)}, u32[]{:S(2)}) collective-permute-start(bf16[8,2,2048]{2,1,0:T(2,128)(2,1)S(1)} %collective-permute-done.1.refs_1_), channel_id=1, source_target_pairs={{0,1},{1,0},{2,3},{3,2},{4,5},{5,4},{6,7},{7,6},{8,9},{9,8},{10,11... | collective-permute-start | bytes 196616 | tf_op jit(solution)/shard_map/ppermute | solution.py:441
  20.0 0.0 collective-permute-done.4.other_ref
  20.0 0.2 shard_map.104
  20.2 0.6 %collective-permute-done.2.refs_0_ = bf16[8,2,2048]{2,1,0:T(2,128)(2,1)S(1)} collective-permute-done((bf16[8,2,2048]{2,1,0:T(2,128)(2,1)S(1)}, bf16[8,2,2048]{2,1,0:T(2,128)(2,1)S(1)}, u32[]{:S(2)}, u32[]{:S(2)}) %collective-permute-start.2) | collective-permute-done | bytes 65568 | tf_op jit(solution)/shard_map/ppermute | solution.py:441
  20.7 0.2 collective-permute-done.3.refs_1_
  20.9 2.2 %shard_map.105 = (bf16[512,128]{1,0:T(8,128)(2,1)S(1)}, bf16[64,2048]{1,0:T(8,128)(2,1)S(1)}, bf16[64,2048]{1,0:T(8,128)(2,1)S(1)}, bf16[64,512]{1,0:T(8,128)(2,...) custom-call(bf16[8,2,2048]{2,1,0:T(2,128)(2,1)S(1)} %collective-permute-done.2.refs_0_, ...), custom_call_target="tpu_custom_call" | custom-call | flops 536870912 | bytes 1769472 | tf_op jit(solution)/shard_map/pallas_call | solution.py:291
  23.1 0.4 %collective-permute-start.5 = (bf16[512,128]{1,0:T(8,128)(2,1)S(1)}, bf16[512,128]{1,0:T(8,128)(2,1)S(1)}, u32[]{:S(2)}, u32[]{:S(2)}) collective-permute-start(bf16[512,128]{1,0:T(8,128)(2,1)S(1)} %get-tuple-element.36), channel_id=1, source_target_pairs={{0,1},{1,0},{2,3},{3,2},{4,5},{5,4},{6,7},{7,6},{8,9},{9,8},{10,11... | collective-permute-start | bytes 393224 | tf_op jit(solution)/shard_map/ppermute | solution.py:446
  23.5 0.8 %shard_map.106.total_ref = f32[512,128]{1,0:T(8,128)S(1)} custom-call(bf16[64,512]{1,0:T(8,128)(2,1)S(1)} %get-tuple-element.40.gate_delta_ref, bf16[64,512]{1,0:T(8,128)(2,1)S(1)} %get-tuple-element.41.up_delta_ref, bf16[2048,512]{1,0:T(8,128)(2,1)S(1)} %get-tuple-element.31.refs_6_.gate_ref, bf16[2048,512]{1,0:T(8,128)(2,1)S(1)} %get-tuple-element.32.refs_7_.up_ref), custom_call_target="tpu_custom_call" | custom-call | flops 134217728 | bytes 2490368 | tf_op jit(solution)/shard_map/pallas_call | solution.py:329
  24.2 0.2 collective-permute-done.5.got_ref
  24.5 0.7 %shard_map.107 = bf16[32,16,128]{2,1,0:T(8,128)(2,1)} custom-call(f32[512,128]{1,0:T(8,128)S(1)} %shard_map.106.total_ref, bf16[512,128]{1,0:T(8,128)(2,1)S(1)} %collective-permute-done.5.got_ref), custom_call_target="tpu_custom_call" | custom-call | tf_op jit(solution)/shard_map/pallas_call | solution.py:363
  25.2 3.9 %all-to-all-start.1 = ((bf16[32,16,128]{2,1,0:T(8,128)(2,1)}), bf16[32,16,128]{2,1,0:T(8,128)(2,1)S(1)}, u32[]{:S(2)}, u32[]{:S(2)}) async-start(bf16[32,16,128]{2,1,0:T(8,128)(2,1)} %shard_map.107), calls=%async_computation.1 | async-start | bytes 262144 | tf_op jit(solution)/shard_map/all_to_all | solution.py:453
  29.1 2.1 %fusion = bf16[1,2048,512]{2,1,0:T(8,128)(2,1)} fusion(bf16[64,2048]{1,0:T(8,128)(2,1)S(1)} %get-tuple-element.39, bf16[64,512]{1,0:T(8,128)(2,1)S(1)} %get-tuple-element.40.gate_delta_ref), kind=kOutput, calls=%fused_computation.3 | convolution fusion | flops 135266304 | bytes 2424832 | tf_op jit(solution)/shard_map/dot_general | solution.py:456
  31.1 2.0 %fusion.1 = bf16[1,2048,512]{2,1,0:T(8,128)(2,1)} fusion(bf16[64,2048]{1,0:T(8,128)(2,1)S(1)} %get-tuple-element.39, bf16[64,512]{1,0:T(8,128)(2,1)S(1)} %get-tuple-element.41.up_delta_ref), kind=kOutput, calls=%fused_computation.4 | convolution fusion | flops 135266304 | bytes 2424832 | tf_op jit(solution)/shard_map/dot_general | solution.py:457
  33.2 2.0 %fusion.2 = bf16[1,512,2048]{2,1,0:T(8,128)(2,1)} fusion(bf16[64,512]{1,0:T(8,128)(2,1)S(1)} %get-tuple-element.42, bf16[64,2048]{1,0:T(8,128)(2,1)S(1)} %get-tuple-element.43), kind=kOutput, calls=%fused_computation.5 | convolution fusion | flops 135266304 | bytes 2424832 | tf_op jit(solution)/shard_map/dot_general | solution.py:455
  35.2 1.9 %all-to-all-done.1.shares_ref = bf16[32,16,128]{2,1,0:T(8,128)(2,1)S(1)} async-done(((bf16[32,16,128]{2,1,0:T(8,128)(2,1)}), bf16[32,16,128]{2,1,0:T(8,128)(2,1)S(1)}, u32[]{:S(2)}, u32[]{:S(2)}) %all-to-all-start.1) | async-done | bytes 131104 | tf_op jit(solution)/shard_map/all_to_all | solution.py:453
  37.1 0.6 %shard_map.108 = bf16[1,2,2048]{2,1,0:T(2,128)(2,1)} custom-call(bf16[32,16,128]{2,1,0:T(8,128)(2,1)S(1)} %all-to-all-done.1.shares_ref), custom_call_target="tpu_custom_call" | custom-call | tf_op jit(solution)/shard_map/pallas_call | solution.py:396
Async XLA Ops:
  13.6 5.0 %collective-permute-start.1 = (bf16[8,2,2048]{2,1,0:T(2,128)(2,1)S(1)}, bf16[8,2,2048]{2,1,0:T(2,128)(2,1)S(1)}, u32[]{:S(2)}, u32[]{:S(2)}) collective-permute-start(bf16[8,2,2048]{2,1,0:T(2,128)(2,1)S(1)} %get-tuple-element.44), channel_id=1, source_target_pairs={{2,0},{3,1},{0,2},{1,3},{6,4},{7,5},{4,6},{5,7},{10,8},{11,9},{8,1... | collective-permute-start | bytes 196616 | tf_op jit(solution)/shard_map/ppermute | solution.py:435
  15.2 4.3 %collective-permute-start = (bf16[8,2,2048]{2,1,0:T(2,128)(2,1)S(1)}, bf16[8,2,2048]{2,1,0:T(2,128)(2,1)S(1)}, u32[]{:S(2)}, u32[]{:S(2)}) collective-permute-start(bf16[8,2,2048]{2,1,0:T(2,128)(2,1)S(1)} %get-tuple-element.45), channel_id=1, source_target_pairs={{2,0},{3,1},{0,2},{1,3},{6,4},{7,5},{4,6},{5,7},{10,8},{11,9},{8,1... | collective-permute-start | bytes 196616 | tf_op jit(solution)/shard_map/ppermute | solution.py:435
  15.7 4.3 %collective-permute-start.4 = (bf16[8,2,4096]{2,1,0:T(2,128)(2,1)S(1)}, bf16[8,2,4096]{2,1,0:T(2,128)(2,1)S(1)}, u32[]{:S(2)}, u32[]{:S(2)}) collective-permute-start(bf16[8,2,4096]{2,1,0:T(2,128)(2,1)S(1)} %all_to_all.10.mine_ref), channel_id=1, source_target_pairs={{0,1},{1,0},{2,3},{3,2},{4,5},{5,4},{6,7},{7,6},{8,9},{9,8},{10,11... | collective-permute-start | bytes 393224 | tf_op jit(solution)/shard_map/ppermute | solution.py:438
  19.5 1.3 %collective-permute-start.2 = (bf16[8,2,2048]{2,1,0:T(2,128)(2,1)S(1)}, bf16[8,2,2048]{2,1,0:T(2,128)(2,1)S(1)}, u32[]{:S(2)}, u32[]{:S(2)}) collective-permute-start(bf16[8,2,2048]{2,1,0:T(2,128)(2,1)S(1)} %collective-permute-done.refs_0_), channel_id=1, source_target_pairs={{0,1},{1,0},{2,3},{3,2},{4,5},{5,4},{6,7},{7,6},{8,9},{9,8},{10,11... | collective-permute-start | bytes 196616 | tf_op jit(solution)/shard_map/ppermute | solution.py:441
  19.5 1.4 %collective-permute-start.3 = (bf16[8,2,2048]{2,1,0:T(2,128)(2,1)S(1)}, bf16[8,2,2048]{2,1,0:T(2,128)(2,1)S(1)}, u32[]{:S(2)}, u32[]{:S(2)}) collective-permute-start(bf16[8,2,2048]{2,1,0:T(2,128)(2,1)S(1)} %collective-permute-done.1.refs_1_), channel_id=1, source_target_pairs={{0,1},{1,0},{2,3},{3,2},{4,5},{5,4},{6,7},{7,6},{8,9},{9,8},{10,11... | collective-permute-start | bytes 196616 | tf_op jit(solution)/shard_map/ppermute | solution.py:441
  23.1 1.4 %collective-permute-start.5 = (bf16[512,128]{1,0:T(8,128)(2,1)S(1)}, bf16[512,128]{1,0:T(8,128)(2,1)S(1)}, u32[]{:S(2)}, u32[]{:S(2)}) collective-permute-start(bf16[512,128]{1,0:T(8,128)(2,1)S(1)} %get-tuple-element.36), channel_id=1, source_target_pairs={{0,1},{1,0},{2,3},{3,2},{4,5},{5,4},{6,7},{7,6},{8,9},{9,8},{10,11... | collective-permute-start | bytes 393224 | tf_op jit(solution)/shard_map/ppermute | solution.py:446
  25.2 12.0 %all-to-all-start.1 = ((bf16[32,16,128]{2,1,0:T(8,128)(2,1)}), bf16[32,16,128]{2,1,0:T(8,128)(2,1)S(1)}, u32[]{:S(2)}, u32[]{:S(2)}) async-start(bf16[32,16,128]{2,1,0:T(8,128)(2,1)} %shard_map.107), calls=%async_computation.1 | async-start | bytes 262144 | tf_op jit(solution)/shard_map/all_to_all | solution.py:453

commit v10 on v8

--- a/solution.py
+++ b/solution.py
@@ -434,10 +434,10 @@
     )
     got = lax.ppermute(sent, BOTH, core_pairs)
     total = finish(gate_delta, up_delta, gate, up)
+    got, gate_delta, up_delta, hidden = lax.optimization_barrier(
+        (got, gate_delta, up_delta, hidden)
+    )
     shares = share(total, got, devices)
-    shares, gate_delta, up_delta, hidden = lax.optimization_barrier(
-        (shares, gate_delta, up_delta, hidden)
-    )
     everyone = [[order_at(place) for place in range(devices)]]
     shares = lax.all_to_all(shares, BOTH, 0, 0, axis_index_groups=everyone, tiled=True)
     token_grad = sum_shares(shares, tokens.shape[1])

time: 37.5 us -> 37.5 us (level)
  no operation moved by 1% of the time
where the time goes in v10:
time: 37.5 us; the launch traced here: 37.1 us
  blocking collectives  11.9 us (32%)
  Pallas kernels  8.29 us (22%)
  matrix products  6.15 us (16%)
  starting transfers between devices  6.11 us (16%)
  waiting for transfers between devices  4 us (11%)
  between operations  0.67 us (2%)
    all_to_all x1, blocking collectives, local(): lax.all_to_all(copies, BOTH, 0, 0, axis_index_groups=groups, tiled=True)  11.9 us
    all_to_all x1, starting transfers between devices, local(): lax.all_to_all(shares, BOTH, 0, 0, axis_index_groups=everyone, tiled=True)  4.35 us
    pallas_call x1, Pallas kernels, fetch(): pl.pallas_call(fetch_kernel, out_shape=tuple((pltpu.VMEM(w.shape[1:], w.d...  2.88 us
    pallas_call x1, Pallas kernels, rows_pass(): pl.pallas_call(rows_kernel, out_shape=(bf16((rows * groups, LANES)), bf16...  2.18 us
    dot_general x1, matrix products, local(): grad_gate = jnp.dot(x.T, gate_delta, preferred_element_type=jnp.float32)  2.05 us
    dot_general x1, matrix products, local(): grad_up = jnp.dot(x.T, up_delta, preferred_element_type=jnp.float32)  2.05 us
    dot_general x1, matrix products, local(): grad_down = jnp.dot(hidden.T, dy, preferred_element_type=jnp.float32)  2.05 us
    all_to_all x1, waiting for transfers between devices, local(): lax.all_to_all(shares, BOTH, 0, 0, axis_index_groups=everyone, tiled=True)  1.86 us
  transfers between devices with their start and end apart: 5, of which 4 were waited for; matrix products, arithmetic and copies ran while one was open for 17% of the time, Pallas kernels for 10%

profile of v10, /device:TPU:0, one launch (start us, length us, event | category | flops | bytes accessed | tf_op | source)
XLA Modules:
  0.0 37.1 jit_solution(13019192567584301993)
XLA Ops:
  0.6 1.0 %shard_map.102 = bf16[8,2,4096]{2,1,0:T(2,128)(2,1)S(1)} custom-call(bf16[1,2,2048]{2,1,0:T(2,128)(2,1)} %tokens_hbm.1, bf16[1,2,2048]{2,1,0:T(2,128)(2,1)} %grad_hbm.1, s32[1,2,4]{2,1,0:T(2,128)} %bitcast.14, bf16[1,2,4]{2,1,0:T(2,128)(2,1)} %bitcast.15), custom_call_target="tpu_custom_call" | custom-call | tf_op jit(solution)/shard_map/pallas_call | solution.py:121
  1.6 11.9 %all_to_all.10.mine_ref = bf16[8,2,4096]{2,1,0:T(2,128)(2,1)S(1)} all-to-all(bf16[8,2,4096]{2,1,0:T(2,128)(2,1)S(1)} %shard_map.102), channel_id=1, replica_groups={{8,4,24,20,12,0,28,16},{9,5,25,21,13,1,29,17},{10,6,26,22,14,2,30,18},{..., dimensions={0} | all-to-all | bytes 262144 | tf_op jit(solution)/shard_map/all_to_all | solution.py:425
  13.5 1.5 %collective-permute-start = (bf16[8,2,4096]{2,1,0:T(2,128)(2,1)S(1)}, bf16[8,2,4096]{2,1,0:T(2,128)(2,1)S(1)}, u32[]{:S(2)}, u32[]{:S(2)}) collective-permute-start(bf16[8,2,4096]{2,1,0:T(2,128)(2,1)S(1)} %all_to_all.10.mine_ref), channel_id=1, source_target_pairs={{2,0},{3,1},{0,2},{1,3},{6,4},{7,5},{4,6},{5,7},{10,8},{11,9},{8,1... | collective-permute-start | bytes 393224 | tf_op jit(solution)/shard_map/ppermute | solution.py:426
  15.0 0.0 collective-permute-start.2
  15.1 2.9 %shard_map.103 = (bf16[2048,512]{1,0:T(8,128)(2,1)S(1)}, bf16[2048,512]{1,0:T(8,128)(2,1)S(1)}, bf16[512,2048]{1,0:T(8,128)(2,1)S(1)}, bf16[16,2048]{1,0:T(8,128)(2,1)S(1)}, bf16[16,2048]{1,0:T(8,128)(2,1)S(1)}) custom-call(bf16[8,2,4096]{2,1,0:T(2,128)(2,1)S(1)} %all_to_all.10.mine_ref, bf16[1,2048,512]{2,1,0:T(8,128)(2,1)} %gate_hbm.1, ...), custom_call_target="tpu_custom_call" | custom-call | bytes 12582912 | tf_op jit(solution)/shard_map/pallas_call | solution.py:178
  17.9 0.6 %collective-permute-done.refs_1_ = bf16[8,2,4096]{2,1,0:T(2,128)(2,1)S(1)} collective-permute-done((bf16[8,2,4096]{2,1,0:T(2,128)(2,1)S(1)}, bf16[8,2,4096]{2,1,0:T(2,128)(2,1)S(1)}, u32[]{:S(2)}, u32[]{:S(2)}) %collective-permute-start) | collective-permute-done | bytes 131104 | tf_op jit(solution)/shard_map/ppermute | solution.py:426
  18.5 0.0 collective-permute-start.1
  18.5 0.0 collective-permute-done.2.refs_0_
  18.5 0.2 shard_map.104
  18.7 1.1 %collective-permute-done.1.refs_0_ = bf16[8,2,4096]{2,1,0:T(2,128)(2,1)S(1)} collective-permute-done((bf16[8,2,4096]{2,1,0:T(2,128)(2,1)S(1)}, bf16[8,2,4096]{2,1,0:T(2,128)(2,1)S(1)}, u32[]{:S(2)}, u32[]{:S(2)}) %collective-permute-start.1) | collective-permute-done | bytes 131104 | tf_op jit(solution)/shard_map/ppermute | solution.py:430
  19.8 2.2 %shard_map.105 = (bf16[512,128]{1,0:T(8,128)(2,1)S(1)}, bf16[64,2048]{1,0:T(8,128)(2,1)S(1)}, bf16[64,2048]{1,0:T(8,128)(2,1)S(1)}, bf16[64,512]{1,0:T(8,128)(2,...) custom-call(bf16[8,2,4096]{2,1,0:T(2,128)(2,1)S(1)} %collective-permute-done.1.refs_0_, ...), custom_call_target="tpu_custom_call" | custom-call | flops 536870912 | bytes 1769472 | tf_op jit(solution)/shard_map/pallas_call | solution.py:285
  22.0 0.2 collective-permute-start.3
  22.2 0.8 %shard_map.106.total_ref = f32[512,128]{1,0:T(8,128)S(1)} custom-call(bf16[64,512]{1,0:T(8,128)(2,1)S(1)} %get-tuple-element.38.gate_delta_ref, bf16[64,512]{1,0:T(8,128)(2,1)S(1)} %get-tuple-element.39.up_delta_ref, bf16[2048,512]{1,0:T(8,128)(2,1)S(1)} %get-tuple-element.29.refs_5_.gate_ref, bf16[2048,512]{1,0:T(8,128)(2,1)S(1)} %get-tuple-element.30.refs_6_.up_ref), custom_call_target="tpu_custom_call" | custom-call | flops 134217728 | bytes 2490368 | tf_op jit(solution)/shard_map/pallas_call | solution.py:323
  23.0 0.4 %collective-permute-done.3.got_ref = bf16[512,128]{1,0:T(8,128)(2,1)S(1)} collective-permute-done((bf16[512,128]{1,0:T(8,128)(2,1)S(1)}, bf16[512,128]{1,0:T(8,128)(2,1)S(1)}, u32[]{:S(2)}, u32[]{:S(2)}) %collective-permute-start.3) | collective-permute-done | bytes 131104 | tf_op jit(solution)/shard_map/ppermute | solution.py:435
  23.4 0.7 %shard_map.107 = bf16[32,16,128]{2,1,0:T(8,128)(2,1)} custom-call(f32[512,128]{1,0:T(8,128)S(1)} %shard_map.106.total_ref, bf16[512,128]{1,0:T(8,128)(2,1)S(1)} %collective-permute-done.3.got_ref), custom_call_target="tpu_custom_call" | custom-call | tf_op jit(solution)/shard_map/pallas_call | solution.py:357
  24.1 4.4 %all-to-all-start.1 = ((bf16[32,16,128]{2,1,0:T(8,128)(2,1)}), bf16[32,16,128]{2,1,0:T(8,128)(2,1)S(1)}, u32[]{:S(2)}, u32[]{:S(2)}) async-start(bf16[32,16,128]{2,1,0:T(8,128)(2,1)} %shard_map.107), calls=%async_computation.1 | async-start | bytes 262144 | tf_op jit(solution)/shard_map/all_to_all | solution.py:442
  28.5 2.1 %fusion = bf16[1,2048,512]{2,1,0:T(8,128)(2,1)} fusion(bf16[64,2048]{1,0:T(8,128)(2,1)S(1)} %get-tuple-element.37, bf16[64,512]{1,0:T(8,128)(2,1)S(1)} %get-tuple-element.38.gate_delta_ref), kind=kOutput, calls=%fused_computation.3 | convolution fusion | flops 135266304 | bytes 2424832 | tf_op jit(solution)/shard_map/dot_general | solution.py:445
  30.5 2.0 %fusion.1 = bf16[1,2048,512]{2,1,0:T(8,128)(2,1)} fusion(bf16[64,2048]{1,0:T(8,128)(2,1)S(1)} %get-tuple-element.37, bf16[64,512]{1,0:T(8,128)(2,1)S(1)} %get-tuple-element.39.up_delta_ref), kind=kOutput, calls=%fused_computation.4 | convolution fusion | flops 135266304 | bytes 2424832 | tf_op jit(solution)/shard_map/dot_general | solution.py:446
  32.6 2.0 %fusion.2 = bf16[1,512,2048]{2,1,0:T(8,128)(2,1)} fusion(bf16[64,512]{1,0:T(8,128)(2,1)S(1)} %get-tuple-element.40, bf16[64,2048]{1,0:T(8,128)(2,1)S(1)} %get-tuple-element.41), kind=kOutput, calls=%fused_computation.5 | convolution fusion | flops 135266304 | bytes 2424832 | tf_op jit(solution)/shard_map/dot_general | solution.py:444
  34.6 1.9 %all-to-all-done.1.shares_ref = bf16[32,16,128]{2,1,0:T(8,128)(2,1)S(1)} async-done(((bf16[32,16,128]{2,1,0:T(8,128)(2,1)}), bf16[32,16,128]{2,1,0:T(8,128)(2,1)S(1)}, u32[]{:S(2)}, u32[]{:S(2)}) %all-to-all-start.1) | async-done | bytes 131104 | tf_op jit(solution)/shard_map/all_to_all | solution.py:442
  36.5 0.6 %shard_map.108 = bf16[1,2,2048]{2,1,0:T(2,128)(2,1)} custom-call(bf16[32,16,128]{2,1,0:T(8,128)(2,1)S(1)} %all-to-all-done.1.shares_ref), custom_call_target="tpu_custom_call" | custom-call | tf_op jit(solution)/shard_map/pallas_call | solution.py:390
Async XLA Ops:
  13.5 5.0 %collective-permute-start = (bf16[8,2,4096]{2,1,0:T(2,128)(2,1)S(1)}, bf16[8,2,4096]{2,1,0:T(2,128)(2,1)S(1)}, u32[]{:S(2)}, u32[]{:S(2)}) collective-permute-start(bf16[8,2,4096]{2,1,0:T(2,128)(2,1)S(1)} %all_to_all.10.mine_ref), channel_id=1, source_target_pairs={{2,0},{3,1},{0,2},{1,3},{6,4},{7,5},{4,6},{5,7},{10,8},{11,9},{8,1... | collective-permute-start | bytes 393224 | tf_op jit(solution)/shard_map/ppermute | solution.py:426
  15.0 3.5 %collective-permute-start.2 = (bf16[8,2,4096]{2,1,0:T(2,128)(2,1)S(1)}, bf16[8,2,4096]{2,1,0:T(2,128)(2,1)S(1)}, u32[]{:S(2)}, u32[]{:S(2)}) collective-permute-start(bf16[8,2,4096]{2,1,0:T(2,128)(2,1)S(1)} %all_to_all.10.mine_ref), channel_id=1, source_target_pairs={{0,1},{1,0},{2,3},{3,2},{4,5},{5,4},{6,7},{7,6},{8,9},{9,8},{10,11... | collective-permute-start | bytes 393224 | tf_op jit(solution)/shard_map/ppermute | solution.py:427
  18.5 1.3 %collective-permute-start.1 = (bf16[8,2,4096]{2,1,0:T(2,128)(2,1)S(1)}, bf16[8,2,4096]{2,1,0:T(2,128)(2,1)S(1)}, u32[]{:S(2)}, u32[]{:S(2)}) collective-permute-start(bf16[8,2,4096]{2,1,0:T(2,128)(2,1)S(1)} %collective-permute-done.refs_1_), channel_id=1, source_target_pairs={{0,1},{1,0},{2,3},{3,2},{4,5},{5,4},{6,7},{7,6},{8,9},{9,8},{10,11... | collective-permute-start | bytes 393224 | tf_op jit(solution)/shard_map/ppermute | solution.py:430
  22.0 1.4 %collective-permute-start.3 = (bf16[512,128]{1,0:T(8,128)(2,1)S(1)}, bf16[512,128]{1,0:T(8,128)(2,1)S(1)}, u32[]{:S(2)}, u32[]{:S(2)}) collective-permute-start(bf16[512,128]{1,0:T(8,128)(2,1)S(1)} %get-tuple-element.34), channel_id=1, source_target_pairs={{0,1},{1,0},{2,3},{3,2},{4,5},{5,4},{6,7},{7,6},{8,9},{9,8},{10,11... | collective-permute-start | bytes 393224 | tf_op jit(solution)/shard_map/ppermute | solution.py:435
  24.1 12.4 %all-to-all-start.1 = ((bf16[32,16,128]{2,1,0:T(8,128)(2,1)}), bf16[32,16,128]{2,1,0:T(8,128)(2,1)S(1)}, u32[]{:S(2)}, u32[]{:S(2)}) async-start(bf16[32,16,128]{2,1,0:T(8,128)(2,1)} %shard_map.107), calls=%async_computation.1 | async-start | bytes 262144 | tf_op jit(solution)/shard_map/all_to_all | solution.py:442

commit v11 on v10

--- a/solution.py
+++ b/solution.py
@@ -51,13 +51,16 @@
     place, core = place // CORES, place % CORES
     place, turn = place // 2, place % 2
     place, expert = place // experts, place % experts
-    return device_at(expert, z_at(turn + 2 * (place // along_y)), place % along_y, core)
+    y = place % along_y
+    y = y + turn * (along_y - 1 - 2 * y)
+    return device_at(expert, z_at(turn + 2 * (place // along_y)), y, core)
 
 
 def order_of(expert, z, y, core):
     experts, along_z, along_y, _ = sizes()
     upper = (z >= along_z // 2) * 1
     step = upper * (z - along_z // 2) + (1 - upper) * (along_z // 2 - 1 - z)
+    y = y + (1 - upper) * (along_y - 1 - 2 * y)
     return (((step * along_y + y) * experts + expert) * 2 + 1 - upper) * CORES + core
 
 

time: 37.5 us -> 37.3 us (level)
  no operation moved by 1% of the time
where the time goes in v11:
time: 37.3 us; the launch traced here: 37.1 us
  blocking collectives  11.9 us (32%)
  Pallas kernels  8.3 us (22%)
  matrix products  6.16 us (17%)
  starting transfers between devices  6.11 us (16%)
  waiting for transfers between devices  3.9 us (10%)
  between operations  0.67 us (2%)
    all_to_all x1, blocking collectives, local(): lax.all_to_all(copies, BOTH, 0, 0, axis_index_groups=groups, tiled=True)  11.9 us
    all_to_all x1, starting transfers between devices, local(): lax.all_to_all(shares, BOTH, 0, 0, axis_index_groups=everyone, tiled=True)  4.35 us
    pallas_call x1, Pallas kernels, fetch(): pl.pallas_call(fetch_kernel, out_shape=tuple((pltpu.VMEM(w.shape[1:], w.d...  2.88 us
    pallas_call x1, Pallas kernels, rows_pass(): pl.pallas_call(rows_kernel, out_shape=(bf16((rows * groups, LANES)), bf16...  2.18 us
    dot_general x1, matrix products, local(): grad_gate = jnp.dot(x.T, gate_delta, preferred_element_type=jnp.float32)  2.06 us
    dot_general x1, matrix products, local(): grad_up = jnp.dot(x.T, up_delta, preferred_element_type=jnp.float32)  2.05 us
    dot_general x1, matrix products, local(): grad_down = jnp.dot(hidden.T, dy, preferred_element_type=jnp.float32)  2.05 us
    all_to_all x1, waiting for transfers between devices, local(): lax.all_to_all(shares, BOTH, 0, 0, axis_index_groups=everyone, tiled=True)  1.76 us
  transfers between devices with their start and end apart: 5, of which 4 were waited for; matrix products, arithmetic and copies ran while one was open for 17% of the time, Pallas kernels for 10%

profile of v11, /device:TPU:0, one launch (start us, length us, event | category | flops | bytes accessed | tf_op | source)
XLA Modules:
  0.0 37.1 jit_solution(11356146701404012206)
XLA Ops:
  0.6 1.0 %shard_map.102 = bf16[8,2,4096]{2,1,0:T(2,128)(2,1)S(1)} custom-call(bf16[1,2,2048]{2,1,0:T(2,128)(2,1)} %tokens_hbm.1, bf16[1,2,2048]{2,1,0:T(2,128)(2,1)} %grad_hbm.1, s32[1,2,4]{2,1,0:T(2,128)} %bitcast.14, bf16[1,2,4]{2,1,0:T(2,128)(2,1)} %bitcast.15), custom_call_target="tpu_custom_call" | custom-call | tf_op jit(solution)/shard_map/pallas_call | solution.py:124
  1.6 11.9 %all_to_all.10.mine_ref = bf16[8,2,4096]{2,1,0:T(2,128)(2,1)S(1)} all-to-all(bf16[8,2,4096]{2,1,0:T(2,128)(2,1)S(1)} %shard_map.102), channel_id=1, replica_groups={{8,4,24,20,12,0,28,16},{9,5,25,21,13,1,29,17},{10,6,26,22,14,2,30,18},{..., dimensions={0} | all-to-all | bytes 262144 | tf_op jit(solution)/shard_map/all_to_all | solution.py:428
  13.5 1.5 %collective-permute-start = (bf16[8,2,4096]{2,1,0:T(2,128)(2,1)S(1)}, bf16[8,2,4096]{2,1,0:T(2,128)(2,1)S(1)}, u32[]{:S(2)}, u32[]{:S(2)}) collective-permute-start(bf16[8,2,4096]{2,1,0:T(2,128)(2,1)S(1)} %all_to_all.10.mine_ref), channel_id=1, source_target_pairs={{2,0},{3,1},{0,2},{1,3},{6,4},{7,5},{4,6},{5,7},{10,8},{11,9},{8,1... | collective-permute-start | bytes 393224 | tf_op jit(solution)/shard_map/ppermute | solution.py:429
  15.0 0.0 collective-permute-start.2
  15.1 2.9 %shard_map.103 = (bf16[2048,512]{1,0:T(8,128)(2,1)S(1)}, bf16[2048,512]{1,0:T(8,128)(2,1)S(1)}, bf16[512,2048]{1,0:T(8,128)(2,1)S(1)}, bf16[16,2048]{1,0:T(8,128)(2,1)S(1)}, bf16[16,2048]{1,0:T(8,128)(2,1)S(1)}) custom-call(bf16[8,2,4096]{2,1,0:T(2,128)(2,1)S(1)} %all_to_all.10.mine_ref, bf16[1,2048,512]{2,1,0:T(8,128)(2,1)} %gate_hbm.1, ...), custom_call_target="tpu_custom_call" | custom-call | bytes 12582912 | tf_op jit(solution)/shard_map/pallas_call | solution.py:181
  17.9 0.6 %collective-permute-done.refs_1_ = bf16[8,2,4096]{2,1,0:T(2,128)(2,1)S(1)} collective-permute-done((bf16[8,2,4096]{2,1,0:T(2,128)(2,1)S(1)}, bf16[8,2,4096]{2,1,0:T(2,128)(2,1)S(1)}, u32[]{:S(2)}, u32[]{:S(2)}) %collective-permute-start) | collective-permute-done | bytes 131104 | tf_op jit(solution)/shard_map/ppermute | solution.py:429
  18.5 0.0 collective-permute-start.1
  18.5 0.0 collective-permute-done.2.refs_0_
  18.5 0.2 shard_map.104
  18.7 1.1 %collective-permute-done.1.refs_0_ = bf16[8,2,4096]{2,1,0:T(2,128)(2,1)S(1)} collective-permute-done((bf16[8,2,4096]{2,1,0:T(2,128)(2,1)S(1)}, bf16[8,2,4096]{2,1,0:T(2,128)(2,1)S(1)}, u32[]{:S(2)}, u32[]{:S(2)}) %collective-permute-start.1) | collective-permute-done | bytes 131104 | tf_op jit(solution)/shard_map/ppermute | solution.py:433
  19.8 2.2 %shard_map.105 = (bf16[512,128]{1,0:T(8,128)(2,1)S(1)}, bf16[64,2048]{1,0:T(8,128)(2,1)S(1)}, bf16[64,2048]{1,0:T(8,128)(2,1)S(1)}, bf16[64,512]{1,0:T(8,128)(2,...) custom-call(bf16[8,2,4096]{2,1,0:T(2,128)(2,1)S(1)} %collective-permute-done.1.refs_0_, ...), custom_call_target="tpu_custom_call" | custom-call | flops 536870912 | bytes 1769472 | tf_op jit(solution)/shard_map/pallas_call | solution.py:288
  22.0 0.2 collective-permute-start.3
  22.2 0.8 %shard_map.106.total_ref = f32[512,128]{1,0:T(8,128)S(1)} custom-call(bf16[64,512]{1,0:T(8,128)(2,1)S(1)} %get-tuple-element.38.gate_delta_ref, bf16[64,512]{1,0:T(8,128)(2,1)S(1)} %get-tuple-element.39.up_delta_ref, bf16[2048,512]{1,0:T(8,128)(2,1)S(1)} %get-tuple-element.29.refs_5_.gate_ref, bf16[2048,512]{1,0:T(8,128)(2,1)S(1)} %get-tuple-element.30.refs_6_.up_ref), custom_call_target="tpu_custom_call" | custom-call | flops 134217728 | bytes 2490368 | tf_op jit(solution)/shard_map/pallas_call | solution.py:326
  23.0 0.4 %collective-permute-done.3.got_ref = bf16[512,128]{1,0:T(8,128)(2,1)S(1)} collective-permute-done((bf16[512,128]{1,0:T(8,128)(2,1)S(1)}, bf16[512,128]{1,0:T(8,128)(2,1)S(1)}, u32[]{:S(2)}, u32[]{:S(2)}) %collective-permute-start.3) | collective-permute-done | bytes 131104 | tf_op jit(solution)/shard_map/ppermute | solution.py:438
  23.4 0.7 %shard_map.107 = bf16[32,16,128]{2,1,0:T(8,128)(2,1)} custom-call(f32[512,128]{1,0:T(8,128)S(1)} %shard_map.106.total_ref, bf16[512,128]{1,0:T(8,128)(2,1)S(1)} %collective-permute-done.3.got_ref), custom_call_target="tpu_custom_call" | custom-call | tf_op jit(solution)/shard_map/pallas_call | solution.py:360
  24.1 4.4 %all-to-all-start.1 = ((bf16[32,16,128]{2,1,0:T(8,128)(2,1)}), bf16[32,16,128]{2,1,0:T(8,128)(2,1)S(1)}, u32[]{:S(2)}, u32[]{:S(2)}) async-start(bf16[32,16,128]{2,1,0:T(8,128)(2,1)} %shard_map.107), calls=%async_computation.1 | async-start | bytes 262144 | tf_op jit(solution)/shard_map/all_to_all | solution.py:445
  28.5 2.1 %fusion = bf16[1,2048,512]{2,1,0:T(8,128)(2,1)} fusion(bf16[64,2048]{1,0:T(8,128)(2,1)S(1)} %get-tuple-element.37, bf16[64,512]{1,0:T(8,128)(2,1)S(1)} %get-tuple-element.38.gate_delta_ref), kind=kOutput, calls=%fused_computation.3 | convolution fusion | flops 135266304 | bytes 2424832 | tf_op jit(solution)/shard_map/dot_general | solution.py:448
  30.5 2.1 %fusion.1 = bf16[1,2048,512]{2,1,0:T(8,128)(2,1)} fusion(bf16[64,2048]{1,0:T(8,128)(2,1)S(1)} %get-tuple-element.37, bf16[64,512]{1,0:T(8,128)(2,1)S(1)} %get-tuple-element.39.up_delta_ref), kind=kOutput, calls=%fused_computation.4 | convolution fusion | flops 135266304 | bytes 2424832 | tf_op jit(solution)/shard_map/dot_general | solution.py:449
  32.6 2.0 %fusion.2 = bf16[1,512,2048]{2,1,0:T(8,128)(2,1)} fusion(bf16[64,512]{1,0:T(8,128)(2,1)S(1)} %get-tuple-element.40, bf16[64,2048]{1,0:T(8,128)(2,1)S(1)} %get-tuple-element.41), kind=kOutput, calls=%fused_computation.5 | convolution fusion | flops 135266304 | bytes 2424832 | tf_op jit(solution)/shard_map/dot_general | solution.py:447
  34.6 1.8 %all-to-all-done.1.shares_ref = bf16[32,16,128]{2,1,0:T(8,128)(2,1)S(1)} async-done(((bf16[32,16,128]{2,1,0:T(8,128)(2,1)}), bf16[32,16,128]{2,1,0:T(8,128)(2,1)S(1)}, u32[]{:S(2)}, u32[]{:S(2)}) %all-to-all-start.1) | async-done | bytes 131104 | tf_op jit(solution)/shard_map/all_to_all | solution.py:445
  36.4 0.6 %shard_map.108 = bf16[1,2,2048]{2,1,0:T(2,128)(2,1)} custom-call(bf16[32,16,128]{2,1,0:T(8,128)(2,1)S(1)} %all-to-all-done.1.shares_ref), custom_call_target="tpu_custom_call" | custom-call | tf_op jit(solution)/shard_map/pallas_call | solution.py:393
Async XLA Ops:
  13.5 5.0 %collective-permute-start = (bf16[8,2,4096]{2,1,0:T(2,128)(2,1)S(1)}, bf16[8,2,4096]{2,1,0:T(2,128)(2,1)S(1)}, u32[]{:S(2)}, u32[]{:S(2)}) collective-permute-start(bf16[8,2,4096]{2,1,0:T(2,128)(2,1)S(1)} %all_to_all.10.mine_ref), channel_id=1, source_target_pairs={{2,0},{3,1},{0,2},{1,3},{6,4},{7,5},{4,6},{5,7},{10,8},{11,9},{8,1... | collective-permute-start | bytes 393224 | tf_op jit(solution)/shard_map/ppermute | solution.py:429
  15.0 3.5 %collective-permute-start.2 = (bf16[8,2,4096]{2,1,0:T(2,128)(2,1)S(1)}, bf16[8,2,4096]{2,1,0:T(2,128)(2,1)S(1)}, u32[]{:S(2)}, u32[]{:S(2)}) collective-permute-start(bf16[8,2,4096]{2,1,0:T(2,128)(2,1)S(1)} %all_to_all.10.mine_ref), channel_id=1, source_target_pairs={{0,1},{1,0},{2,3},{3,2},{4,5},{5,4},{6,7},{7,6},{8,9},{9,8},{10,11... | collective-permute-start | bytes 393224 | tf_op jit(solution)/shard_map/ppermute | solution.py:430
  18.5 1.3 %collective-permute-start.1 = (bf16[8,2,4096]{2,1,0:T(2,128)(2,1)S(1)}, bf16[8,2,4096]{2,1,0:T(2,128)(2,1)S(1)}, u32[]{:S(2)}, u32[]{:S(2)}) collective-permute-start(bf16[8,2,4096]{2,1,0:T(2,128)(2,1)S(1)} %collective-permute-done.refs_1_), channel_id=1, source_target_pairs={{0,1},{1,0},{2,3},{3,2},{4,5},{5,4},{6,7},{7,6},{8,9},{9,8},{10,11... | collective-permute-start | bytes 393224 | tf_op jit(solution)/shard_map/ppermute | solution.py:433
  22.0 1.4 %collective-permute-start.3 = (bf16[512,128]{1,0:T(8,128)(2,1)S(1)}, bf16[512,128]{1,0:T(8,128)(2,1)S(1)}, u32[]{:S(2)}, u32[]{:S(2)}) collective-permute-start(bf16[512,128]{1,0:T(8,128)(2,1)S(1)} %get-tuple-element.34), channel_id=1, source_target_pairs={{0,1},{1,0},{2,3},{3,2},{4,5},{5,4},{6,7},{7,6},{8,9},{9,8},{10,11... | collective-permute-start | bytes 393224 | tf_op jit(solution)/shard_map/ppermute | solution.py:438
  24.1 12.3 %all-to-all-start.1 = ((bf16[32,16,128]{2,1,0:T(8,128)(2,1)}), bf16[32,16,128]{2,1,0:T(8,128)(2,1)S(1)}, u32[]{:S(2)}, u32[]{:S(2)}) async-start(bf16[32,16,128]{2,1,0:T(8,128)(2,1)} %shard_map.107), calls=%async_computation.1 | async-start | bytes 262144 | tf_op jit(solution)/shard_map/all_to_all | solution.py:445

commit v12 on v11

--- a/solution.py
+++ b/solution.py
@@ -41,9 +41,8 @@
 
 
 def place_at(place):
-    experts = sizes()[0]
-    pair = place // 2
-    return pair % experts, z_at(place % 2 + 2 * (pair // experts))
+    experts, along_z, _, _ = sizes()
+    return place % experts, (place // experts + along_z // 2) % along_z
 
 
 def order_at(place):
@@ -83,7 +82,7 @@
     ]
     for copy in copies:
         copy.start()
-    for copy in copies:
+    for copy in copies[:2]:
         copy.wait()
     places, tok_dev, _ = out_ref.shape
     width = tokens_ref.shape[2]
@@ -101,6 +100,8 @@
         score = jnp.sum(jnp.where(mine, scores, 0.0), axis=1, keepdims=True)
         weights = jnp.sum(jnp.where(lane == named, score, 0.0), axis=0, keepdims=True)
         table = jnp.where(row == i, weights, table)
+    for copy in copies[2:]:
+        copy.wait()
     grad = grad_ref[0].astype(jnp.float32)
     for expert in range(experts):
         weighted_ref[expert] = (grad * table[:, expert : expert + 1]).astype(jnp.bfloat16)

time: 37.3 us -> 37.1 us (level)
  starting transfers between devices: 6.11 us -> 5.27 us
  blocking collectives: 11.9 us -> 12.6 us
    all_to_all x1, starting transfers between devices: 4.35 us -> 3.51 us  [local(): lax.all_to_all(shares, BOTH, 0, 0, axis_index_groups=everyone, tiled=True)]
    all_to_all x1, blocking collectives: 11.9 us -> 12.6 us  [local(): lax.all_to_all(copies, BOTH, 0, 0, axis_index_groups=groups, tiled=True)]
where the time goes in v12:
time: 37.1 us; the launch traced here: 36.8 us
  blocking collectives  12.6 us (34%)
  Pallas kernels  8.22 us (22%)
  matrix products  6.15 us (17%)
  starting transfers between devices  5.27 us (14%)
  waiting for transfers between devices  3.9 us (11%)
  between operations  0.67 us (2%)
    all_to_all x1, blocking collectives, local(): lax.all_to_all(copies, BOTH, 0, 0, axis_index_groups=groups, tiled=True)  12.6 us
    all_to_all x1, starting transfers between devices, local(): lax.all_to_all(shares, BOTH, 0, 0, axis_index_groups=everyone, tiled=True)  3.51 us
    pallas_call x1, Pallas kernels, fetch(): pl.pallas_call(fetch_kernel, out_shape=tuple((pltpu.VMEM(w.shape[1:], w.d...  2.88 us
    pallas_call x1, Pallas kernels, rows_pass(): pl.pallas_call(rows_kernel, out_shape=(bf16((rows * groups, LANES)), bf16...  2.18 us
    dot_general x1, matrix products, local(): grad_gate = jnp.dot(x.T, gate_delta, preferred_element_type=jnp.float32)  2.05 us
    dot_general x1, matrix products, local(): grad_up = jnp.dot(x.T, up_delta, preferred_element_type=jnp.float32)  2.05 us
    dot_general x1, matrix products, local(): grad_down = jnp.dot(hidden.T, dy, preferred_element_type=jnp.float32)  2.05 us
    all_to_all x1, waiting for transfers between devices, local(): lax.all_to_all(shares, BOTH, 0, 0, axis_index_groups=everyone, tiled=True)  1.76 us
  transfers between devices with their start and end apart: 5, of which 4 were waited for; matrix products, arithmetic and copies ran while one was open for 17% of the time, Pallas kernels for 10%

profile of v12, /device:TPU:0, one launch (start us, length us, event | category | flops | bytes accessed | tf_op | source)
XLA Modules:
  0.0 36.8 jit_solution(13835452710007472179)
XLA Ops:
  0.6 0.9 %shard_map.102 = bf16[8,2,4096]{2,1,0:T(2,128)(2,1)S(1)} custom-call(bf16[1,2,2048]{2,1,0:T(2,128)(2,1)} %tokens_hbm.1, bf16[1,2,2048]{2,1,0:T(2,128)(2,1)} %grad_hbm.1, s32[1,2,4]{2,1,0:T(2,128)} %bitcast.14, bf16[1,2,4]{2,1,0:T(2,128)(2,1)} %bitcast.15), custom_call_target="tpu_custom_call" | custom-call | tf_op jit(solution)/shard_map/pallas_call | solution.py:125
  1.5 12.6 %all_to_all.10.mine_ref = bf16[8,2,4096]{2,1,0:T(2,128)(2,1)S(1)} all-to-all(bf16[8,2,4096]{2,1,0:T(2,128)(2,1)S(1)} %shard_map.102), channel_id=1, replica_groups={{8,24,12,28,0,16,4,20},{9,25,13,29,1,17,5,21},{10,26,14,30,2,18,6,22},{..., dimensions={0} | all-to-all | bytes 262144 | tf_op jit(solution)/shard_map/all_to_all | solution.py:429
  14.1 1.5 %collective-permute-start = (bf16[8,2,4096]{2,1,0:T(2,128)(2,1)S(1)}, bf16[8,2,4096]{2,1,0:T(2,128)(2,1)S(1)}, u32[]{:S(2)}, u32[]{:S(2)}) collective-permute-start(bf16[8,2,4096]{2,1,0:T(2,128)(2,1)S(1)} %all_to_all.10.mine_ref), channel_id=1, source_target_pairs={{2,0},{3,1},{0,2},{1,3},{6,4},{7,5},{4,6},{5,7},{10,8},{11,9},{8,1... | collective-permute-start | bytes 393224 | tf_op jit(solution)/shard_map/ppermute | solution.py:430
  15.7 0.0 collective-permute-start.2
  15.7 2.9 %shard_map.103 = (bf16[2048,512]{1,0:T(8,128)(2,1)S(1)}, bf16[2048,512]{1,0:T(8,128)(2,1)S(1)}, bf16[512,2048]{1,0:T(8,128)(2,1)S(1)}, bf16[16,2048]{1,0:T(8,128)(2,1)S(1)}, bf16[16,2048]{1,0:T(8,128)(2,1)S(1)}) custom-call(bf16[8,2,4096]{2,1,0:T(2,128)(2,1)S(1)} %all_to_all.10.mine_ref, bf16[1,2048,512]{2,1,0:T(8,128)(2,1)} %gate_hbm.1, ...), custom_call_target="tpu_custom_call" | custom-call | bytes 12582912 | tf_op jit(solution)/shard_map/pallas_call | solution.py:182
  18.5 0.6 %collective-permute-done.refs_1_ = bf16[8,2,4096]{2,1,0:T(2,128)(2,1)S(1)} collective-permute-done((bf16[8,2,4096]{2,1,0:T(2,128)(2,1)S(1)}, bf16[8,2,4096]{2,1,0:T(2,128)(2,1)S(1)}, u32[]{:S(2)}, u32[]{:S(2)}) %collective-permute-start) | collective-permute-done | bytes 131104 | tf_op jit(solution)/shard_map/ppermute | solution.py:430
  19.1 0.0 collective-permute-start.1
  19.1 0.0 collective-permute-done.2.refs_0_
  19.1 0.2 shard_map.104
  19.3 1.1 %collective-permute-done.1.refs_0_ = bf16[8,2,4096]{2,1,0:T(2,128)(2,1)S(1)} collective-permute-done((bf16[8,2,4096]{2,1,0:T(2,128)(2,1)S(1)}, bf16[8,2,4096]{2,1,0:T(2,128)(2,1)S(1)}, u32[]{:S(2)}, u32[]{:S(2)}) %collective-permute-start.1) | collective-permute-done | bytes 131104 | tf_op jit(solution)/shard_map/ppermute | solution.py:434
  20.5 2.2 %shard_map.105 = (bf16[512,128]{1,0:T(8,128)(2,1)S(1)}, bf16[64,2048]{1,0:T(8,128)(2,1)S(1)}, bf16[64,2048]{1,0:T(8,128)(2,1)S(1)}, bf16[64,512]{1,0:T(8,128)(2,...) custom-call(bf16[8,2,4096]{2,1,0:T(2,128)(2,1)S(1)} %collective-permute-done.1.refs_0_, ...), custom_call_target="tpu_custom_call" | custom-call | flops 536870912 | bytes 1769472 | tf_op jit(solution)/shard_map/pallas_call | solution.py:289
  22.6 0.2 collective-permute-start.3
  22.9 0.8 %shard_map.106.total_ref = f32[512,128]{1,0:T(8,128)S(1)} custom-call(bf16[64,512]{1,0:T(8,128)(2,1)S(1)} %get-tuple-element.38.gate_delta_ref, bf16[64,512]{1,0:T(8,128)(2,1)S(1)} %get-tuple-element.39.up_delta_ref, bf16[2048,512]{1,0:T(8,128)(2,1)S(1)} %get-tuple-element.29.refs_5_.gate_ref, bf16[2048,512]{1,0:T(8,128)(2,1)S(1)} %get-tuple-element.30.refs_6_.up_ref), custom_call_target="tpu_custom_call" | custom-call | flops 134217728 | bytes 2490368 | tf_op jit(solution)/shard_map/pallas_call | solution.py:327
  23.6 0.4 %collective-permute-done.3.got_ref = bf16[512,128]{1,0:T(8,128)(2,1)S(1)} collective-permute-done((bf16[512,128]{1,0:T(8,128)(2,1)S(1)}, bf16[512,128]{1,0:T(8,128)(2,1)S(1)}, u32[]{:S(2)}, u32[]{:S(2)}) %collective-permute-start.3) | collective-permute-done | bytes 131104 | tf_op jit(solution)/shard_map/ppermute | solution.py:439
  24.1 0.7 %shard_map.107 = bf16[32,16,128]{2,1,0:T(8,128)(2,1)} custom-call(f32[512,128]{1,0:T(8,128)S(1)} %shard_map.106.total_ref, bf16[512,128]{1,0:T(8,128)(2,1)S(1)} %collective-permute-done.3.got_ref), custom_call_target="tpu_custom_call" | custom-call | tf_op jit(solution)/shard_map/pallas_call | solution.py:361
  24.7 3.5 %all-to-all-start.1 = ((bf16[32,16,128]{2,1,0:T(8,128)(2,1)}), bf16[32,16,128]{2,1,0:T(8,128)(2,1)S(1)}, u32[]{:S(2)}, u32[]{:S(2)}) async-start(bf16[32,16,128]{2,1,0:T(8,128)(2,1)} %shard_map.107), calls=%async_computation.1 | async-start | bytes 262144 | tf_op jit(solution)/shard_map/all_to_all | solution.py:446
  28.2 2.1 %fusion = bf16[1,2048,512]{2,1,0:T(8,128)(2,1)} fusion(bf16[64,2048]{1,0:T(8,128)(2,1)S(1)} %get-tuple-element.37, bf16[64,512]{1,0:T(8,128)(2,1)S(1)} %get-tuple-element.38.gate_delta_ref), kind=kOutput, calls=%fused_computation.3 | convolution fusion | flops 135266304 | bytes 2424832 | tf_op jit(solution)/shard_map/dot_general | solution.py:449
  30.3 2.0 %fusion.1 = bf16[1,2048,512]{2,1,0:T(8,128)(2,1)} fusion(bf16[64,2048]{1,0:T(8,128)(2,1)S(1)} %get-tuple-element.37, bf16[64,512]{1,0:T(8,128)(2,1)S(1)} %get-tuple-element.39.up_delta_ref), kind=kOutput, calls=%fused_computation.4 | convolution fusion | flops 135266304 | bytes 2424832 | tf_op jit(solution)/shard_map/dot_general | solution.py:450
  32.4 2.0 %fusion.2 = bf16[1,512,2048]{2,1,0:T(8,128)(2,1)} fusion(bf16[64,512]{1,0:T(8,128)(2,1)S(1)} %get-tuple-element.40, bf16[64,2048]{1,0:T(8,128)(2,1)S(1)} %get-tuple-element.41), kind=kOutput, calls=%fused_computation.5 | convolution fusion | flops 135266304 | bytes 2424832 | tf_op jit(solution)/shard_map/dot_general | solution.py:448
  34.4 1.8 %all-to-all-done.1.shares_ref = bf16[32,16,128]{2,1,0:T(8,128)(2,1)S(1)} async-done(((bf16[32,16,128]{2,1,0:T(8,128)(2,1)}), bf16[32,16,128]{2,1,0:T(8,128)(2,1)S(1)}, u32[]{:S(2)}, u32[]{:S(2)}) %all-to-all-start.1) | async-done | bytes 131104 | tf_op jit(solution)/shard_map/all_to_all | solution.py:446
  36.2 0.6 %shard_map.108 = bf16[1,2,2048]{2,1,0:T(2,128)(2,1)} custom-call(bf16[32,16,128]{2,1,0:T(8,128)(2,1)S(1)} %all-to-all-done.1.shares_ref), custom_call_target="tpu_custom_call" | custom-call | tf_op jit(solution)/shard_map/pallas_call | solution.py:394
Async XLA Ops:
  14.1 5.0 %collective-permute-start = (bf16[8,2,4096]{2,1,0:T(2,128)(2,1)S(1)}, bf16[8,2,4096]{2,1,0:T(2,128)(2,1)S(1)}, u32[]{:S(2)}, u32[]{:S(2)}) collective-permute-start(bf16[8,2,4096]{2,1,0:T(2,128)(2,1)S(1)} %all_to_all.10.mine_ref), channel_id=1, source_target_pairs={{2,0},{3,1},{0,2},{1,3},{6,4},{7,5},{4,6},{5,7},{10,8},{11,9},{8,1... | collective-permute-start | bytes 393224 | tf_op jit(solution)/shard_map/ppermute | solution.py:430
  15.7 3.5 %collective-permute-start.2 = (bf16[8,2,4096]{2,1,0:T(2,128)(2,1)S(1)}, bf16[8,2,4096]{2,1,0:T(2,128)(2,1)S(1)}, u32[]{:S(2)}, u32[]{:S(2)}) collective-permute-start(bf16[8,2,4096]{2,1,0:T(2,128)(2,1)S(1)} %all_to_all.10.mine_ref), channel_id=1, source_target_pairs={{0,1},{1,0},{2,3},{3,2},{4,5},{5,4},{6,7},{7,6},{8,9},{9,8},{10,11... | collective-permute-start | bytes 393224 | tf_op jit(solution)/shard_map/ppermute | solution.py:431
  19.1 1.3 %collective-permute-start.1 = (bf16[8,2,4096]{2,1,0:T(2,128)(2,1)S(1)}, bf16[8,2,4096]{2,1,0:T(2,128)(2,1)S(1)}, u32[]{:S(2)}, u32[]{:S(2)}) collective-permute-start(bf16[8,2,4096]{2,1,0:T(2,128)(2,1)S(1)} %collective-permute-done.refs_1_), channel_id=1, source_target_pairs={{0,1},{1,0},{2,3},{3,2},{4,5},{5,4},{6,7},{7,6},{8,9},{9,8},{10,11... | collective-permute-start | bytes 393224 | tf_op jit(solution)/shard_map/ppermute | solution.py:434
  22.6 1.4 %collective-permute-start.3 = (bf16[512,128]{1,0:T(8,128)(2,1)S(1)}, bf16[512,128]{1,0:T(8,128)(2,1)S(1)}, u32[]{:S(2)}, u32[]{:S(2)}) collective-permute-start(bf16[512,128]{1,0:T(8,128)(2,1)S(1)} %get-tuple-element.34), channel_id=1, source_target_pairs={{0,1},{1,0},{2,3},{3,2},{4,5},{5,4},{6,7},{7,6},{8,9},{9,8},{10,11... | collective-permute-start | bytes 393224 | tf_op jit(solution)/shard_map/ppermute | solution.py:439
  24.7 11.4 %all-to-all-start.1 = ((bf16[32,16,128]{2,1,0:T(8,128)(2,1)}), bf16[32,16,128]{2,1,0:T(8,128)(2,1)S(1)}, u32[]{:S(2)}, u32[]{:S(2)}) async-start(bf16[32,16,128]{2,1,0:T(8,128)(2,1)} %shard_map.107), calls=%async_computation.1 | async-start | bytes 262144 | tf_op jit(solution)/shard_map/all_to_all | solution.py:446

commit v13 on v11

--- a/solution.py
+++ b/solution.py
@@ -83,7 +83,7 @@
     ]
     for copy in copies:
         copy.start()
-    for copy in copies:
+    for copy in copies[:2]:
         copy.wait()
     places, tok_dev, _ = out_ref.shape
     width = tokens_ref.shape[2]
@@ -101,6 +101,8 @@
         score = jnp.sum(jnp.where(mine, scores, 0.0), axis=1, keepdims=True)
         weights = jnp.sum(jnp.where(lane == named, score, 0.0), axis=0, keepdims=True)
         table = jnp.where(row == i, weights, table)
+    for copy in copies[2:]:
+        copy.wait()
     grad = grad_ref[0].astype(jnp.float32)
     for expert in range(experts):
         weighted_ref[expert] = (grad * table[:, expert : expert + 1]).astype(jnp.bfloat16)

time: 37.3 us -> 37.3 us (level)
  no operation moved by 1% of the time
where the time goes in v13:
time: 37.3 us; the launch traced here: 37 us
  blocking collectives  11.9 us (32%)
  Pallas kernels  8.22 us (22%)
  matrix products  6.16 us (17%)
  starting transfers between devices  6.12 us (16%)
  waiting for transfers between devices  3.9 us (10%)
  between operations  0.67 us (2%)
    all_to_all x1, blocking collectives, local(): lax.all_to_all(copies, BOTH, 0, 0, axis_index_groups=groups, tiled=True)  11.9 us
    all_to_all x1, starting transfers between devices, local(): lax.all_to_all(shares, BOTH, 0, 0, axis_index_groups=everyone, tiled=True)  4.36 us
    pallas_call x1, Pallas kernels, fetch(): pl.pallas_call(fetch_kernel, out_shape=tuple((pltpu.VMEM(w.shape[1:], w.d...  2.88 us
    pallas_call x1, Pallas kernels, rows_pass(): pl.pallas_call(rows_kernel, out_shape=(bf16((rows * groups, LANES)), bf16...  2.18 us
    dot_general x1, matrix products, local(): grad_gate = jnp.dot(x.T, gate_delta, preferred_element_type=jnp.float32)  2.06 us
    dot_general x1, matrix products, local(): grad_up = jnp.dot(x.T, up_delta, preferred_element_type=jnp.float32)  2.05 us
    dot_general x1, matrix products, local(): grad_down = jnp.dot(hidden.T, dy, preferred_element_type=jnp.float32)  2.05 us
    all_to_all x1, waiting for transfers between devices, local(): lax.all_to_all(shares, BOTH, 0, 0, axis_index_groups=everyone, tiled=True)  1.76 us
  transfers between devices with their start and end apart: 5, of which 4 were waited for; matrix products, arithmetic and copies ran while one was open for 17% of the time, Pallas kernels for 10%

profile of v13, /device:TPU:0, one launch (start us, length us, event | category | flops | bytes accessed | tf_op | source)
XLA Modules:
  0.0 37.0 jit_solution(3584959006267193404)
XLA Ops:
  0.6 0.9 %shard_map.102 = bf16[8,2,4096]{2,1,0:T(2,128)(2,1)S(1)} custom-call(bf16[1,2,2048]{2,1,0:T(2,128)(2,1)} %tokens_hbm.1, bf16[1,2,2048]{2,1,0:T(2,128)(2,1)} %grad_hbm.1, s32[1,2,4]{2,1,0:T(2,128)} %bitcast.14, bf16[1,2,4]{2,1,0:T(2,128)(2,1)} %bitcast.15), custom_call_target="tpu_custom_call" | custom-call | tf_op jit(solution)/shard_map/pallas_call | solution.py:126
  1.5 11.9 %all_to_all.10.mine_ref = bf16[8,2,4096]{2,1,0:T(2,128)(2,1)S(1)} all-to-all(bf16[8,2,4096]{2,1,0:T(2,128)(2,1)S(1)} %shard_map.102), channel_id=1, replica_groups={{8,4,24,20,12,0,28,16},{9,5,25,21,13,1,29,17},{10,6,26,22,14,2,30,18},{..., dimensions={0} | all-to-all | bytes 262144 | tf_op jit(solution)/shard_map/all_to_all | solution.py:430
  13.5 1.5 %collective-permute-start = (bf16[8,2,4096]{2,1,0:T(2,128)(2,1)S(1)}, bf16[8,2,4096]{2,1,0:T(2,128)(2,1)S(1)}, u32[]{:S(2)}, u32[]{:S(2)}) collective-permute-start(bf16[8,2,4096]{2,1,0:T(2,128)(2,1)S(1)} %all_to_all.10.mine_ref), channel_id=1, source_target_pairs={{2,0},{3,1},{0,2},{1,3},{6,4},{7,5},{4,6},{5,7},{10,8},{11,9},{8,1... | collective-permute-start | bytes 393224 | tf_op jit(solution)/shard_map/ppermute | solution.py:431
  15.0 0.0 collective-permute-start.2
  15.0 2.9 %shard_map.103 = (bf16[2048,512]{1,0:T(8,128)(2,1)S(1)}, bf16[2048,512]{1,0:T(8,128)(2,1)S(1)}, bf16[512,2048]{1,0:T(8,128)(2,1)S(1)}, bf16[16,2048]{1,0:T(8,128)(2,1)S(1)}, bf16[16,2048]{1,0:T(8,128)(2,1)S(1)}) custom-call(bf16[8,2,4096]{2,1,0:T(2,128)(2,1)S(1)} %all_to_all.10.mine_ref, bf16[1,2048,512]{2,1,0:T(8,128)(2,1)} %gate_hbm.1, ...), custom_call_target="tpu_custom_call" | custom-call | bytes 12582912 | tf_op jit(solution)/shard_map/pallas_call | solution.py:183
  17.9 0.6 %collective-permute-done.refs_1_ = bf16[8,2,4096]{2,1,0:T(2,128)(2,1)S(1)} collective-permute-done((bf16[8,2,4096]{2,1,0:T(2,128)(2,1)S(1)}, bf16[8,2,4096]{2,1,0:T(2,128)(2,1)S(1)}, u32[]{:S(2)}, u32[]{:S(2)}) %collective-permute-start) | collective-permute-done | bytes 131104 | tf_op jit(solution)/shard_map/ppermute | solution.py:431
  18.4 0.0 collective-permute-start.1
  18.4 0.0 collective-permute-done.2.refs_0_
  18.5 0.2 shard_map.104
  18.6 1.1 %collective-permute-done.1.refs_0_ = bf16[8,2,4096]{2,1,0:T(2,128)(2,1)S(1)} collective-permute-done((bf16[8,2,4096]{2,1,0:T(2,128)(2,1)S(1)}, bf16[8,2,4096]{2,1,0:T(2,128)(2,1)S(1)}, u32[]{:S(2)}, u32[]{:S(2)}) %collective-permute-start.1) | collective-permute-done | bytes 131104 | tf_op jit(solution)/shard_map/ppermute | solution.py:435
  19.8 2.2 %shard_map.105 = (bf16[512,128]{1,0:T(8,128)(2,1)S(1)}, bf16[64,2048]{1,0:T(8,128)(2,1)S(1)}, bf16[64,2048]{1,0:T(8,128)(2,1)S(1)}, bf16[64,512]{1,0:T(8,128)(2,...) custom-call(bf16[8,2,4096]{2,1,0:T(2,128)(2,1)S(1)} %collective-permute-done.1.refs_0_, ...), custom_call_target="tpu_custom_call" | custom-call | flops 536870912 | bytes 1769472 | tf_op jit(solution)/shard_map/pallas_call | solution.py:290
  22.0 0.2 collective-permute-start.3
  22.2 0.8 %shard_map.106.total_ref = f32[512,128]{1,0:T(8,128)S(1)} custom-call(bf16[64,512]{1,0:T(8,128)(2,1)S(1)} %get-tuple-element.38.gate_delta_ref, bf16[64,512]{1,0:T(8,128)(2,1)S(1)} %get-tuple-element.39.up_delta_ref, bf16[2048,512]{1,0:T(8,128)(2,1)S(1)} %get-tuple-element.29.refs_5_.gate_ref, bf16[2048,512]{1,0:T(8,128)(2,1)S(1)} %get-tuple-element.30.refs_6_.up_ref), custom_call_target="tpu_custom_call" | custom-call | flops 134217728 | bytes 2490368 | tf_op jit(solution)/shard_map/pallas_call | solution.py:328
  22.9 0.4 %collective-permute-done.3.got_ref = bf16[512,128]{1,0:T(8,128)(2,1)S(1)} collective-permute-done((bf16[512,128]{1,0:T(8,128)(2,1)S(1)}, bf16[512,128]{1,0:T(8,128)(2,1)S(1)}, u32[]{:S(2)}, u32[]{:S(2)}) %collective-permute-start.3) | collective-permute-done | bytes 131104 | tf_op jit(solution)/shard_map/ppermute | solution.py:440
  23.4 0.7 %shard_map.107 = bf16[32,16,128]{2,1,0:T(8,128)(2,1)} custom-call(f32[512,128]{1,0:T(8,128)S(1)} %shard_map.106.total_ref, bf16[512,128]{1,0:T(8,128)(2,1)S(1)} %collective-permute-done.3.got_ref), custom_call_target="tpu_custom_call" | custom-call | tf_op jit(solution)/shard_map/pallas_call | solution.py:362
  24.1 4.4 %all-to-all-start.1 = ((bf16[32,16,128]{2,1,0:T(8,128)(2,1)}), bf16[32,16,128]{2,1,0:T(8,128)(2,1)S(1)}, u32[]{:S(2)}, u32[]{:S(2)}) async-start(bf16[32,16,128]{2,1,0:T(8,128)(2,1)} %shard_map.107), calls=%async_computation.1 | async-start | bytes 262144 | tf_op jit(solution)/shard_map/all_to_all | solution.py:447
  28.4 2.1 %fusion = bf16[1,2048,512]{2,1,0:T(8,128)(2,1)} fusion(bf16[64,2048]{1,0:T(8,128)(2,1)S(1)} %get-tuple-element.37, bf16[64,512]{1,0:T(8,128)(2,1)S(1)} %get-tuple-element.38.gate_delta_ref), kind=kOutput, calls=%fused_computation.3 | convolution fusion | flops 135266304 | bytes 2424832 | tf_op jit(solution)/shard_map/dot_general | solution.py:450
  30.5 2.1 %fusion.1 = bf16[1,2048,512]{2,1,0:T(8,128)(2,1)} fusion(bf16[64,2048]{1,0:T(8,128)(2,1)S(1)} %get-tuple-element.37, bf16[64,512]{1,0:T(8,128)(2,1)S(1)} %get-tuple-element.39.up_delta_ref), kind=kOutput, calls=%fused_computation.4 | convolution fusion | flops 135266304 | bytes 2424832 | tf_op jit(solution)/shard_map/dot_general | solution.py:451
  32.5 2.0 %fusion.2 = bf16[1,512,2048]{2,1,0:T(8,128)(2,1)} fusion(bf16[64,512]{1,0:T(8,128)(2,1)S(1)} %get-tuple-element.40, bf16[64,2048]{1,0:T(8,128)(2,1)S(1)} %get-tuple-element.41), kind=kOutput, calls=%fused_computation.5 | convolution fusion | flops 135266304 | bytes 2424832 | tf_op jit(solution)/shard_map/dot_general | solution.py:449
  34.6 1.8 %all-to-all-done.1.shares_ref = bf16[32,16,128]{2,1,0:T(8,128)(2,1)S(1)} async-done(((bf16[32,16,128]{2,1,0:T(8,128)(2,1)}), bf16[32,16,128]{2,1,0:T(8,128)(2,1)S(1)}, u32[]{:S(2)}, u32[]{:S(2)}) %all-to-all-start.1) | async-done | bytes 131104 | tf_op jit(solution)/shard_map/all_to_all | solution.py:447
  36.3 0.6 %shard_map.108 = bf16[1,2,2048]{2,1,0:T(2,128)(2,1)} custom-call(bf16[32,16,128]{2,1,0:T(8,128)(2,1)S(1)} %all-to-all-done.1.shares_ref), custom_call_target="tpu_custom_call" | custom-call | tf_op jit(solution)/shard_map/pallas_call | solution.py:395
Async XLA Ops:
  13.5 5.0 %collective-permute-start = (bf16[8,2,4096]{2,1,0:T(2,128)(2,1)S(1)}, bf16[8,2,4096]{2,1,0:T(2,128)(2,1)S(1)}, u32[]{:S(2)}, u32[]{:S(2)}) collective-permute-start(bf16[8,2,4096]{2,1,0:T(2,128)(2,1)S(1)} %all_to_all.10.mine_ref), channel_id=1, source_target_pairs={{2,0},{3,1},{0,2},{1,3},{6,4},{7,5},{4,6},{5,7},{10,8},{11,9},{8,1... | collective-permute-start | bytes 393224 | tf_op jit(solution)/shard_map/ppermute | solution.py:431
  15.0 3.5 %collective-permute-start.2 = (bf16[8,2,4096]{2,1,0:T(2,128)(2,1)S(1)}, bf16[8,2,4096]{2,1,0:T(2,128)(2,1)S(1)}, u32[]{:S(2)}, u32[]{:S(2)}) collective-permute-start(bf16[8,2,4096]{2,1,0:T(2,128)(2,1)S(1)} %all_to_all.10.mine_ref), channel_id=1, source_target_pairs={{0,1},{1,0},{2,3},{3,2},{4,5},{5,4},{6,7},{7,6},{8,9},{9,8},{10,11... | collective-permute-start | bytes 393224 | tf_op jit(solution)/shard_map/ppermute | solution.py:432
  18.4 1.3 %collective-permute-start.1 = (bf16[8,2,4096]{2,1,0:T(2,128)(2,1)S(1)}, bf16[8,2,4096]{2,1,0:T(2,128)(2,1)S(1)}, u32[]{:S(2)}, u32[]{:S(2)}) collective-permute-start(bf16[8,2,4096]{2,1,0:T(2,128)(2,1)S(1)} %collective-permute-done.refs_1_), channel_id=1, source_target_pairs={{0,1},{1,0},{2,3},{3,2},{4,5},{5,4},{6,7},{7,6},{8,9},{9,8},{10,11... | collective-permute-start | bytes 393224 | tf_op jit(solution)/shard_map/ppermute | solution.py:435
  22.0 1.4 %collective-permute-start.3 = (bf16[512,128]{1,0:T(8,128)(2,1)S(1)}, bf16[512,128]{1,0:T(8,128)(2,1)S(1)}, u32[]{:S(2)}, u32[]{:S(2)}) collective-permute-start(bf16[512,128]{1,0:T(8,128)(2,1)S(1)} %get-tuple-element.34), channel_id=1, source_target_pairs={{0,1},{1,0},{2,3},{3,2},{4,5},{5,4},{6,7},{7,6},{8,9},{9,8},{10,11... | collective-permute-start | bytes 393224 | tf_op jit(solution)/shard_map/ppermute | solution.py:440
  24.1 12.3 %all-to-all-start.1 = ((bf16[32,16,128]{2,1,0:T(8,128)(2,1)}), bf16[32,16,128]{2,1,0:T(8,128)(2,1)S(1)}, u32[]{:S(2)}, u32[]{:S(2)}) async-start(bf16[32,16,128]{2,1,0:T(8,128)(2,1)} %shard_map.107), calls=%async_computation.1 | async-start | bytes 262144 | tf_op jit(solution)/shard_map/all_to_all | solution.py:447

commit v14 on v13

--- a/solution.py
+++ b/solution.py
@@ -247,18 +247,27 @@
     my_x_ref, my_dy_ref, laid_x_ref, laid_dy_ref, gate_ref, up_ref, down_ref, *refs = refs
     sent_ref, x_ref, dy_ref, gate_delta_ref, up_delta_ref, hidden_ref, total_ref = refs
     size = my_x_ref.shape[0]
-    x_ref[:size] = my_x_ref[...]
-    dy_ref[:size] = my_dy_ref[...]
-    for i in range(along_y):
+    one_block = x_ref.shape[0] == ROWS and along_y == CORES and size == TILE
+    if one_block:
+        width = x_ref.shape[1]
+        last = jnp.concatenate([other_refs[0][j] for j in range(other_refs[0].shape[0])], axis=0)
+        all_x = jnp.concatenate([my_x_ref[...], laid_x_ref[...], last[:, :width]], axis=0)
+        all_dy = jnp.concatenate([my_dy_ref[...], laid_dy_ref[...], last[:, width:]], axis=0)
+        x_ref[...] = all_x
+        dy_ref[...] = all_dy
+    else:
+        x_ref[:size] = my_x_ref[...]
+        dy_ref[:size] = my_dy_ref[...]
+    for i in range(0 if one_block else along_y):
         there = pl.ds(size if i == 0 else 2 * i * size, size)
         x_ref[there] = laid_x_ref[i * size : (i + 1) * size]
         dy_ref[there] = laid_dy_ref[i * size : (i + 1) * size]
-    for i, other_ref in enumerate(other_refs):
+    for i, other_ref in enumerate(() if one_block else other_refs):
         lay_out(other_ref, x_ref, dy_ref, (2 * i + 3) * size)
 
     def step(block, first):
         rows = pl.ds(pl.multiple_of(block * ROWS, ROWS), ROWS)
-        x = x_ref[rows]
+        x, dy = (all_x, all_dy) if one_block else (x_ref[rows], dy_ref[rows])
         pre_gate = jnp.dot(x, gate_ref[...], preferred_element_type=jnp.float32)
         pre_up = jnp.dot(x, up_ref[...], preferred_element_type=jnp.float32)
         sigmoid_gate = jax.nn.sigmoid(pre_gate)
@@ -266,7 +275,7 @@
         slope = sigmoid_gate * (1.0 + pre_gate * (1.0 - sigmoid_gate))
         hidden_ref[rows] = (activated * pre_up).astype(jnp.bfloat16)
         grad_hidden = lax.dot_general(
-            dy_ref[rows], down_ref[...], CONTRACT_LAST, preferred_element_type=jnp.float32
+            dy, down_ref[...], CONTRACT_LAST, preferred_element_type=jnp.float32
         )
         gate_delta = (grad_hidden * pre_up * slope).astype(jnp.bfloat16)
         up_delta = (grad_hidden * activated).astype(jnp.bfloat16)
@@ -368,10 +377,11 @@
     )(total, got)
 
 
-def sum_kernel(shares_ref, out_hbm, wide_ref, out_ref, sem):
+def sum_kernel(shares_ref, out_hbm, wide_ref, out_ref, sems):
     devices, size, _ = shares_ref.shape
     _, tok_dev, width = out_ref.shape
     groups = size // tok_dev
+    copies = []
     for core in range(CORES):
         total = lax.fori_loop(
             0,
@@ -383,10 +393,14 @@
         for row in range(size):
             token, lane = row // groups, (core * groups + row % groups) * LANES
             wide_ref[token : token + 1, lane : lane + LANES] = total[row : row + 1]
-    out_ref[0] = wide_ref[...].astype(jnp.bfloat16)
-    copy = pltpu.make_async_copy(out_ref, out_hbm, sem)
-    copy.start()
-    copy.wait()
+        half = pl.ds(core * groups * LANES, groups * LANES)
+        out_ref[0, :, half] = wide_ref[:, half].astype(jnp.bfloat16)
+        copies.append(
+            pltpu.make_async_copy(out_ref.at[:, :, half], out_hbm.at[:, :, half], sems.at[core])
+        )
+        copies[-1].start()
+    for copy in copies:
+        copy.wait()
 
 
 def sum_shares(shares, tok_dev):
@@ -400,7 +414,7 @@
         scratch_shapes=[
             pltpu.VMEM((tok_dev, width), jnp.float32),
             pltpu.VMEM((1, tok_dev, width), jnp.bfloat16),
-            pltpu.SemaphoreType.DMA,
+            pltpu.SemaphoreType.DMA((CORES,)),
         ],
         compiler_params=vmem(16 << 20),
     )(shares)

time: 37.3 us -> 37.3 us (level)
  no operation moved by 1% of the time
where the time goes in v14:
time: 37.3 us; the launch traced here: 37 us
  blocking collectives  11.9 us (32%)
  Pallas kernels  8.23 us (22%)
  matrix products  6.16 us (17%)
  starting transfers between devices  6.12 us (16%)
  waiting for transfers between devices  3.9 us (10%)
  between operations  0.67 us (2%)
    all_to_all x1, blocking collectives, local(): lax.all_to_all(copies, BOTH, 0, 0, axis_index_groups=groups, tiled=True)  11.9 us
    all_to_all x1, starting transfers between devices, local(): lax.all_to_all(shares, BOTH, 0, 0, axis_index_groups=everyone, tiled=True)  4.36 us
    pallas_call x1, Pallas kernels, fetch(): pl.pallas_call(fetch_kernel, out_shape=tuple((pltpu.VMEM(w.shape[1:], w.d...  2.88 us
    pallas_call x1, Pallas kernels, rows_pass(): pl.pallas_call(rows_kernel, out_shape=(bf16((rows * groups, LANES)), bf16...  2.19 us
    dot_general x1, matrix products, local(): grad_gate = jnp.dot(x.T, gate_delta, preferred_element_type=jnp.float32)  2.06 us
    dot_general x1, matrix products, local(): grad_up = jnp.dot(x.T, up_delta, preferred_element_type=jnp.float32)  2.05 us
    dot_general x1, matrix products, local(): grad_down = jnp.dot(hidden.T, dy, preferred_element_type=jnp.float32)  2.05 us
    all_to_all x1, waiting for transfers between devices, local(): lax.all_to_all(shares, BOTH, 0, 0, axis_index_groups=everyone, tiled=True)  1.76 us
  transfers between devices with their start and end apart: 5, of which 4 were waited for; matrix products, arithmetic and copies ran while one was open for 17% of the time, Pallas kernels for 10%

profile of v14, /device:TPU:0, one launch (start us, length us, event | category | flops | bytes accessed | tf_op | source)
XLA Modules:
  0.0 37.0 jit_solution(10649690707042952241)
XLA Ops:
  0.6 0.9 %shard_map.102 = bf16[8,2,4096]{2,1,0:T(2,128)(2,1)S(1)} custom-call(bf16[1,2,2048]{2,1,0:T(2,128)(2,1)} %tokens_hbm.1, bf16[1,2,2048]{2,1,0:T(2,128)(2,1)} %grad_hbm.1, s32[1,2,4]{2,1,0:T(2,128)} %bitcast.14, bf16[1,2,4]{2,1,0:T(2,128)(2,1)} %bitcast.15), custom_call_target="tpu_custom_call" | custom-call | tf_op jit(solution)/shard_map/pallas_call | solution.py:126
  1.5 11.9 %all_to_all.10.mine_ref = bf16[8,2,4096]{2,1,0:T(2,128)(2,1)S(1)} all-to-all(bf16[8,2,4096]{2,1,0:T(2,128)(2,1)S(1)} %shard_map.102), channel_id=1, replica_groups={{8,4,24,20,12,0,28,16},{9,5,25,21,13,1,29,17},{10,6,26,22,14,2,30,18},{..., dimensions={0} | all-to-all | bytes 262144 | tf_op jit(solution)/shard_map/all_to_all | solution.py:444
  13.5 1.5 %collective-permute-start = (bf16[8,2,4096]{2,1,0:T(2,128)(2,1)S(1)}, bf16[8,2,4096]{2,1,0:T(2,128)(2,1)S(1)}, u32[]{:S(2)}, u32[]{:S(2)}) collective-permute-start(bf16[8,2,4096]{2,1,0:T(2,128)(2,1)S(1)} %all_to_all.10.mine_ref), channel_id=1, source_target_pairs={{2,0},{3,1},{0,2},{1,3},{6,4},{7,5},{4,6},{5,7},{10,8},{11,9},{8,1... | collective-permute-start | bytes 393224 | tf_op jit(solution)/shard_map/ppermute | solution.py:445
  15.0 0.0 collective-permute-start.2
  15.0 2.9 %shard_map.103 = (bf16[2048,512]{1,0:T(8,128)(2,1)S(1)}, bf16[2048,512]{1,0:T(8,128)(2,1)S(1)}, bf16[512,2048]{1,0:T(8,128)(2,1)S(1)}, bf16[16,2048]{1,0:T(8,128)(2,1)S(1)}, bf16[16,2048]{1,0:T(8,128)(2,1)S(1)}) custom-call(bf16[8,2,4096]{2,1,0:T(2,128)(2,1)S(1)} %all_to_all.10.mine_ref, bf16[1,2048,512]{2,1,0:T(8,128)(2,1)} %gate_hbm.1, ...), custom_call_target="tpu_custom_call" | custom-call | bytes 12582912 | tf_op jit(solution)/shard_map/pallas_call | solution.py:183
  17.9 0.6 %collective-permute-done.refs_1_ = bf16[8,2,4096]{2,1,0:T(2,128)(2,1)S(1)} collective-permute-done((bf16[8,2,4096]{2,1,0:T(2,128)(2,1)S(1)}, bf16[8,2,4096]{2,1,0:T(2,128)(2,1)S(1)}, u32[]{:S(2)}, u32[]{:S(2)}) %collective-permute-start) | collective-permute-done | bytes 131104 | tf_op jit(solution)/shard_map/ppermute | solution.py:445
  18.4 0.0 collective-permute-start.1
  18.4 0.0 collective-permute-done.2.refs_0_
  18.5 0.2 shard_map.104
  18.6 1.1 %collective-permute-done.1.refs_0_ = bf16[8,2,4096]{2,1,0:T(2,128)(2,1)S(1)} collective-permute-done((bf16[8,2,4096]{2,1,0:T(2,128)(2,1)S(1)}, bf16[8,2,4096]{2,1,0:T(2,128)(2,1)S(1)}, u32[]{:S(2)}, u32[]{:S(2)}) %collective-permute-start.1) | collective-permute-done | bytes 131104 | tf_op jit(solution)/shard_map/ppermute | solution.py:449
  19.8 2.2 %shard_map.105 = (bf16[512,128]{1,0:T(8,128)(2,1)S(1)}, bf16[64,2048]{1,0:T(8,128)(2,1)S(1)}, bf16[64,2048]{1,0:T(8,128)(2,1)S(1)}, bf16[64,512]{1,0:T(8,128)(2,...) custom-call(bf16[8,2,4096]{2,1,0:T(2,128)(2,1)S(1)} %collective-permute-done.1.refs_0_, ...), custom_call_target="tpu_custom_call" | custom-call | flops 536870912 | bytes 1769472 | tf_op jit(solution)/shard_map/pallas_call | solution.py:299
  22.0 0.2 collective-permute-start.3
  22.2 0.8 %shard_map.106.total_ref = f32[512,128]{1,0:T(8,128)S(1)} custom-call(bf16[64,512]{1,0:T(8,128)(2,1)S(1)} %get-tuple-element.38.gate_delta_ref, bf16[64,512]{1,0:T(8,128)(2,1)S(1)} %get-tuple-element.39.up_delta_ref, bf16[2048,512]{1,0:T(8,128)(2,1)S(1)} %get-tuple-element.29.refs_5_.gate_ref, bf16[2048,512]{1,0:T(8,128)(2,1)S(1)} %get-tuple-element.30.refs_6_.up_ref), custom_call_target="tpu_custom_call" | custom-call | flops 134217728 | bytes 2490368 | tf_op jit(solution)/shard_map/pallas_call | solution.py:337
  22.9 0.4 %collective-permute-done.3.got_ref = bf16[512,128]{1,0:T(8,128)(2,1)S(1)} collective-permute-done((bf16[512,128]{1,0:T(8,128)(2,1)S(1)}, bf16[512,128]{1,0:T(8,128)(2,1)S(1)}, u32[]{:S(2)}, u32[]{:S(2)}) %collective-permute-start.3) | collective-permute-done | bytes 131104 | tf_op jit(solution)/shard_map/ppermute | solution.py:454
  23.4 0.7 %shard_map.107 = bf16[32,16,128]{2,1,0:T(8,128)(2,1)} custom-call(f32[512,128]{1,0:T(8,128)S(1)} %shard_map.106.total_ref, bf16[512,128]{1,0:T(8,128)(2,1)S(1)} %collective-permute-done.3.got_ref), custom_call_target="tpu_custom_call" | custom-call | tf_op jit(solution)/shard_map/pallas_call | solution.py:371
  24.1 4.4 %all-to-all-start.1 = ((bf16[32,16,128]{2,1,0:T(8,128)(2,1)}), bf16[32,16,128]{2,1,0:T(8,128)(2,1)S(1)}, u32[]{:S(2)}, u32[]{:S(2)}) async-start(bf16[32,16,128]{2,1,0:T(8,128)(2,1)} %shard_map.107), calls=%async_computation.1 | async-start | bytes 262144 | tf_op jit(solution)/shard_map/all_to_all | solution.py:461
  28.4 2.1 %fusion = bf16[1,2048,512]{2,1,0:T(8,128)(2,1)} fusion(bf16[64,2048]{1,0:T(8,128)(2,1)S(1)} %get-tuple-element.37, bf16[64,512]{1,0:T(8,128)(2,1)S(1)} %get-tuple-element.38.gate_delta_ref), kind=kOutput, calls=%fused_computation.3 | convolution fusion | flops 135266304 | bytes 2424832 | tf_op jit(solution)/shard_map/dot_general | solution.py:464
  30.5 2.1 %fusion.1 = bf16[1,2048,512]{2,1,0:T(8,128)(2,1)} fusion(bf16[64,2048]{1,0:T(8,128)(2,1)S(1)} %get-tuple-element.37, bf16[64,512]{1,0:T(8,128)(2,1)S(1)} %get-tuple-element.39.up_delta_ref), kind=kOutput, calls=%fused_computation.4 | convolution fusion | flops 135266304 | bytes 2424832 | tf_op jit(solution)/shard_map/dot_general | solution.py:465
  32.5 2.0 %fusion.2 = bf16[1,512,2048]{2,1,0:T(8,128)(2,1)} fusion(bf16[64,512]{1,0:T(8,128)(2,1)S(1)} %get-tuple-element.40, bf16[64,2048]{1,0:T(8,128)(2,1)S(1)} %get-tuple-element.41), kind=kOutput, calls=%fused_computation.5 | convolution fusion | flops 135266304 | bytes 2424832 | tf_op jit(solution)/shard_map/dot_general | solution.py:463
  34.6 1.8 %all-to-all-done.1.shares_ref = bf16[32,16,128]{2,1,0:T(8,128)(2,1)S(1)} async-done(((bf16[32,16,128]{2,1,0:T(8,128)(2,1)}), bf16[32,16,128]{2,1,0:T(8,128)(2,1)S(1)}, u32[]{:S(2)}, u32[]{:S(2)}) %all-to-all-start.1) | async-done | bytes 131104 | tf_op jit(solution)/shard_map/all_to_all | solution.py:461
  36.3 0.7 %shard_map.108 = bf16[1,2,2048]{2,1,0:T(2,128)(2,1)} custom-call(bf16[32,16,128]{2,1,0:T(8,128)(2,1)S(1)} %all-to-all-done.1.shares_ref), custom_call_target="tpu_custom_call" | custom-call | tf_op jit(solution)/shard_map/pallas_call | solution.py:409
Async XLA Ops:
  13.5 5.0 %collective-permute-start = (bf16[8,2,4096]{2,1,0:T(2,128)(2,1)S(1)}, bf16[8,2,4096]{2,1,0:T(2,128)(2,1)S(1)}, u32[]{:S(2)}, u32[]{:S(2)}) collective-permute-start(bf16[8,2,4096]{2,1,0:T(2,128)(2,1)S(1)} %all_to_all.10.mine_ref), channel_id=1, source_target_pairs={{2,0},{3,1},{0,2},{1,3},{6,4},{7,5},{4,6},{5,7},{10,8},{11,9},{8,1... | collective-permute-start | bytes 393224 | tf_op jit(solution)/shard_map/ppermute | solution.py:445
  15.0 3.5 %collective-permute-start.2 = (bf16[8,2,4096]{2,1,0:T(2,128)(2,1)S(1)}, bf16[8,2,4096]{2,1,0:T(2,128)(2,1)S(1)}, u32[]{:S(2)}, u32[]{:S(2)}) collective-permute-start(bf16[8,2,4096]{2,1,0:T(2,128)(2,1)S(1)} %all_to_all.10.mine_ref), channel_id=1, source_target_pairs={{0,1},{1,0},{2,3},{3,2},{4,5},{5,4},{6,7},{7,6},{8,9},{9,8},{10,11... | collective-permute-start | bytes 393224 | tf_op jit(solution)/shard_map/ppermute | solution.py:446
  18.4 1.3 %collective-permute-start.1 = (bf16[8,2,4096]{2,1,0:T(2,128)(2,1)S(1)}, bf16[8,2,4096]{2,1,0:T(2,128)(2,1)S(1)}, u32[]{:S(2)}, u32[]{:S(2)}) collective-permute-start(bf16[8,2,4096]{2,1,0:T(2,128)(2,1)S(1)} %collective-permute-done.refs_1_), channel_id=1, source_target_pairs={{0,1},{1,0},{2,3},{3,2},{4,5},{5,4},{6,7},{7,6},{8,9},{9,8},{10,11... | collective-permute-start | bytes 393224 | tf_op jit(solution)/shard_map/ppermute | solution.py:449
  22.0 1.4 %collective-permute-start.3 = (bf16[512,128]{1,0:T(8,128)(2,1)S(1)}, bf16[512,128]{1,0:T(8,128)(2,1)S(1)}, u32[]{:S(2)}, u32[]{:S(2)}) collective-permute-start(bf16[512,128]{1,0:T(8,128)(2,1)S(1)} %get-tuple-element.34), channel_id=1, source_target_pairs={{0,1},{1,0},{2,3},{3,2},{4,5},{5,4},{6,7},{7,6},{8,9},{9,8},{10,11... | collective-permute-start | bytes 393224 | tf_op jit(solution)/shard_map/ppermute | solution.py:454
  24.1 12.3 %all-to-all-start.1 = ((bf16[32,16,128]{2,1,0:T(8,128)(2,1)}), bf16[32,16,128]{2,1,0:T(8,128)(2,1)S(1)}, u32[]{:S(2)}, u32[]{:S(2)}) async-start(bf16[32,16,128]{2,1,0:T(8,128)(2,1)} %shard_map.107), calls=%async_computation.1 | async-start | bytes 262144 | tf_op jit(solution)/shard_map/all_to_all | solution.py:461

commit v15 on v13

--- a/solution.py
+++ b/solution.py
@@ -101,18 +101,22 @@
         score = jnp.sum(jnp.where(mine, scores, 0.0), axis=1, keepdims=True)
         weights = jnp.sum(jnp.where(lane == named, score, 0.0), axis=0, keepdims=True)
         table = jnp.where(row == i, weights, table)
-    for copy in copies[2:]:
-        copy.wait()
+    copies[2].wait()
+
+    def write_tokens(place, carry):
+        out_ref[place, :, :width] = tokens_ref[0]
+        return carry
+
+    def write_grads(place, carry):
+        out_ref[place, :, width:] = weighted_ref[place_at(place)[0]]
+        return carry
+
+    lax.fori_loop(0, places, write_tokens, 0, unroll=places <= 16)
+    copies[3].wait()
     grad = grad_ref[0].astype(jnp.float32)
     for expert in range(experts):
         weighted_ref[expert] = (grad * table[:, expert : expert + 1]).astype(jnp.bfloat16)
-
-    def write(place, carry):
-        out_ref[place, :, :width] = tokens_ref[0]
-        out_ref[place, :, width:] = weighted_ref[place_at(place)[0]]
-        return carry
-
-    lax.fori_loop(0, places, write, 0, unroll=places <= 16)
+    lax.fori_loop(0, places, write_grads, 0, unroll=places <= 16)
 
 
 def pack(tokens, out_grad, expert_ids, gate_scores, places):

time: 37.3 us -> 37.3 us (level)
  no operation moved by 1% of the time
where the time goes in v15:
time: 37.3 us; the launch traced here: 37 us
  blocking collectives  11.9 us (32%)
  Pallas kernels  8.22 us (22%)
  matrix products  6.16 us (17%)
  starting transfers between devices  6.13 us (16%)
  waiting for transfers between devices  3.9 us (10%)
  between operations  0.67 us (2%)
    all_to_all x1, blocking collectives, local(): lax.all_to_all(copies, BOTH, 0, 0, axis_index_groups=groups, tiled=True)  11.9 us
    all_to_all x1, starting transfers between devices, local(): lax.all_to_all(shares, BOTH, 0, 0, axis_index_groups=everyone, tiled=True)  4.37 us
    pallas_call x1, Pallas kernels, fetch(): pl.pallas_call(fetch_kernel, out_shape=tuple((pltpu.VMEM(w.shape[1:], w.d...  2.88 us
    pallas_call x1, Pallas kernels, rows_pass(): pl.pallas_call(rows_kernel, out_shape=(bf16((rows * groups, LANES)), bf16...  2.18 us
    dot_general x1, matrix products, local(): grad_gate = jnp.dot(x.T, gate_delta, preferred_element_type=jnp.float32)  2.06 us
    dot_general x1, matrix products, local(): grad_up = jnp.dot(x.T, up_delta, preferred_element_type=jnp.float32)  2.05 us
    dot_general x1, matrix products, local(): grad_down = jnp.dot(hidden.T, dy, preferred_element_type=jnp.float32)  2.05 us
    all_to_all x1, waiting for transfers between devices, local(): lax.all_to_all(shares, BOTH, 0, 0, axis_index_groups=everyone, tiled=True)  1.76 us
  transfers between devices with their start and end apart: 5, of which 4 were waited for; matrix products, arithmetic and copies ran while one was open for 17% of the time, Pallas kernels for 10%

profile of v15, /device:TPU:0, one launch (start us, length us, event | category | flops | bytes accessed | tf_op | source)
XLA Modules:
  0.0 37.0 jit_solution(4776443550651431172)
XLA Ops:
  0.6 0.9 %shard_map.102 = bf16[8,2,4096]{2,1,0:T(2,128)(2,1)S(1)} custom-call(bf16[1,2,2048]{2,1,0:T(2,128)(2,1)} %tokens_hbm.1, bf16[1,2,2048]{2,1,0:T(2,128)(2,1)} %grad_hbm.1, s32[1,2,4]{2,1,0:T(2,128)} %bitcast.14, bf16[1,2,4]{2,1,0:T(2,128)(2,1)} %bitcast.15), custom_call_target="tpu_custom_call" | custom-call | tf_op jit(solution)/shard_map/pallas_call | solution.py:130
  1.5 11.9 %all_to_all.10.mine_ref = bf16[8,2,4096]{2,1,0:T(2,128)(2,1)S(1)} all-to-all(bf16[8,2,4096]{2,1,0:T(2,128)(2,1)S(1)} %shard_map.102), channel_id=1, replica_groups={{8,4,24,20,12,0,28,16},{9,5,25,21,13,1,29,17},{10,6,26,22,14,2,30,18},{..., dimensions={0} | all-to-all | bytes 262144 | tf_op jit(solution)/shard_map/all_to_all | solution.py:434
  13.5 1.5 %collective-permute-start = (bf16[8,2,4096]{2,1,0:T(2,128)(2,1)S(1)}, bf16[8,2,4096]{2,1,0:T(2,128)(2,1)S(1)}, u32[]{:S(2)}, u32[]{:S(2)}) collective-permute-start(bf16[8,2,4096]{2,1,0:T(2,128)(2,1)S(1)} %all_to_all.10.mine_ref), channel_id=1, source_target_pairs={{2,0},{3,1},{0,2},{1,3},{6,4},{7,5},{4,6},{5,7},{10,8},{11,9},{8,1... | collective-permute-start | bytes 393224 | tf_op jit(solution)/shard_map/ppermute | solution.py:435
  15.0 0.0 collective-permute-start.2
  15.0 2.9 %shard_map.103 = (bf16[2048,512]{1,0:T(8,128)(2,1)S(1)}, bf16[2048,512]{1,0:T(8,128)(2,1)S(1)}, bf16[512,2048]{1,0:T(8,128)(2,1)S(1)}, bf16[16,2048]{1,0:T(8,128)(2,1)S(1)}, bf16[16,2048]{1,0:T(8,128)(2,1)S(1)}) custom-call(bf16[8,2,4096]{2,1,0:T(2,128)(2,1)S(1)} %all_to_all.10.mine_ref, bf16[1,2048,512]{2,1,0:T(8,128)(2,1)} %gate_hbm.1, ...), custom_call_target="tpu_custom_call" | custom-call | bytes 12582912 | tf_op jit(solution)/shard_map/pallas_call | solution.py:187
  17.9 0.6 %collective-permute-done.refs_1_ = bf16[8,2,4096]{2,1,0:T(2,128)(2,1)S(1)} collective-permute-done((bf16[8,2,4096]{2,1,0:T(2,128)(2,1)S(1)}, bf16[8,2,4096]{2,1,0:T(2,128)(2,1)S(1)}, u32[]{:S(2)}, u32[]{:S(2)}) %collective-permute-start) | collective-permute-done | bytes 131104 | tf_op jit(solution)/shard_map/ppermute | solution.py:435
  18.4 0.0 collective-permute-start.1
  18.5 0.0 collective-permute-done.2.refs_0_
  18.5 0.2 shard_map.104
  18.6 1.1 %collective-permute-done.1.refs_0_ = bf16[8,2,4096]{2,1,0:T(2,128)(2,1)S(1)} collective-permute-done((bf16[8,2,4096]{2,1,0:T(2,128)(2,1)S(1)}, bf16[8,2,4096]{2,1,0:T(2,128)(2,1)S(1)}, u32[]{:S(2)}, u32[]{:S(2)}) %collective-permute-start.1) | collective-permute-done | bytes 131104 | tf_op jit(solution)/shard_map/ppermute | solution.py:439
  19.8 2.2 %shard_map.105 = (bf16[512,128]{1,0:T(8,128)(2,1)S(1)}, bf16[64,2048]{1,0:T(8,128)(2,1)S(1)}, bf16[64,2048]{1,0:T(8,128)(2,1)S(1)}, bf16[64,512]{1,0:T(8,128)(2,...) custom-call(bf16[8,2,4096]{2,1,0:T(2,128)(2,1)S(1)} %collective-permute-done.1.refs_0_, ...), custom_call_target="tpu_custom_call" | custom-call | flops 536870912 | bytes 1769472 | tf_op jit(solution)/shard_map/pallas_call | solution.py:294
  22.0 0.2 collective-permute-start.3
  22.2 0.8 %shard_map.106.total_ref = f32[512,128]{1,0:T(8,128)S(1)} custom-call(bf16[64,512]{1,0:T(8,128)(2,1)S(1)} %get-tuple-element.38.gate_delta_ref, bf16[64,512]{1,0:T(8,128)(2,1)S(1)} %get-tuple-element.39.up_delta_ref, bf16[2048,512]{1,0:T(8,128)(2,1)S(1)} %get-tuple-element.29.refs_5_.gate_ref, bf16[2048,512]{1,0:T(8,128)(2,1)S(1)} %get-tuple-element.30.refs_6_.up_ref), custom_call_target="tpu_custom_call" | custom-call | flops 134217728 | bytes 2490368 | tf_op jit(solution)/shard_map/pallas_call | solution.py:332
  22.9 0.4 %collective-permute-done.3.got_ref = bf16[512,128]{1,0:T(8,128)(2,1)S(1)} collective-permute-done((bf16[512,128]{1,0:T(8,128)(2,1)S(1)}, bf16[512,128]{1,0:T(8,128)(2,1)S(1)}, u32[]{:S(2)}, u32[]{:S(2)}) %collective-permute-start.3) | collective-permute-done | bytes 131104 | tf_op jit(solution)/shard_map/ppermute | solution.py:444
  23.4 0.7 %shard_map.107 = bf16[32,16,128]{2,1,0:T(8,128)(2,1)} custom-call(f32[512,128]{1,0:T(8,128)S(1)} %shard_map.106.total_ref, bf16[512,128]{1,0:T(8,128)(2,1)S(1)} %collective-permute-done.3.got_ref), custom_call_target="tpu_custom_call" | custom-call | tf_op jit(solution)/shard_map/pallas_call | solution.py:366
  24.1 4.4 %all-to-all-start.1 = ((bf16[32,16,128]{2,1,0:T(8,128)(2,1)}), bf16[32,16,128]{2,1,0:T(8,128)(2,1)S(1)}, u32[]{:S(2)}, u32[]{:S(2)}) async-start(bf16[32,16,128]{2,1,0:T(8,128)(2,1)} %shard_map.107), calls=%async_computation.1 | async-start | bytes 262144 | tf_op jit(solution)/shard_map/all_to_all | solution.py:451
  28.4 2.1 %fusion = bf16[1,2048,512]{2,1,0:T(8,128)(2,1)} fusion(bf16[64,2048]{1,0:T(8,128)(2,1)S(1)} %get-tuple-element.37, bf16[64,512]{1,0:T(8,128)(2,1)S(1)} %get-tuple-element.38.gate_delta_ref), kind=kOutput, calls=%fused_computation.3 | convolution fusion | flops 135266304 | bytes 2424832 | tf_op jit(solution)/shard_map/dot_general | solution.py:454
  30.5 2.1 %fusion.1 = bf16[1,2048,512]{2,1,0:T(8,128)(2,1)} fusion(bf16[64,2048]{1,0:T(8,128)(2,1)S(1)} %get-tuple-element.37, bf16[64,512]{1,0:T(8,128)(2,1)S(1)} %get-tuple-element.39.up_delta_ref), kind=kOutput, calls=%fused_computation.4 | convolution fusion | flops 135266304 | bytes 2424832 | tf_op jit(solution)/shard_map/dot_general | solution.py:455
  32.5 2.0 %fusion.2 = bf16[1,512,2048]{2,1,0:T(8,128)(2,1)} fusion(bf16[64,512]{1,0:T(8,128)(2,1)S(1)} %get-tuple-element.40, bf16[64,2048]{1,0:T(8,128)(2,1)S(1)} %get-tuple-element.41), kind=kOutput, calls=%fused_computation.5 | convolution fusion | flops 135266304 | bytes 2424832 | tf_op jit(solution)/shard_map/dot_general | solution.py:453
  34.6 1.8 %all-to-all-done.1.shares_ref = bf16[32,16,128]{2,1,0:T(8,128)(2,1)S(1)} async-done(((bf16[32,16,128]{2,1,0:T(8,128)(2,1)}), bf16[32,16,128]{2,1,0:T(8,128)(2,1)S(1)}, u32[]{:S(2)}, u32[]{:S(2)}) %all-to-all-start.1) | async-done | bytes 131104 | tf_op jit(solution)/shard_map/all_to_all | solution.py:451
  36.3 0.6 %shard_map.108 = bf16[1,2,2048]{2,1,0:T(2,128)(2,1)} custom-call(bf16[32,16,128]{2,1,0:T(8,128)(2,1)S(1)} %all-to-all-done.1.shares_ref), custom_call_target="tpu_custom_call" | custom-call | tf_op jit(solution)/shard_map/pallas_call | solution.py:399
Async XLA Ops:
  13.5 5.0 %collective-permute-start = (bf16[8,2,4096]{2,1,0:T(2,128)(2,1)S(1)}, bf16[8,2,4096]{2,1,0:T(2,128)(2,1)S(1)}, u32[]{:S(2)}, u32[]{:S(2)}) collective-permute-start(bf16[8,2,4096]{2,1,0:T(2,128)(2,1)S(1)} %all_to_all.10.mine_ref), channel_id=1, source_target_pairs={{2,0},{3,1},{0,2},{1,3},{6,4},{7,5},{4,6},{5,7},{10,8},{11,9},{8,1... | collective-permute-start | bytes 393224 | tf_op jit(solution)/shard_map/ppermute | solution.py:435
  15.0 3.5 %collective-permute-start.2 = (bf16[8,2,4096]{2,1,0:T(2,128)(2,1)S(1)}, bf16[8,2,4096]{2,1,0:T(2,128)(2,1)S(1)}, u32[]{:S(2)}, u32[]{:S(2)}) collective-permute-start(bf16[8,2,4096]{2,1,0:T(2,128)(2,1)S(1)} %all_to_all.10.mine_ref), channel_id=1, source_target_pairs={{0,1},{1,0},{2,3},{3,2},{4,5},{5,4},{6,7},{7,6},{8,9},{9,8},{10,11... | collective-permute-start | bytes 393224 | tf_op jit(solution)/shard_map/ppermute | solution.py:436
  18.4 1.3 %collective-permute-start.1 = (bf16[8,2,4096]{2,1,0:T(2,128)(2,1)S(1)}, bf16[8,2,4096]{2,1,0:T(2,128)(2,1)S(1)}, u32[]{:S(2)}, u32[]{:S(2)}) collective-permute-start(bf16[8,2,4096]{2,1,0:T(2,128)(2,1)S(1)} %collective-permute-done.refs_1_), channel_id=1, source_target_pairs={{0,1},{1,0},{2,3},{3,2},{4,5},{5,4},{6,7},{7,6},{8,9},{9,8},{10,11... | collective-permute-start | bytes 393224 | tf_op jit(solution)/shard_map/ppermute | solution.py:439
  22.0 1.4 %collective-permute-start.3 = (bf16[512,128]{1,0:T(8,128)(2,1)S(1)}, bf16[512,128]{1,0:T(8,128)(2,1)S(1)}, u32[]{:S(2)}, u32[]{:S(2)}) collective-permute-start(bf16[512,128]{1,0:T(8,128)(2,1)S(1)} %get-tuple-element.34), channel_id=1, source_target_pairs={{0,1},{1,0},{2,3},{3,2},{4,5},{5,4},{6,7},{7,6},{8,9},{9,8},{10,11... | collective-permute-start | bytes 393224 | tf_op jit(solution)/shard_map/ppermute | solution.py:444
  24.1 12.3 %all-to-all-start.1 = ((bf16[32,16,128]{2,1,0:T(8,128)(2,1)}), bf16[32,16,128]{2,1,0:T(8,128)(2,1)S(1)}, u32[]{:S(2)}, u32[]{:S(2)}) async-start(bf16[32,16,128]{2,1,0:T(8,128)(2,1)} %shard_map.107), calls=%async_computation.1 | async-start | bytes 262144 | tf_op jit(solution)/shard_map/all_to_all | solution.py:451
